TPU v7x, 32 devices: a whole 2x2x4 slice. The times are simulated.
32 devices in a mesh: patch: 4 (over y, x), dir: 8 (over z, core).
Axes of the slice: x: 2, y: 2, z: 4, core: 2. Of those that a mesh axis runs over, the one named last changes fastest.
Arguments:
- fine_out: bfloat16 [24, 32, 2, 4, 512], P('patch', 'dir'), may hold values from -6 to 6
- interp: bfloat16 [512, 2048], replicated, may hold values from -0.25 to 0.25
- child_phase: float32 [4, 2048], replicated, may hold values from -3.140625 to 3.140625
- fine_ops: float32 [40, 2, 512], replicated, may hold values from -1.2 to 1.2
- parent_ops: float32 [40, 2, 2048], P(None, None, 'dir'), may hold values from -0.6 to 0.6
- fine_src: int32 [24, 32, 32], P('patch'), may hold values from 0 to 767, as said below
- fine_op: int32 [24, 32, 32], P('patch'), may hold values from 0 to 40, as said below
- parent_src: int32 [12, 16, 32], P('patch'), may hold values from 0 to 191, as said below
- parent_op: int32 [12, 16, 32], P('patch'), may hold values from 0 to 40, as said below
Outputs:
- fine_in: float32 [24, 32, 2, 4, 512], P('patch', 'dir')
Inputs may be any that keep to these rules, and one draw needn't show every extreme that they name: `fine_src`: A slot with op id 40 is padding and names the box itself. Every other slot names a distinct box at most 3 rows and 3 columns away, not adjacent to the box, whose parent is adjacent to or equal to the box's parent; its op id is the index of the offset (dr, dc), in order of dr then dc over -3..3, among the offsets with max(|dr|, |dc|) > 1. `fine_op`: as for fine_src. `parent_src`: as for fine_src, on the parent grid. `parent_op`: as for fine_op, on the parent grid.
All inputs are finite; a program needn't handle non-finite values.
Results may differ from a plain program's by a relative error of at most 0.0022.
Values may be sent and summed in bfloat16 or wider, within the bound.
No kernel may reach another device: no remote copies, remote signals or barrier semaphores. Data moves between devices by JAX's collectives and lax.ppermute only.
A program may use at most 128 MiB of HBM per device.

v0:
```python
import functools

import jax
import jax.numpy as jnp
import numpy as np
from jax import lax
from jax.experimental import pallas as pl
from jax.experimental.pallas import tpu as pltpu
from jax.sharding import PartitionSpec as P

CHUNK = 512
F32, BF16 = jnp.float32, jnp.bfloat16


def offset_pairs():
    return [(dr, dc) for dr in range(-3, 4) for dc in range(-3, 4) if max(abs(dr), abs(dc)) > 1]


def class_offsets(row_odd, col_odd):
    return [
        (op_id, dr, dc)
        for op_id, (dr, dc) in enumerate(offset_pairs())
        if -2 <= dr + row_odd <= 3 and -2 <= dc + col_odd <= 3
    ]


def halo_sizes(count):
    return (3, 2) if count % 2 else (2, 2)


def stored_at(rel, count, odd):
    first, second = halo_sizes(count)
    if 0 <= rel < count:
        return rel
    if rel < 0:
        return count + first + rel if odd else count + first + second + rel
    return rel if not odd else rel + first


def place(row, col, rows, cols, row_odd, col_odd, scale):
    at_r = stored_at(row // scale, rows, row_odd) * scale + row % scale
    at_c = stored_at(col // scale, cols, col_odd) * scale + col % scale
    for group, width in enumerate((cols, *halo_sizes(cols))):
        if at_c < width * scale:
            return group, at_r * width * scale + at_c
        at_c -= width * scale


def slots_of(row, col, rows, cols, row_odd, col_odd, scale):
    shift_r, shift_c = (row_odd * rows, col_odd * cols) if scale == 1 else (0, 0)
    found = ([], [], [])
    for op_id, dr, dc in class_offsets((row + shift_r) % 2, (col + shift_c) % 2):
        group, index = place(row + dr, col + dc, rows, cols, row_odd, col_odd, scale)
        found[group].append((op_id, index))
    return found


def slot_counts(rows, cols, scale):
    most = [0, 0, 0]
    for row_odd in range(2):
        for col_odd in range(2):
            for r in range(rows * scale):
                for c in range(cols * scale):
                    lists = slots_of(r, c, rows, cols, row_odd, col_odd, scale)
                    most = [max(m, len(found)) for m, found in zip(most, lists)]
    return most[0], max(most[1:])


def build_tables(rows, cols, zeros):
    fine_own, fine_side = slot_counts(rows, cols, 2)
    par_own, par_side = slot_counts(rows, cols, 1)
    width = max(fine_own + 2 * fine_side, par_own + 2 * par_side)
    sources, op_ids = [], []
    for row_odd in range(2):
        for col_odd in range(2):
            src_rows, id_rows = [], []
            for scale, sizes in ((2, (fine_own, fine_side, fine_side)), (1, (par_own, par_side, par_side))):
                zero = zeros[scale]
                for r in range(rows * scale):
                    for c in range(cols * scale):
                        src_row, id_row = [], []
                        lists = slots_of(r, c, rows, cols, row_odd, col_odd, scale)
                        for size, found in zip(sizes, lists):
                            found = found + [(0, zero)] * (size - len(found))
                            src_row += [s for _, s in found]
                            id_row += [o for o, _ in found]
                        pad = width - len(src_row)
                        src_rows.append(src_row + [zero] * pad)
                        id_rows.append(id_row + [0] * pad)
            sources.append(src_rows)
            op_ids.append(id_rows)
    return np.array(sources, np.int32), np.array(op_ids, np.int32)


def pairs(count, first):
    if first:
        return [(i, i ^ 1) for i in range(count) if (i ^ 1) < count]
    found = []
    for i in range(1, count - 1, 2):
        found += [(i, i + 1), (i + 1, i)]
    return found


def exchange(block, axis, unit, count):
    n = lax.axis_size(axis)
    odd = lax.rem(lax.axis_index(axis), 2)
    got = []
    for first, size in zip((True, False), halo_sizes(count)):
        edge = block
        if size < count:
            low = (1 - odd) if first else odd
            edge = lax.dynamic_slice_in_dim(block, low * ((count - size) * unit), size * unit, 0)
        got.append(lax.ppermute(edge, axis, pairs(n, first)))
    return got


def swap_bits(axis):
    return lax.axis_size(axis).bit_length() - 1


def gather_stage(block, axis, bit):
    other = lax.ppermute(block, axis, [(i, i ^ (1 << bit)) for i in range(lax.axis_size(axis))])
    return jnp.concatenate([block, other], axis=0)


def in_order(block, axis):
    n, bits = lax.axis_size(axis), swap_bits(axis)
    spots = [int(format(s, "0%db" % bits)[::-1], 2) for s in range(n)] if bits else [0]
    at = jnp.asarray(np.array(spots, np.int32))[jnp.arange(n, dtype=jnp.int32) ^ lax.axis_index(axis)]
    block = jnp.take(block, at, axis=0)
    return block.transpose(1, 2, 0, 3).reshape(1, block.shape[1], 2, n * block.shape[3])


def times_i(v, sides):
    sign = jnp.where(lax.broadcasted_iota(jnp.int32, (2 * sides, 1), 0) < sides, -1.0, 1.0)
    return sign.astype(F32) * pltpu.roll(v, sides, 0)


def row_of(ref, lead, part, lane, width, comps):
    return jnp.broadcast_to(ref[(*lead, slice(part, part + 1), pl.ds(lane, width))], (comps, width))


def add_slots(sums, coefs, pieces):
    real, imag = coefs
    for m, piece in enumerate(pieces):
        add = [real * piece, imag * piece]
        sums[m] = add if sums[m] is None else [a + b for a, b in zip(sums[m], add)]


def widen(src, fine, comps):
    count = src.shape[0] // comps
    fine[:count] = src[...].astype(F32).reshape(count, comps, src.shape[1])
    fine[count] = jnp.zeros(fine.shape[1:], F32)


def spread_chunk(src, interp, j, buffer, comps):
    lanes = slice(j * CHUNK, (j + 1) * CHUNK)
    out = jnp.dot(src[...], interp[:, lanes], preferred_element_type=F32)
    buffer[...] = out.reshape(-1, comps, CHUNK)


def shifts(trig, j, comps):
    lanes = slice(j * CHUNK, (j + 1) * CHUNK)
    return [jnp.broadcast_to(trig[k : k + 1, lanes], (comps, CHUNK)) for k in range(8)]


def aggregate_chunk(buffer, shift, pattern, lanes, width, sides):
    boxes = buffer.shape[0] // 4
    for q in range(boxes):
        r, c = divmod(q, width)
        total = [None, None]
        for k in range(4):
            piece = buffer[(2 * r + k // 2) * (2 * width) + 2 * c + k % 2]
            for i in range(2):
                add = shift[4 * i + k] * piece
                total[i] = add if k == 0 else total[i] + add
        whole = total[0] + times_i(total[1], sides)
        pattern[q, :, lanes] = whole.astype(BF16).astype(F32)
    pattern[boxes, :, lanes] = jnp.zeros(whole.shape, F32)


def near_side(table, ids, fops, fine, rows, cols, sides, base, count, first_col, store):
    comps, fdirs = fine.shape[1:]
    for a in range(2):
        for c in range(2):
            group = [(2 * r + a) * (2 * cols) + first_col + c for r in range(rows)]
            sums = [None] * rows
            for t in range(base, base + count):
                op_id = ids[group[0], t]
                coefs = [row_of(fops, (op_id,), i, 0, fdirs, comps) for i in range(2)]
                add_slots(sums, coefs, [fine[table[box, t]] for box in group])
            for r in range(rows):
                store((2 * r + a) * 2 + c, sums[r][0] + times_i(sums[r][1], sides))


def own_kernel(rows, cols, sides, table, src, interp, phase, fops, pattern, near, trig, fine, even, odd):
    comps, fdirs = fine.shape[1:]
    buffers = (even, odd)
    steps = interp.shape[1] // CHUNK
    trig[:4] = jnp.cos(phase[...])
    trig[4:] = jnp.sin(phase[...])
    widen(src, fine, comps)
    spread_chunk(src, interp, 0, buffers[0], comps)
    for j in range(steps):
        if j + 1 < steps:
            spread_chunk(src, interp, j + 1, buffers[(j + 1) % 2], comps)
        lanes = slice(j * CHUNK, (j + 1) * CHUNK)
        aggregate_chunk(buffers[j % 2], shifts(trig, j, comps), pattern, lanes, cols, sides)
    for a in range(2):
        for c in range(2 * cols):
            found = slots_of(a, c, rows, cols, 0, 0, 2)[0]
            group = [(2 * r + a) * (2 * cols) + c for r in range(rows)]
            sums = [None] * rows
            for t, (op_id, _) in enumerate(found):
                coefs = [row_of(fops, (op_id,), i, 0, fdirs, comps) for i in range(2)]
                add_slots(sums, coefs, [fine[table[box, t]] for box in group])
            for box, (real, imag) in zip(group, sums):
                near[box] = real + times_i(imag, sides)


def side_kernel(rows, cols, sides, table, ids, info, src, interp, trig, fops, pattern, near, fine, even, odd):
    comps = fine.shape[1]
    buffers = (even, odd)
    steps = interp.shape[1] // CHUNK
    own, side = slot_counts(rows, cols, 2)
    width = halo_sizes(cols)[0]
    widen(src, fine, comps)

    def store(at, value):
        near[at] = value

    spread_chunk(src, interp, 0, buffers[0], comps)
    for j in range(steps):
        if j + 1 < steps:
            spread_chunk(src, interp, j + 1, buffers[(j + 1) % 2], comps)
        lanes = slice(j * CHUNK, (j + 1) * CHUNK)
        aggregate_chunk(buffers[j % 2], shifts(trig, j, comps), pattern, lanes, width, sides)
    near_side(table, ids, fops, fine, rows, cols, sides, own, side, info[0, 0] * (2 * cols - 2), store)


def last_kernel(
    rows, cols, sides,
    table, ids, info,
    src, interp, trig, fops, pops, pat_own, pat_a, near_own, near_a,
    out,
    fine, even, odd, pat_b0, pat_b1, child0, child1, near_b, acc,
):
    comps, fdirs = fine.shape[1:]
    fcols = 2 * cols
    width = halo_sizes(cols)[1]
    steps = interp.shape[1] // CHUNK
    buffers, patterns, children = (even, odd), (pat_b0, pat_b1), (child0, child1)
    own, side = slot_counts(rows, cols, 2)
    par_own, par_side = slot_counts(rows, cols, 1)
    a_right = info[0, 0]
    piece_w = min(CHUNK, pops.shape[3])

    widen(src, fine, comps)

    def store(at, value):
        near_b[1 - a_right, at] = value

    spread_chunk(src, interp, 0, buffers[0], comps)
    near_side(
        table, ids, fops, fine, rows, cols, sides, own + side, side, (1 - a_right) * (fcols - 2), store
    )
    for at in range(near_a.shape[0]):
        near_b[a_right, at] = near_a[at]

    for j in range(steps):
        if j + 1 < steps:
            spread_chunk(src, interp, j + 1, buffers[(j + 1) % 2], comps)
        shift = shifts(trig, j, comps)
        lanes = slice(j * CHUNK, (j + 1) * CHUNK)
        pat_b, child = patterns[j % 2], children[j % 2]
        aggregate_chunk(buffers[j % 2], shift, pat_b, slice(0, CHUNK), width, sides)
        spots = []
        for lane in range(j * CHUNK, (j + 1) * CHUNK, piece_w):
            spots.append((info[1, lane // pops.shape[3]], lane % pops.shape[3]))
        for c in range(cols):
            for start in range(2):
                members = range(start, rows, 2)
                group = [2 * rows * fcols + r * cols + c for r in members]
                sums = [None] * len(group)
                for first, count, ref, cut in (
                    (0, par_own, pat_own, lanes),
                    (par_own, par_side, pat_a, lanes),
                    (par_own + par_side, par_side, pat_b, slice(0, CHUNK)),
                ):
                    for t in range(first, first + count):
                        op_id = ids[group[0], t]
                        coefs = [
                            jnp.concatenate(
                                [row_of(pops, (e, op_id), i, at, piece_w, comps) for e, at in spots], axis=1
                            )
                            for i in range(2)
                        ]
                        add_slots(sums, coefs, [ref[table[box, t], :, cut] for box in group])
                for r, (real, imag) in zip(members, sums):
                    total = (real + times_i(imag, sides)).astype(BF16).astype(F32)
                    turned = times_i(total, sides)
                    for k in range(4):
                        at = (2 * r + k // 2) * fcols + 2 * c + k % 2
                        child[at] = (shift[k] * total - shift[4 + k] * turned).astype(BF16)
        back = lax.dot_general(
            child[...].reshape(-1, CHUNK), interp[:, lanes], (((1,), (1,)), ((), ())),
            preferred_element_type=F32,
        ).reshape(acc.shape)
        acc[...] = back if j == 0 else acc[...] + back

    scale = fdirs / interp.shape[1]
    for r in range(2 * rows):
        for c in range(fcols):
            at = r * fcols + c
            value = near_own[at] + acc[at] * scale
            if c < 2:
                value = value + near_b[0, r * 2 + c]
            if c >= fcols - 2:
                value = value + near_b[1, r * 2 + c - (fcols - 2)]
            out[r, c, 0] = value[:sides]
            out[r, c, 1] = value[sides:]


def per_device(
    fine_out, interp, child_phase, fine_ops, parent_ops, fine_src, fine_op, parent_src, parent_op
):
    frows, fcols, _, sides, fdirs = fine_out.shape
    rows, cols = frows // 2, fcols // 2
    comps = 2 * sides
    pdirs = interp.shape[1]
    assert all(size == cols for size in halo_sizes(cols)) and pdirs % CHUNK == 0
    patch_odd = lax.rem(lax.axis_index("patch"), 2)
    dir_at = lax.axis_index("dir")
    dir_odd = lax.rem(dir_at, 2)
    height = rows + sum(halo_sizes(rows))
    boxes = height * cols
    n_dir, bits = lax.axis_size("dir"), swap_bits("dir")

    own = fine_out.reshape(frows * fcols * comps, fdirs)
    patch_halo = exchange(own, "patch", 2 * fcols * comps, rows)
    strip = jnp.concatenate([own] + patch_halo, axis=0)
    side_a, side_b = exchange(strip, "dir", 1, cols)

    pops = parent_ops[None]
    for bit in reversed(range(bits)):
        pops = gather_stage(pops, "dir", bit)
    shard = parent_ops.shape[2]
    if shard % 128 == 0 and CHUNK % shard == 0:
        spots = functools.reduce(
            jnp.add, [(((jnp.arange(n_dir, dtype=jnp.int32) ^ dir_at) >> b) & 1) << (bits - 1 - b) for b in range(bits)],
            jnp.zeros((n_dir,), jnp.int32),
        )
    else:
        pops = in_order(pops, "dir")
        spots = jnp.zeros((n_dir,), jnp.int32)
    info = jnp.stack([jnp.full((n_dir,), 1 - dir_odd, jnp.int32), spots])

    sources, op_ids = build_tables(rows, cols, {2: 4 * boxes, 1: boxes})
    which = patch_odd * 2 + dir_odd
    sources, ids = jnp.asarray(sources)[which], jnp.asarray(op_ids)[which]
    lists = jnp.concatenate([
        lax.dynamic_slice_in_dim(op, dir_at * width, width, 1).reshape(-1, 1, op.shape[2])
        for op, width in ((fine_op, fcols), (parent_op, cols))
    ])
    present = jnp.any(lists == ids[:, :, None], axis=2)
    nothing = np.array([4 * boxes] * (frows * fcols) + [boxes] * (rows * cols), np.int32)[:, None]
    table = jnp.where(present, sources, jnp.asarray(nothing))

    smem = pl.BlockSpec(memory_space=pltpu.SMEM)
    vmem = pl.BlockSpec(memory_space=pltpu.VMEM)
    params = pltpu.CompilerParams(vmem_limit_bytes=40 * 1024 * 1024)
    pattern = jax.ShapeDtypeStruct((boxes + 1, comps, pdirs), F32)
    fine_scratch = pltpu.VMEM((4 * boxes + 1, comps, fdirs), F32)
    spread = pltpu.VMEM((4 * boxes, comps, CHUNK), F32)
    half_pattern = pltpu.VMEM((boxes + 1, comps, CHUNK), F32)
    child = pltpu.VMEM((frows * fcols, comps, CHUNK), BF16)
    pat_own, near_own, trig = pl.pallas_call(
        functools.partial(own_kernel, rows, cols, sides),
        out_shape=[
            pattern,
            jax.ShapeDtypeStruct((frows * fcols, comps, fdirs), F32),
            jax.ShapeDtypeStruct((8, pdirs), F32),
        ],
        in_specs=[smem] + [vmem] * 4,
        out_specs=[vmem] * 3,
        scratch_shapes=[fine_scratch, spread, spread],
        compiler_params=params,
        name="own",
    )(table, strip, interp, child_phase, fine_ops)
    pat_a, near_a = pl.pallas_call(
        functools.partial(side_kernel, rows, cols, sides),
        out_shape=[pattern, jax.ShapeDtypeStruct((frows * 2, comps, fdirs), F32)],
        in_specs=[smem] * 3 + [vmem] * 4,
        out_specs=[vmem] * 2,
        scratch_shapes=[fine_scratch, spread, spread],
        compiler_params=params,
        name="side",
    )(table, ids, info, side_a, interp, trig, fine_ops)
    return pl.pallas_call(
        functools.partial(last_kernel, rows, cols, sides),
        out_shape=jax.ShapeDtypeStruct(fine_out.shape, F32),
        in_specs=[smem] * 3 + [vmem] * 9,
        out_specs=vmem,
        scratch_shapes=[
            fine_scratch, spread, spread, half_pattern, half_pattern, child, child,
            pltpu.VMEM((2, frows * 2, comps, fdirs), F32),
            pltpu.VMEM((frows * fcols, comps, fdirs), F32),
        ],
        compiler_params=params,
        name="last",
    )(table, ids, info, side_b, interp, trig, fine_ops, pops, pat_own, pat_a, near_own, near_a)


def solution(mesh):
    in_specs = (
        P("patch", "dir", None, None, None),
        P(),
        P(),
        P(),
        P(None, None, "dir"),
        P("patch", None, None),
        P("patch", None, None),
        P("patch", None, None),
        P("patch", None, None),
    )
    out_specs = P("patch", "dir", None, None, None)
    return jax.shard_map(
        per_device, mesh=mesh, in_specs=in_specs, out_specs=out_specs, check_vma=False
    )
```

profile of v0, /device:TPU:3, one launch (start us, length us, event | category | flops | bytes accessed | tf_op | source)
XLA Modules:
  0.0 33.5 jit_solution(6019916465250397414)
XLA Ops:
  0.0 0.0 copy-start
  0.0 0.0 copy-start.4
  0.0 2.3 %collective-permute-start.3 = (f32[1,40,2,256]{3,2,1,0:T(2,128)}, f32[1,40,2,256]{3,2,1,0:T(2,128)S(1)}, u32[]{:S(2)}, u32[]{:S(2)}) collective-permute-start(f32[1,40,2,256]{3,2,1,0:T(2,128)} %bitcast.8), channel_id=1, source_target_pairs={{0,4},{1,5},{2,6},{3,7},{4,0},{5,1},{6,2},{7,3},{8,12},{9,13},{10,... | collective-permute-start | bytes 245768 | tf_op jit(solution)/shard_map/ppermute | solution.py:122
  2.3 1.0 %reshape.52 = bf16[192,512]{1,0:T(8,128)(2,1)S(1)} reshape(bf16[6,4,2,4,512]{4,3,2,1,0:T(4,128)(2,1)} %param.12) | data formatting | bytes 393216 | tf_op jit(solution)/shard_map/reshape | solution.py:339
  3.3 0.3 collective-permute-start
  3.6 0.0 copy-start.2
  3.6 0.7 %constant_dynamic-slice_fusion = bf16[128,512]{1,0:T(8,128)(2,1)} fusion(bf16[192,512]{1,0:T(8,128)(2,1)S(1)} %reshape.52, s32[]{:T(128)S(6)} %select_n.21), kind=kLoop, calls=%fused_computation.10 | loop fusion | bytes 262148 | tf_op jit(solution)/shard_map/dynamic_slice | solution.py:112
  4.3 0.0 copy-start.5
  4.3 4.2 %collective-permute-start.1 = (bf16[128,512]{1,0:T(8,128)(2,1)}, bf16[128,512]{1,0:T(8,128)(2,1)}, u32[]{:S(2)}, u32[]{:S(2)}) collective-permute-start(bf16[128,512]{1,0:T(8,128)(2,1)} %constant_dynamic-slice_fusion), channel_id=1, source_target_pairs={{8,16},{16,8},{9,17},{17,9},{10,18},{18,10},{11,19},{19,11},{12,20... | collective-permute-start | bytes 393224 | tf_op jit(solution)/shard_map/ppermute | solution.py:113
  8.5 0.0 copy-start.1
  8.5 0.0 copy-start.3
  8.6 0.9 %constant_dynamic-slice_fusion.1 = s32[3,2,32]{2,1,0:T(2,128)S(1)} fusion(s32[3,16,32]{2,1,0:T(8,128)} %param.18, s32[]{:T(128)S(6)} %select_n.18), kind=kLoop, calls=%fused_computation.11 | loop fusion | bytes 1540 | tf_op jit(solution)/shard_map/dynamic_slice | solution.py:362
  9.5 0.0 copy-done
  9.5 0.7 %dynamic-slice_bitcast_fusion.ids = s32[30,42]{1,0:T(8,128)S(1)} fusion(s32[4,30,42]{2,1,0:T(8,128)} %constant.40.clone, s32[]{:T(128)S(6)} %select_n.19), kind=kLoop, calls=%fused_computation.6 | loop fusion | bytes 10084 | tf_op jit(solution)/shard_map/eq | solution.py:365
  10.2 0.0 collective-permute-done.3
  10.2 0.0 copy-done.4
  10.2 0.1 pad_maximum_fusion.2
  10.3 1.4 %collective-permute-start.4 = (f32[2,40,2,256]{3,2,1,0:T(2,128)S(1)}, f32[2,40,2,256]{3,2,1,0:T(2,128)S(1)}, u32[]{:S(2)}, u32[]{:S(2)}) collective-permute-start(f32[2,40,2,256]{3,2,1,0:T(2,128)S(1)} %pad_maximum_fusion.2), channel_id=1, source_target_pairs={{0,2},{1,3},{2,0},{3,1},{4,6},{5,7},{6,4},{7,5},{8,10},{9,11},{10,... | collective-permute-start | bytes 491528 | tf_op jit(solution)/shard_map/ppermute | solution.py:122
  11.7 0.0 collective-permute-done
  11.7 1.4 %collective-permute-done.1 = bf16[128,512]{1,0:T(8,128)(2,1)} collective-permute-done((bf16[128,512]{1,0:T(8,128)(2,1)}, bf16[128,512]{1,0:T(8,128)(2,1)}, u32[]{:S(2)}, u32[]{:S(2)}) %collective-permute-start.1) | collective-permute-done | bytes 131104 | tf_op jit(solution)/shard_map/ppermute | solution.py:113
  13.1 0.9 %constant_dynamic-update-slice_fusion.src = bf16[512,512]{1,0:T(8,128)(2,1)S(1)} fusion(bf16[512,512]{1,0:T(8,128)(2,1)S(1)} %constant_dynamic-update-slice_fusion.1, bf16[128,512]{1,0:T(8,128)(2,1)} %collective-permute-done.1), kind=kLoop, calls=%fused_computation.7 | loop fusion | bytes 262144 | tf_op jit(solution)/shard_map/concatenate | solution.py:341
  14.0 1.5 %collective-permute-start.6 = (bf16[512,512]{1,0:T(8,128)(2,1)S(1)}, bf16[512,512]{1,0:T(8,128)(2,1)S(1)}, u32[]{:S(2)}, u32[]{:S(2)}) collective-permute-start(bf16[512,512]{1,0:T(8,128)(2,1)S(1)} %constant_dynamic-update-slice_fusion.src), channel_id=1, source_target_pairs={{0,1},{1,0},{2,3},{3,2},{4,5},{5,4},{6,7},{7,6},{8,9},{9,8},{10,11... | collective-permute-start | bytes 1572872 | tf_op jit(solution)/shard_map/ppermute | solution.py:113
  15.5 3.1 %collective-permute-start.2 = (bf16[512,512]{1,0:T(8,128)(2,1)S(1)}, bf16[512,512]{1,0:T(8,128)(2,1)S(1)}, u32[]{:S(2)}, u32[]{:S(2)}) collective-permute-start(bf16[512,512]{1,0:T(8,128)(2,1)S(1)} %constant_dynamic-update-slice_fusion.src), channel_id=1, source_target_pairs={{1,2},{2,1},{3,4},{4,3},{5,6},{6,5},{9,10},{10,9},{11,12},{12,11},... | collective-permute-start | bytes 1572872 | tf_op jit(solution)/shard_map/ppermute | solution.py:113
  18.6 0.0 collective-permute-done.4
  18.7 0.2 pad_maximum_fusion.1
  18.8 0.1 collective-permute-start.5
  18.9 0.2 compare_reduce_fusion
  19.1 0.0 copy-done.5
  19.1 0.8 %bitcast_select_fusion.table = s32[30,42]{1,0:T(8,128)S(1)} fusion(pred[30,42]{1,0:T(8,128)(4,1)S(1)} %compare_reduce_fusion, s32[4,30,42]{2,1,0:T(8,128)} %constant.39.clone, s32[]{:T(128)S(6)} %select_n.19, s32[30]{0:T(128)S(1)} %copy-done.5), kind=kLoop, calls=%fused_computation.5 | loop fusion | flops 1260 | bytes 11464 | tf_op jit(solution)/shard_map/jit(_where)/select_n | solution.py:367
  19.9 0.0 copy-done.2
  19.9 0.0 copy-done.1
  19.9 0.0 copy-done.3
  19.9 3.2 %own.1 = (f32[17,8,2048]{2,1,0:T(8,128)S(1)}, f32[24,8,512]{2,1,0:T(8,128)S(1)}, f32[8,2048]{1,0:T(8,128)S(1)}) custom-call(s32[30,42]{1,0:T(8,128)S(1)} %bitcast_select_fusion.table, bf16[512,512]{1,0:T(8,128)(2,1)S(1)} %constant_dynamic-update-slice_fusion.src, bf16[512,2048]{1,0:T(8,128)(2,1)S(1)} %copy-done.1, f32[4,2048]{1,0:T(4,128)S(1)} %copy-done.3, ...), custom_call_target="tpu_custom_call" | custom-call | tf_op jit(solution)/shard_map/own/pallas_call | solution.py:377
  23.1 0.0 collective-permute-done.5
  23.1 0.3 pad_maximum_fusion.pops
  23.5 0.0 collective-permute-done.6.src
  23.5 2.9 %side.1 = (f32[17,8,2048]{2,1,0:T(8,128)S(1)}, f32[12,8,512]{2,1,0:T(8,128)S(1)}) custom-call(s32[30,42]{1,0:T(8,128)S(1)} %bitcast_select_fusion.table, s32[30,42]{1,0:T(8,128)S(1)} %dynamic-slice_bitcast_fusion.ids, s32[2,8]{1,0:T(2,128)S(1)} %stack.4.info, bf16[512,512]{1,0:T(8,128)(2,1)S(1)} %collective-permute-done.6.src, ...), custom_call_target="tpu_custom_call" | custom-call | tf_op jit(solution)/shard_map/side/pallas_call | solution.py:390
  26.4 0.0 collective-permute-done.2.src
  26.4 7.0 %last.1 = f32[6,4,2,4,512]{4,3,2,1,0:T(4,128)} custom-call(s32[30,42]{1,0:T(8,128)S(1)} %bitcast_select_fusion.table, s32[30,42]{1,0:T(8,128)S(1)} %dynamic-slice_bitcast_fusion.ids, s32[2,8]{1,0:T(2,128)S(1)} %stack.4.info, bf16[512,512]{1,0:T(8,128)(2,1)S(1)} %collective-permute-done.2.src, bf16[512,2048]{1,0:T(8,128)(2,1)S(1)} %copy-done.1, ...), custom_call_target="tpu_custom_call" | custom-call | tf_op jit(solution)/shard_map/last/pallas_call | solution.py:399
  (7 shorter events, 0.1 us)
Async XLA Ops:
  0.0 9.5 %copy-start = (s32[6,32,32]{2,1,0:T(8,128)S(1)}, s32[6,32,32]{2,1,0:T(8,128)}, u32[]{:S(2)}) copy-start(s32[6,32,32]{2,1,0:T(8,128)} %param.17) | copy-start | bytes 73732
  0.0 10.2 %copy-start.4 = (f32[40,2,256]{2,1,0:T(2,128)S(1)}, f32[40,2,256]{2,1,0:T(2,128)}, u32[]{:S(2)}) copy-start(f32[40,2,256]{2,1,0:T(2,128)} %param.16) | copy-start | bytes 245764
  0.0 10.2 %collective-permute-start.3 = (f32[1,40,2,256]{3,2,1,0:T(2,128)}, f32[1,40,2,256]{3,2,1,0:T(2,128)S(1)}, u32[]{:S(2)}, u32[]{:S(2)}) collective-permute-start(f32[1,40,2,256]{3,2,1,0:T(2,128)} %bitcast.8), channel_id=1, source_target_pairs={{0,4},{1,5},{2,6},{3,7},{4,0},{5,1},{6,2},{7,3},{8,12},{9,13},{10,... | collective-permute-start | bytes 245768 | tf_op jit(solution)/shard_map/ppermute | solution.py:122
  3.3 8.4 %collective-permute-start = (bf16[192,512]{1,0:T(8,128)(2,1)S(1)}, bf16[192,512]{1,0:T(8,128)(2,1)S(1)}, u32[]{:S(2)}, u32[]{:S(2)}) collective-permute-start(bf16[192,512]{1,0:T(8,128)(2,1)S(1)} %reshape.52), channel_id=1, source_target_pairs={{0,8},{8,0},{16,24},{24,16},{1,9},{9,1},{17,25},{25,17},{2,10},{10... | collective-permute-start | bytes 589832 | tf_op jit(solution)/shard_map/ppermute | solution.py:113
  3.6 16.3 %copy-start.2 = (f32[40,2,512]{2,1,0:T(2,128)S(1)}, f32[40,2,512]{2,1,0:T(2,128)}, u32[]{:S(2)}) copy-start(f32[40,2,512]{2,1,0:T(2,128)} %fops.5) | copy-start | bytes 491524
  4.3 14.8 %copy-start.5 = (s32[30]{0:T(128)S(1)}, s32[30]{0:T(128)}, u32[]{:S(2)}) copy-start(s32[30]{0:T(128)} %constant.47) | copy-start | bytes 364
  4.3 8.8 %collective-permute-start.1 = (bf16[128,512]{1,0:T(8,128)(2,1)}, bf16[128,512]{1,0:T(8,128)(2,1)}, u32[]{:S(2)}, u32[]{:S(2)}) collective-permute-start(bf16[128,512]{1,0:T(8,128)(2,1)} %constant_dynamic-slice_fusion), channel_id=1, source_target_pairs={{8,16},{16,8},{9,17},{17,9},{10,18},{18,10},{11,19},{19,11},{12,20... | collective-permute-start | bytes 393224 | tf_op jit(solution)/shard_map/ppermute | solution.py:113
  8.5 11.4 %copy-start.1 = (bf16[512,2048]{1,0:T(8,128)(2,1)S(1)}, bf16[512,2048]{1,0:T(8,128)(2,1)}, u32[]{:S(2)}) copy-start(bf16[512,2048]{1,0:T(8,128)(2,1)} %interp.5) | copy-start | bytes 6291460
  8.5 11.4 %copy-start.3 = (f32[4,2048]{1,0:T(4,128)S(1)}, f32[4,2048]{1,0:T(4,128)}, u32[]{:S(2)}) copy-start(f32[4,2048]{1,0:T(4,128)} %phase.1) | copy-start | bytes 98308
  10.3 8.3 %collective-permute-start.4 = (f32[2,40,2,256]{3,2,1,0:T(2,128)S(1)}, f32[2,40,2,256]{3,2,1,0:T(2,128)S(1)}, u32[]{:S(2)}, u32[]{:S(2)}) collective-permute-start(f32[2,40,2,256]{3,2,1,0:T(2,128)S(1)} %pad_maximum_fusion.2), channel_id=1, source_target_pairs={{0,2},{1,3},{2,0},{3,1},{4,6},{5,7},{6,4},{7,5},{8,10},{9,11},{10,... | collective-permute-start | bytes 491528 | tf_op jit(solution)/shard_map/ppermute | solution.py:122
  14.0 9.5 %collective-permute-start.6 = (bf16[512,512]{1,0:T(8,128)(2,1)S(1)}, bf16[512,512]{1,0:T(8,128)(2,1)S(1)}, u32[]{:S(2)}, u32[]{:S(2)}) collective-permute-start(bf16[512,512]{1,0:T(8,128)(2,1)S(1)} %constant_dynamic-update-slice_fusion.src), channel_id=1, source_target_pairs={{0,1},{1,0},{2,3},{3,2},{4,5},{5,4},{6,7},{7,6},{8,9},{9,8},{10,11... | collective-permute-start | bytes 1572872 | tf_op jit(solution)/shard_map/ppermute | solution.py:113
  15.5 10.9 %collective-permute-start.2 = (bf16[512,512]{1,0:T(8,128)(2,1)S(1)}, bf16[512,512]{1,0:T(8,128)(2,1)S(1)}, u32[]{:S(2)}, u32[]{:S(2)}) collective-permute-start(bf16[512,512]{1,0:T(8,128)(2,1)S(1)} %constant_dynamic-update-slice_fusion.src), channel_id=1, source_target_pairs={{1,2},{2,1},{3,4},{4,3},{5,6},{6,5},{9,10},{10,9},{11,12},{12,11},... | collective-permute-start | bytes 1572872 | tf_op jit(solution)/shard_map/ppermute | solution.py:113
  18.8 4.3 %collective-permute-start.5 = (f32[4,40,2,256]{3,2,1,0:T(2,128)S(1)}, f32[4,40,2,256]{3,2,1,0:T(2,128)S(1)}, u32[]{:S(2)}, u32[]{:S(2)}) collective-permute-start(f32[4,40,2,256]{3,2,1,0:T(2,128)S(1)} %pad_maximum_fusion.1), channel_id=1, source_target_pairs={{0,1},{1,0},{2,3},{3,2},{4,5},{5,4},{6,7},{7,6},{8,9},{9,8},{10,11... | collective-permute-start | bytes 983048 | tf_op jit(solution)/shard_map/ppermute | solution.py:122
where the time goes:
time: 34 us; the launch traced here: 33.5 us
  Pallas kernels  13.2 us (39%)
  starting transfers between devices  12.9 us (38%)
  local copies, waits for them, and re-layouts  4.23 us (12%)
  other arithmetic  1.59 us (5%)
  waiting for transfers between devices  1.42 us (4%)
    ppermute x4, starting transfers between devices, exchange(): got.append(lax.ppermute(edge, axis, pairs(n, first)))  9.14 us
    pallas_call x1, Pallas kernels, per_device(): pl.pallas_call(functools.partial(last_kernel, rows, cols, sides), out_sha...  7.04 us
    ppermute x3, starting transfers between devices, gather_stage(): lax.ppermute(block, axis, [(i, i ^ 1 << bit) for i in range(lax.axis_size...  3.74 us
    pallas_call x1, Pallas kernels, per_device(): pl.pallas_call(functools.partial(own_kernel, rows, cols, sides), out_shap...  3.18 us
    pallas_call x1, Pallas kernels, per_device(): pl.pallas_call(functools.partial(side_kernel, rows, cols, sides), out_sha...  2.95 us
    ppermute x4, waiting for transfers between devices, exchange(): got.append(lax.ppermute(edge, axis, pairs(n, first)))  1.41 us
    reshape x1, local copies, waits for them, and re-layouts, per_device(): own = fine_out.reshape(frows * fcols * comps, fdirs)  0.98 us
    concatenate x1, local copies, waits for them, and re-layouts, per_device(): strip = jnp.concatenate([own] + patch_halo, axis=0)  0.91 us
  transfers between devices with their start and end apart: 7, of which 1 were waited for; matrix products, arithmetic and copies ran while one was open for 17% of the time, Pallas kernels for 18%

commit v1 on v0

v1 whole, which is shorter than its diff:
```python
import functools

import jax
import jax.numpy as jnp
import numpy as np
from jax import lax
from jax.experimental import pallas as pl
from jax.experimental.pallas import tpu as pltpu
from jax.sharding import PartitionSpec as P

CHUNK = 512
F32, BF16 = jnp.float32, jnp.bfloat16


def offset_pairs():
    return [(dr, dc) for dr in range(-3, 4) for dc in range(-3, 4) if max(abs(dr), abs(dc)) > 1]


def class_offsets(row_odd, col_odd):
    return [
        (op_id, dr, dc)
        for op_id, (dr, dc) in enumerate(offset_pairs())
        if -2 <= dr + row_odd <= 3 and -2 <= dc + col_odd <= 3
    ]


def halo_sizes(count):
    return (3, 2) if count % 2 else (2, 2)


def stored_at(rel, count, odd):
    first, second = halo_sizes(count)
    if 0 <= rel < count:
        return rel
    if rel < 0:
        return count + first + rel if odd else count + first + second + rel
    return rel if not odd else rel + first


def place(row, col, rows, cols, row_odd, col_odd, scale):
    at_r = stored_at(row // scale, rows, row_odd) * scale + row % scale
    at_c = stored_at(col // scale, cols, col_odd) * scale + col % scale
    for group, width in enumerate((cols, *halo_sizes(cols))):
        if at_c < width * scale:
            return group, at_r * width * scale + at_c
        at_c -= width * scale


def fine_slots(row, col, rows, cols, row_odd, col_odd):
    inside, found = 4 * rows * cols, ([], [], [], [])
    for op_id, dr, dc in class_offsets(row % 2, col % 2):
        group, index = place(row + dr, col + dc, rows, cols, row_odd, col_odd, 2)
        if group:
            found[group + 1].append((op_id, index))
        elif index >= inside:
            found[0].append((op_id, None))
            found[1].append((op_id, index - inside))
        else:
            found[0].append((op_id, index))
    return found


def parent_slots(row, col, rows, cols, row_odd, col_odd):
    found = ([], [], [])
    for op_id, dr, dc in class_offsets((row + row_odd * rows) % 2, (col + col_odd * cols) % 2):
        group, index = place(row + dr, col + dc, rows, cols, row_odd, col_odd, 1)
        found[group].append((op_id, index))
    return found


PARITIES = [(a, b) for a in range(2) for b in range(2)]


def slot_counts(rows, cols, scale):
    slots = fine_slots if scale == 2 else parent_slots
    lists = [
        [len(found) for found in slots(r, c, rows, cols, *odd)]
        for odd in PARITIES for r in range(rows * scale) for c in range(cols * scale)
    ]
    most = [max(column) for column in zip(*lists)]
    return most[:-2] + [max(most[-2:])] * 2


def starts(counts):
    return [sum(counts[:i]) for i in range(len(counts))]


def build_tables(rows, cols, zeros):
    counts = {scale: slot_counts(rows, cols, scale) for scale in (2, 1)}
    width = max(sum(c) for c in counts.values())
    sources, op_ids, nothing = [], [], []
    for odd in PARITIES:
        src_rows, id_rows, none_rows = [], [], []
        for scale, slots in ((2, fine_slots), (1, parent_slots)):
            for r in range(rows * scale):
                for c in range(cols * scale):
                    src_row, id_row, none_row = [], [], []
                    for size, found, zero in zip(counts[scale], slots(r, c, rows, cols, *odd), zeros[scale]):
                        found = found + [(0, None)] * (size - len(found))
                        src_row += [zero if at is None else at for _, at in found]
                        id_row += [o for o, _ in found]
                        none_row += [zero] * size
                    pad = [0] * (width - len(src_row))
                    src_rows.append(src_row + pad)
                    id_rows.append(id_row + pad)
                    none_rows.append(none_row + pad)
        sources.append(src_rows)
        op_ids.append(id_rows)
        nothing = none_rows
    return np.array(sources, np.int32), np.array(op_ids, np.int32), np.array(nothing, np.int32)


def pairs(count, first):
    if first:
        return [(i, i ^ 1) for i in range(count) if (i ^ 1) < count]
    found = []
    for i in range(1, count - 1, 2):
        found += [(i, i + 1), (i + 1, i)]
    return found


def exchange(block, axis, unit, count):
    n = lax.axis_size(axis)
    odd = lax.rem(lax.axis_index(axis), 2)
    got = []
    for first, size in zip((True, False), halo_sizes(count)):
        edge = block
        if size < count:
            low = (1 - odd) if first else odd
            edge = lax.dynamic_slice_in_dim(block, low * ((count - size) * unit), size * unit, 0)
        got.append(lax.ppermute(edge, axis, pairs(n, first)))
    return got


def swap_bits(axis):
    return lax.axis_size(axis).bit_length() - 1


def in_order(block, axis):
    n, bits = lax.axis_size(axis), swap_bits(axis)
    spots = [int(format(s, "0%db" % bits)[::-1], 2) for s in range(n)] if bits else [0]
    at = jnp.asarray(np.array(spots, np.int32))[jnp.arange(n, dtype=jnp.int32) ^ lax.axis_index(axis)]
    block = jnp.take(block, at, axis=0)
    return block.transpose(1, 2, 0, 3).reshape(1, block.shape[1], 2, n * block.shape[3])


def times_i(v, sides):
    sign = jnp.where(lax.broadcasted_iota(jnp.int32, (2 * sides, 1), 0) < sides, -1.0, 1.0)
    return sign.astype(F32) * pltpu.roll(v, sides, 0)


def row_of(ref, lead, part, lane, width, comps):
    return jnp.broadcast_to(ref[(*lead, slice(part, part + 1), pl.ds(lane, width))], (comps, width))


def add_slots(sums, coefs, pieces):
    real, imag = coefs
    for m, piece in enumerate(pieces):
        add = [real * piece, imag * piece]
        sums[m] = add if sums[m] is None else [a + b for a, b in zip(sums[m], add)]


def widen(src, fine, comps):
    count = src.shape[0] // comps
    fine[:count] = src[...].astype(F32).reshape(count, comps, src.shape[1])
    fine[count] = jnp.zeros(fine.shape[1:], F32)


def spread_chunk(src, interp, j, buffer, comps):
    lanes = slice(j * CHUNK, (j + 1) * CHUNK)
    out = jnp.dot(src[...], interp[:, lanes], preferred_element_type=F32)
    buffer[...] = out.reshape(-1, comps, CHUNK)


def shifts(trig, j, comps, width=CHUNK):
    lanes = slice(j * CHUNK, j * CHUNK + width)
    return [jnp.broadcast_to(trig[k : k + 1, lanes], (comps, width)) for k in range(8)]


def aggregate_chunk(buffer, shift, pattern, lanes, width, sides, base=0):
    for q in range(buffer.shape[0] // 4):
        r, c = divmod(q, width)
        total = [None, None]
        for k in range(4):
            piece = buffer[(2 * r + k // 2) * (2 * width) + 2 * c + k % 2]
            for i in range(2):
                add = shift[4 * i + k] * piece
                total[i] = add if k == 0 else total[i] + add
        whole = total[0] + times_i(total[1], sides)
        pattern[base + q, :, lanes] = whole.astype(BF16).astype(F32)


def aggregate(src, interp, trig, buffers, pattern, width, sides, base=0, done=lambda j: None):
    comps = 2 * sides
    steps = interp.shape[1] // CHUNK
    spread_chunk(src, interp, 0, buffers[0], comps)
    for j in range(steps):
        if j + 1 < steps:
            spread_chunk(src, interp, j + 1, buffers[(j + 1) % 2], comps)
        lanes = slice(j * CHUNK, (j + 1) * CHUNK)
        aggregate_chunk(buffers[j % 2], shifts(trig, j, comps), pattern, lanes, width, sides, base)
        done(j)


def zero_box(pattern):
    pattern[pattern.shape[0] - 1] = jnp.zeros(pattern.shape[1:], F32)


def near_sums(table, fops, fine, group, base, op_ids):
    comps, fdirs = fine.shape[1:]
    sums = [None] * len(group)
    for t, op_id in enumerate(op_ids, base):
        coefs = [row_of(fops, (op_id,), i, 0, fdirs, comps) for i in range(2)]
        add_slots(sums, coefs, [fine[table[box, t]] for box in group])
    return [real + times_i(imag, comps // 2) for real, imag in sums]


def near_side(table, ids, fops, fine, rows, cols, base, count, first_col, store):
    for a in range(2):
        for c in range(2):
            group = [(2 * r + a) * (2 * cols) + first_col + c for r in range(rows)]
            op_ids = [ids[group[0], t] for t in range(base, base + count)]
            for r, value in enumerate(near_sums(table, fops, fine, group, base, op_ids)):
                store((2 * r + a) * 2 + c, value)


def block_kernel(rows, cols, sides, table, src, interp, phase, fops, pattern, near, trig, fine, even, odd):
    trig[:4] = jnp.cos(phase[...])
    trig[4:] = jnp.sin(phase[...])
    widen(src, fine, 2 * sides)
    aggregate(src, interp, trig, (even, odd), pattern, cols, sides)
    for a in range(2):
        for c in range(2 * cols):
            op_ids = [o for o, _ in fine_slots(a, c, rows, cols, 0, 0)[0]]
            group = [(2 * r + a) * (2 * cols) + c for r in range(rows)]
            for box, value in zip(group, near_sums(table, fops, fine, group, 0, op_ids)):
                near[box] = value


def halo_kernel(
    rows, cols, sides, table, src, interp, trig, fops, pat_block, near_block, pattern, near, fine, even, odd
):
    base = starts(slot_counts(rows, cols, 2))[1]
    widen(src, fine, 2 * sides)
    near[...] = near_block[...]
    pattern[: pat_block.shape[0]] = pat_block[...]
    aggregate(src, interp, trig, (even, odd), pattern, cols, sides, pat_block.shape[0])
    zero_box(pattern)
    for r in range(2 * rows):
        for c in range(2 * cols):
            op_ids = [o for o, _ in fine_slots(r, c, rows, cols, 0, 0)[1]]
            if op_ids:
                box = r * 2 * cols + c
                near[box] += near_sums(table, fops, fine, [box], base, op_ids)[0]


def side_kernel(rows, cols, sides, table, ids, info, src, interp, trig, fops, pattern, near, fine, even, odd):
    counts = slot_counts(rows, cols, 2)
    widen(src, fine, 2 * sides)

    def store(at, value):
        near[at] = value

    aggregate(src, interp, trig, (even, odd), pattern, halo_sizes(cols)[0], sides)
    zero_box(pattern)
    near_side(
        table, ids, fops, fine, rows, cols, starts(counts)[2], counts[2], info[0, 0] * (2 * cols - 2), store
    )


def parent_groups(rows, cols):
    return [[(r, c) for r in range(start, rows, 2)] for c in range(cols) for start in range(2)]


def parent_sums(rows, cols, sides, table, ids, pops, sources, group, first, width):
    comps = 2 * sides
    rows_at = [4 * rows * cols + r * cols + c for r, c in group]
    sums = [None] * len(group)
    for base, count, ref in sources:
        for t in range(base, base + count):
            op_id = ids[rows_at[0], t]
            coefs = [row_of(pops, (op_id,), i, first, width, comps) for i in range(2)]
            add_slots(sums, coefs, [ref[table[row, t], :, first : first + width] for row in rows_at])
    return sums


def inner_kernel(rows, cols, sides, table, ids, info, pat_own, pat_a, *refs):
    *shards, pops, real, imag = refs
    at = 0
    for ref in shards:
        held = ref.shape[3]
        for k in range(ref.shape[0]):
            lane = pl.multiple_of(info[1, at] * held, held)
            pops[:, :, pl.ds(lane, held)] = ref[k]
            at += 1
    counts = slot_counts(rows, cols, 1)
    at = starts(counts)
    sources = [(at[0], counts[0], pat_own), (at[1], counts[1], pat_a)]
    for first in range(0, real.shape[2], 2 * CHUNK):
        for group in parent_groups(rows, cols):
            sums = parent_sums(
                rows, cols, sides, table, ids, pops, sources, group, first, 2 * CHUNK
            )
            for (r, c), (re, im) in zip(group, sums):
                real[r * cols + c, :, first : first + 2 * CHUNK] = re
                imag[r * cols + c, :, first : first + 2 * CHUNK] = im


def last_kernel(
    rows, cols, sides,
    table, ids, info,
    src, interp, trig, fops, pops, real, imag, near_own, near_a,
    out,
    fine, even, odd, pat_b, child, near_b, acc,
):
    comps, fdirs = fine.shape[1:]
    fcols = 2 * cols
    wide = 2 * CHUNK
    counts = slot_counts(rows, cols, 2)
    par_counts = slot_counts(rows, cols, 1)
    a_right = info[0, 0]
    widen(src, fine, comps)
    zero_box(pat_b)

    def store(at, value):
        near_b[1 - a_right, at] = value

    near_side(
        table, ids, fops, fine, rows, cols, starts(counts)[3], counts[3], (1 - a_right) * (fcols - 2), store
    )
    for at in range(near_a.shape[0]):
        near_b[a_right, at] = near_a[at]

    def far(j):
        if j % 2 == 0:
            return
        first = (j - 1) * CHUNK
        shift = shifts(trig, j - 1, comps, wide)
        sources = [(starts(par_counts)[2], par_counts[2], pat_b)]
        for group in parent_groups(rows, cols):
            sums = parent_sums(rows, cols, sides, table, ids, pops, sources, group, first, wide)
            for (r, c), (re, im) in zip(group, sums):
                box = r * cols + c
                re = re + real[box, :, first : first + wide]
                im = im + imag[box, :, first : first + wide]
                total = (re + times_i(im, sides)).astype(BF16).astype(F32)
                turned = times_i(total, sides)
                for k in range(4):
                    at = (2 * r + k // 2) * fcols + 2 * c + k % 2
                    child[at, :, first : first + wide] = (
                        shift[k] * total - shift[4 + k] * turned
                    ).astype(BF16)
        back = lax.dot_general(
            child[:, :, first : first + wide].reshape(-1, wide), interp[:, first : first + wide],
            (((1,), (1,)), ((), ())), preferred_element_type=F32,
        ).reshape(acc.shape)
        acc[...] = back if j == 1 else acc[...] + back

    aggregate(src, interp, trig, (even, odd), pat_b, halo_sizes(cols)[1], sides, 0, far)

    scale = fdirs / interp.shape[1]
    for r in range(2 * rows):
        for c in range(fcols):
            at = r * fcols + c
            value = near_own[at] + acc[at] * scale
            if c < 2:
                value = value + near_b[0, r * 2 + c]
            if c >= fcols - 2:
                value = value + near_b[1, r * 2 + c - (fcols - 2)]
            out[r, c, 0] = value[:sides]
            out[r, c, 1] = value[sides:]


def per_device(
    fine_out, interp, child_phase, fine_ops, parent_ops, fine_src, fine_op, parent_src, parent_op
):
    frows, fcols, _, sides, fdirs = fine_out.shape
    rows, cols = frows // 2, fcols // 2
    comps = 2 * sides
    pdirs = interp.shape[1]
    assert all(size == cols for size in halo_sizes(cols)) and pdirs % (2 * CHUNK) == 0
    patch_odd = lax.rem(lax.axis_index("patch"), 2)
    dir_at = lax.axis_index("dir")
    dir_odd = lax.rem(dir_at, 2)
    height = rows + sum(halo_sizes(rows))
    boxes = height * cols
    n_dir, bits = lax.axis_size("dir"), swap_bits("dir")

    own = fine_out.reshape(frows * fcols * comps, fdirs)
    patch_halo = exchange(own, "patch", 2 * fcols * comps, rows)
    strip = jnp.concatenate([own] + patch_halo, axis=0)
    side_a, side_b = exchange(strip, "dir", 1, cols)

    shards = [parent_ops[None]]
    for bit in reversed(range(bits)):
        held = jnp.concatenate(shards, axis=0)
        shards.append(lax.ppermute(held, "dir", [(i, i ^ (1 << bit)) for i in range(n_dir)]))
    if parent_ops.shape[2] % 128 == 0:
        places = jnp.arange(n_dir, dtype=jnp.int32)
        spots = dir_at
        for b in range(bits):
            spots = spots ^ (((places >> b) & 1) << (bits - 1 - b))
    else:
        shards = [in_order(jnp.concatenate(shards, axis=0), "dir")]
        spots = jnp.zeros((n_dir,), jnp.int32)
    info = jnp.stack([jnp.full((n_dir,), 1 - dir_odd, jnp.int32), spots])

    outside = boxes - rows * cols
    sources, op_ids, nothing = build_tables(
        rows, cols, {2: [frows * fcols, 4 * outside, 4 * boxes, 4 * boxes], 1: [boxes] * 3}
    )
    which = patch_odd * 2 + dir_odd
    sources, ids = jnp.asarray(sources)[which], jnp.asarray(op_ids)[which]
    lists = jnp.concatenate([
        lax.dynamic_slice_in_dim(op, dir_at * width, width, 1).reshape(-1, 1, op.shape[2])
        for op, width in ((fine_op, fcols), (parent_op, cols))
    ])
    present = jnp.any(lists == ids[:, :, None], axis=2)
    table = jnp.where(present, sources, jnp.asarray(nothing))

    smem = pl.BlockSpec(memory_space=pltpu.SMEM)
    vmem = pl.BlockSpec(memory_space=pltpu.VMEM)

    def shape(*dims):
        return jax.ShapeDtypeStruct(dims, F32)

    def scratch(*dims, kind=F32):
        return pltpu.VMEM(dims, kind)

    def group_scratch(count):
        return [scratch(count + 1, comps, fdirs)] + [scratch(count, comps, CHUNK)] * 2

    def call(body, name, n_smem, outs, scratches, *args):
        return pl.pallas_call(
            functools.partial(body, rows, cols, sides),
            out_shape=outs,
            in_specs=[smem] * n_smem + [vmem] * (len(args) - n_smem),
            out_specs=[vmem] * len(outs),
            scratch_shapes=scratches,
            compiler_params=pltpu.CompilerParams(vmem_limit_bytes=40 * 1024 * 1024),
            name=name,
        )(*args)

    near = shape(frows * fcols, comps, fdirs)
    pattern = shape(boxes + 1, comps, pdirs)
    pat_block, near_block, trig = call(
        block_kernel, "block", 1,
        [shape(rows * cols, comps, pdirs), near, shape(8, pdirs)], group_scratch(frows * fcols),
        table, own, interp, child_phase, fine_ops,
    )
    pat_own, near_own = call(
        halo_kernel, "halo", 1, [pattern, near], group_scratch(4 * outside),
        table, strip[own.shape[0] :], interp, trig, fine_ops, pat_block, near_block,
    )
    pat_a, near_a = call(
        side_kernel, "side", 3, [pattern, shape(frows * 2, comps, fdirs)], group_scratch(4 * boxes),
        table, ids, info, side_a, interp, trig, fine_ops,
    )
    part = shape(rows * cols, comps, pdirs)
    pops, real, imag = call(
        inner_kernel, "inner", 3, [shape(parent_ops.shape[0], 2, pdirs), part, part], [],
        table, ids, info, pat_own, pat_a, *shards,
    )
    return call(
        last_kernel, "last", 3, [jax.ShapeDtypeStruct(fine_out.shape, F32)],
        group_scratch(4 * boxes) + [
            scratch(boxes + 1, comps, pdirs),
            scratch(frows * fcols, comps, pdirs, kind=BF16),
            scratch(2, frows * 2, comps, fdirs),
            scratch(frows * fcols, comps, fdirs),
        ],
        table, ids, info, side_b, interp, trig, fine_ops, pops, real, imag, near_own, near_a,
    )[0]


def solution(mesh):
    in_specs = (
        P("patch", "dir", None, None, None),
        P(),
        P(),
        P(),
        P(None, None, "dir"),
        P("patch", None, None),
        P("patch", None, None),
        P("patch", None, None),
        P("patch", None, None),
    )
    out_specs = P("patch", "dir", None, None, None)
    return jax.shard_map(
        per_device, mesh=mesh, in_specs=in_specs, out_specs=out_specs, check_vma=False
    )
```

time: 34 us -> 34.1 us (level)
  Pallas kernels: 13.2 us -> 15 us
  local copies, waits for them, and re-layouts: 4.23 us -> 2.66 us
  starting transfers between devices: 12.9 us -> 13.6 us
  other arithmetic: 1.59 us -> 1.21 us
  waiting for transfers between devices: 1.42 us -> 1.05 us
    pallas_call x3 -> x5, Pallas kernels: 13.2 us -> 15 us  [call(): pl.pallas_call(functools.partial(body, rows, cols, sides), out_shape=outs...]
    concatenate x1, local copies, waits for them, and re-layouts: 0.91 us -> 0.01 us  [per_device(): strip = jnp.concatenate([own] + patch_halo, axis=0)]
    ppermute x4, starting transfers between devices: 9.14 us -> 9.86 us  [exchange(): got.append(lax.ppermute(edge, axis, pairs(n, first)))]
    dynamic_slice x1, local copies, waits for them, and re-layouts: 0.66 us -> 0.01 us  [exchange(): lax.dynamic_slice_in_dim(block, low * ((count - size) * unit), size * uni...]
    ppermute x4, waiting for transfers between devices: 1.41 us -> 1.04 us  [exchange(): got.append(lax.ppermute(edge, axis, pairs(n, first)))]
  transfers between devices with their start and end apart: 7 -> 7, of which waited for: 1 -> 1; matrix products, arithmetic and copies ran while one was open for 17% -> 11% of each run, Pallas kernels for 18% -> 29%
where the time goes in v1:
time: 34.1 us; the launch traced here: 33.7 us
  Pallas kernels  15 us (44%)
  starting transfers between devices  13.6 us (40%)
  local copies, waits for them, and re-layouts  2.66 us (8%)
  other arithmetic  1.21 us (4%)
  waiting for transfers between devices  1.05 us (3%)
    pallas_call x5, Pallas kernels, call(): pl.pallas_call(functools.partial(body, rows, cols, sides), out_shape=outs...  15 us
    ppermute x4, starting transfers between devices, exchange(): got.append(lax.ppermute(edge, axis, pairs(n, first)))  9.86 us
    ppermute x3, starting transfers between devices, per_device(): lax.ppermute(held, 'dir', [(i, i ^ 1 << bit) for i in range(n_dir)])  3.74 us
    ppermute x4, waiting for transfers between devices, exchange(): got.append(lax.ppermute(edge, axis, pairs(n, first)))  1.04 us
    reshape x1, local copies, waits for them, and re-layouts, per_device(): own = fine_out.reshape(frows * fcols * comps, fdirs)  0.98 us
    eq x1, local copies, waits for them, and re-layouts, per_device(): present = jnp.any(lists == ids[:, :, None], axis=2)  0.86 us
    dynamic_slice x2, local copies, waits for them, and re-layouts, per_device(): lax.dynamic_slice_in_dim(op, dir_at * width, width, 1)  0.73 us
    select_n x1, other arithmetic, per_device(): table = jnp.where(present, sources, jnp.asarray(nothing))  0.73 us
  transfers between devices with their start and end apart: 7, of which 1 were waited for; matrix products, arithmetic and copies ran while one was open for 11% of the time, Pallas kernels for 29%

profile of v1, /device:TPU:3, one launch (start us, length us, event | category | flops | bytes accessed | tf_op | source)
XLA Modules:
  0.0 33.7 jit_solution(10413595850156996188)
XLA Ops:
  0.0 0.0 copy-start
  0.0 0.0 copy-start.3
  0.0 2.3 %collective-permute-start.4 = (f32[1,40,2,256]{3,2,1,0:T(2,128)}, f32[1,40,2,256]{3,2,1,0:T(2,128)S(1)}, u32[]{:S(2)}, u32[]{:S(2)}) collective-permute-start(f32[1,40,2,256]{3,2,1,0:T(2,128)} %bitcast.8), channel_id=1, source_target_pairs={{0,4},{1,5},{2,6},{3,7},{4,0},{5,1},{6,2},{7,3},{8,12},{9,13},{10,... | collective-permute-start | bytes 245768 | tf_op jit(solution)/shard_map/ppermute | solution.py:397
  2.3 1.0 %reshape.58.src = bf16[192,512]{1,0:T(8,128)(2,1)S(1)} reshape(bf16[6,4,2,4,512]{4,3,2,1,0:T(4,128)(2,1)} %param.12) | data formatting | bytes 393216 | tf_op jit(solution)/shard_map/reshape | solution.py:389
  3.3 0.3 collective-permute-start
  3.6 0.0 copy-start.2
  3.6 0.0 copy-start.5
  3.6 4.2 %collective-permute-start.1 = (bf16[128,512]{1,0:T(8,128)(2,1)S(1)}, bf16[128,512]{1,0:T(8,128)(2,1)S(1)}, u32[]{:S(2)}, u32[]{:S(2)}) collective-permute-start(bf16[128,512]{1,0:T(8,128)(2,1)S(1)} %constant_dynamic-slice_fusion), channel_id=1, source_target_pairs={{8,16},{16,8},{9,17},{17,9},{10,18},{18,10},{11,19},{19,11},{12,20... | collective-permute-start | bytes 393224 | tf_op jit(solution)/shard_map/ppermute | solution.py:131
  7.9 0.7 %constant_dynamic-slice_fusion.1 = s32[3,2,32]{2,1,0:T(2,128)S(1)} fusion(s32[3,16,32]{2,1,0:T(8,128)} %param.18, s32[]{:T(128)S(6)} %select_n.18), kind=kLoop, calls=%fused_computation.11 | loop fusion | bytes 1540 | tf_op jit(solution)/shard_map/dynamic_slice | solution.py:415
  8.6 0.0 copy-start.1
  8.6 0.0 copy-start.4
  8.6 0.0 copy-done
  8.7 0.9 %dynamic-slice_bitcast_fusion.ids = s32[30,50]{1,0:T(8,128)S(1)} fusion(s32[4,30,50]{2,1,0:T(8,128)} %constant.40.clone, s32[]{:T(128)S(6)} %select_n.19), kind=kLoop, calls=%fused_computation.6 | loop fusion | bytes 12004 | tf_op jit(solution)/shard_map/eq | solution.py:418
  9.5 0.2 compare_reduce_fusion
  9.8 0.0 collective-permute-done.4.refs_1_
  9.8 0.0 copy-done.3
  9.8 0.1 pad_maximum_fusion.2
  9.9 1.4 %collective-permute-start.5 = (f32[2,40,2,256]{3,2,1,0:T(2,128)S(1)}, f32[2,40,2,256]{3,2,1,0:T(2,128)S(1)}, u32[]{:S(2)}, u32[]{:S(2)}) collective-permute-start(f32[2,40,2,256]{3,2,1,0:T(2,128)S(1)} %pad_maximum_fusion.2), channel_id=1, source_target_pairs={{0,2},{1,3},{2,0},{3,1},{4,6},{5,7},{6,4},{7,5},{8,10},{9,11},{10,... | collective-permute-start | bytes 491528 | tf_op jit(solution)/shard_map/ppermute | solution.py:397
  11.2 0.0 collective-permute-done
  11.3 1.0 %collective-permute-done.1 = bf16[128,512]{1,0:T(8,128)(2,1)S(1)} collective-permute-done((bf16[128,512]{1,0:T(8,128)(2,1)S(1)}, bf16[128,512]{1,0:T(8,128)(2,1)S(1)}, u32[]{:S(2)}, u32[]{:S(2)}) %collective-permute-start.1) | collective-permute-done | bytes 131104 | tf_op jit(solution)/shard_map/ppermute | solution.py:131
  12.3 2.2 %collective-permute-start.3 = (bf16[512,512]{1,0:T(8,128)(2,1)S(1)}, bf16[512,512]{1,0:T(8,128)(2,1)S(1)}, u32[]{:S(2)}, u32[]{:S(2)}) collective-permute-start(bf16[512,512]{1,0:T(8,128)(2,1)S(1)} %constant_dynamic-update-slice_fusion), channel_id=1, source_target_pairs={{0,1},{1,0},{2,3},{3,2},{4,5},{5,4},{6,7},{7,6},{8,9},{9,8},{10,11... | collective-permute-start | bytes 1572872 | tf_op jit(solution)/shard_map/ppermute | solution.py:131
  14.5 3.1 %collective-permute-start.2 = (bf16[512,512]{1,0:T(8,128)(2,1)S(1)}, bf16[512,512]{1,0:T(8,128)(2,1)S(1)}, u32[]{:S(2)}, u32[]{:S(2)}) collective-permute-start(bf16[512,512]{1,0:T(8,128)(2,1)S(1)} %constant_dynamic-update-slice_fusion), channel_id=1, source_target_pairs={{1,2},{2,1},{3,4},{4,3},{5,6},{6,5},{9,10},{10,9},{11,12},{12,11},... | collective-permute-start | bytes 1572872 | tf_op jit(solution)/shard_map/ppermute | solution.py:131
  17.7 0.0 collective-permute-done.5.refs_2_
  17.7 0.2 pad_maximum_fusion.1
  17.8 0.1 collective-permute-start.6
  17.9 0.0 copy-done.5
  17.9 0.7 %bitcast_select_fusion.table = s32[30,50]{1,0:T(8,128)S(1)} fusion(pred[30,50]{1,0:T(8,128)(4,1)S(1)} %compare_reduce_fusion, s32[30,50]{1,0:T(8,128)S(1)} %copy-done.5, s32[4,30,50]{2,1,0:T(8,128)} %constant.39.clone, s32[]{:T(128)S(6)} %select_n.19), kind=kLoop, calls=%fused_computation.5 | loop fusion | flops 1500 | bytes 19504 | tf_op jit(solution)/shard_map/jit(_where)/select_n | solution.py:419
  18.6 0.0 copy-done.2
  18.7 0.0 copy-done.1
  18.7 0.0 copy-done.4
  18.7 2.3 %block.1 = (f32[6,8,2048]{2,1,0:T(8,128)S(1)}, f32[24,8,512]{2,1,0:T(8,128)S(1)}, f32[8,2048]{1,0:T(8,128)S(1)}) custom-call(s32[30,50]{1,0:T(8,128)S(1)} %bitcast_select_fusion.table, bf16[192,512]{1,0:T(8,128)(2,1)S(1)} %reshape.58.src, bf16[512,2048]{1,0:T(8,128)(2,1)S(1)} %copy-done.1, f32[4,2048]{1,0:T(4,128)S(1)} %copy-done.4, f32[40,2,512]{2,1,0:T(2,128)S(1)} %copy-done.2), custom_call_target="tpu_custom_call" | custom-call | tf_op jit(solution)/shard_map/block/pallas_call | solution.py:434
  21.0 2.0 %halo.1 = (f32[17,8,2048]{2,1,0:T(8,128)S(1)}, f32[24,8,512]{2,1,0:T(8,128)S(1)}) custom-call(s32[30,50]{1,0:T(8,128)S(1)} %bitcast_select_fusion.table, bf16[320,512]{1,0:T(8,128)(2,1)S(1)} %pad_maximum_fusion.src, bf16[512,2048]{1,0:T(8,128)(2,1)S(1)} %copy-done.1, f32[8,2048]{1,0:T(8,128)S(1)} %get-tuple-element.15.trig, f32[40,2,512]{2,1,0:T(2,128)S(1)} %copy-done.2, ...), custom_call_target="tpu_custom_call" | custom-call | tf_op jit(solution)/shard_map/halo/pallas_call | solution.py:434
  23.1 0.0 collective-permute-done.3.src
  23.1 2.9 %side.1 = (f32[17,8,2048]{2,1,0:T(8,128)S(1)}, f32[12,8,512]{2,1,0:T(8,128)S(1)}) custom-call(s32[30,50]{1,0:T(8,128)S(1)} %bitcast_select_fusion.table, s32[30,50]{1,0:T(8,128)S(1)} %dynamic-slice_bitcast_fusion.ids, s32[2,8]{1,0:T(2,128)S(1)} %stack.4.info, bf16[512,512]{1,0:T(8,128)(2,1)S(1)} %collective-permute-done.3.src, ...), custom_call_target="tpu_custom_call" | custom-call | tf_op jit(solution)/shard_map/side/pallas_call | solution.py:434
  26.0 0.0 collective-permute-done.6.refs_3_
  26.0 2.4 %inner.1 = (f32[40,2,2048]{2,1,0:T(2,128)S(1)}, f32[6,8,2048]{2,1,0:T(8,128)S(1)}, f32[6,8,2048]{2,1,0:T(8,128)S(1)}) custom-call(s32[30,50]{1,0:T(8,128)S(1)} %bitcast_select_fusion.table, s32[30,50]{1,0:T(8,128)S(1)} %dynamic-slice_bitcast_fusion.ids, s32[2,8]{1,0:T(2,128)S(1)} %stack.4.info, f32[17,8,2048]{2,1,0:T(8,128)S(1)} %get-tuple-element.18.pat_own, ...), custom_call_target="tpu_custom_call" | custom-call | tf_op jit(solution)/shard_map/inner/pallas_call | solution.py:434
  28.4 0.0 collective-permute-done.2.src
  28.4 5.3 %last.1 = f32[6,4,2,4,512]{4,3,2,1,0:T(4,128)} custom-call(s32[30,50]{1,0:T(8,128)S(1)} %bitcast_select_fusion.table, s32[30,50]{1,0:T(8,128)S(1)} %dynamic-slice_bitcast_fusion.ids, s32[2,8]{1,0:T(2,128)S(1)} %stack.4.info, bf16[512,512]{1,0:T(8,128)(2,1)S(1)} %collective-permute-done.2.src, bf16[512,2048]{1,0:T(8,128)(2,1)S(1)} %copy-done.1, ...), custom_call_target="tpu_custom_call" | custom-call | tf_op jit(solution)/shard_map/last/pallas_call | solution.py:434
  (10 shorter events, 0.1 us)
Async XLA Ops:
  0.0 8.6 %copy-start = (s32[6,32,32]{2,1,0:T(8,128)S(1)}, s32[6,32,32]{2,1,0:T(8,128)}, u32[]{:S(2)}) copy-start(s32[6,32,32]{2,1,0:T(8,128)} %param.17) | copy-start | bytes 73732
  0.0 9.8 %copy-start.3 = (f32[40,2,256]{2,1,0:T(2,128)S(1)}, f32[40,2,256]{2,1,0:T(2,128)}, u32[]{:S(2)}) copy-start(f32[40,2,256]{2,1,0:T(2,128)} %param.16) | copy-start | bytes 245764
  0.0 9.8 %collective-permute-start.4 = (f32[1,40,2,256]{3,2,1,0:T(2,128)}, f32[1,40,2,256]{3,2,1,0:T(2,128)S(1)}, u32[]{:S(2)}, u32[]{:S(2)}) collective-permute-start(f32[1,40,2,256]{3,2,1,0:T(2,128)} %bitcast.8), channel_id=1, source_target_pairs={{0,4},{1,5},{2,6},{3,7},{4,0},{5,1},{6,2},{7,3},{8,12},{9,13},{10,... | collective-permute-start | bytes 245768 | tf_op jit(solution)/shard_map/ppermute | solution.py:397
  3.3 7.9 %collective-permute-start = (bf16[192,512]{1,0:T(8,128)(2,1)S(1)}, bf16[192,512]{1,0:T(8,128)(2,1)S(1)}, u32[]{:S(2)}, u32[]{:S(2)}) collective-permute-start(bf16[192,512]{1,0:T(8,128)(2,1)S(1)} %reshape.58.src), channel_id=1, source_target_pairs={{0,8},{8,0},{16,24},{24,16},{1,9},{9,1},{17,25},{25,17},{2,10},{10... | collective-permute-start | bytes 589832 | tf_op jit(solution)/shard_map/ppermute | solution.py:131
  3.6 15.0 %copy-start.2 = (f32[40,2,512]{2,1,0:T(2,128)S(1)}, f32[40,2,512]{2,1,0:T(2,128)}, u32[]{:S(2)}) copy-start(f32[40,2,512]{2,1,0:T(2,128)} %fops.7) | copy-start | bytes 491524
  3.6 14.3 %copy-start.5 = (s32[30,50]{1,0:T(8,128)S(1)}, s32[30,50]{1,0:T(8,128)}, u32[]{:S(2)}) copy-start(s32[30,50]{1,0:T(8,128)} %constant.41.clone) | copy-start | bytes 18004
  3.6 8.6 %collective-permute-start.1 = (bf16[128,512]{1,0:T(8,128)(2,1)S(1)}, bf16[128,512]{1,0:T(8,128)(2,1)S(1)}, u32[]{:S(2)}, u32[]{:S(2)}) collective-permute-start(bf16[128,512]{1,0:T(8,128)(2,1)S(1)} %constant_dynamic-slice_fusion), channel_id=1, source_target_pairs={{8,16},{16,8},{9,17},{17,9},{10,18},{18,10},{11,19},{19,11},{12,20... | collective-permute-start | bytes 393224 | tf_op jit(solution)/shard_map/ppermute | solution.py:131
  8.6 10.1 %copy-start.1 = (bf16[512,2048]{1,0:T(8,128)(2,1)S(1)}, bf16[512,2048]{1,0:T(8,128)(2,1)}, u32[]{:S(2)}) copy-start(bf16[512,2048]{1,0:T(8,128)(2,1)} %interp.7) | copy-start | bytes 6291460
  8.6 10.1 %copy-start.4 = (f32[4,2048]{1,0:T(4,128)S(1)}, f32[4,2048]{1,0:T(4,128)}, u32[]{:S(2)}) copy-start(f32[4,2048]{1,0:T(4,128)} %phase.1) | copy-start | bytes 98308
  9.9 7.8 %collective-permute-start.5 = (f32[2,40,2,256]{3,2,1,0:T(2,128)S(1)}, f32[2,40,2,256]{3,2,1,0:T(2,128)S(1)}, u32[]{:S(2)}, u32[]{:S(2)}) collective-permute-start(f32[2,40,2,256]{3,2,1,0:T(2,128)S(1)} %pad_maximum_fusion.2), channel_id=1, source_target_pairs={{0,2},{1,3},{2,0},{3,1},{4,6},{5,7},{6,4},{7,5},{8,10},{9,11},{10,... | collective-permute-start | bytes 491528 | tf_op jit(solution)/shard_map/ppermute | solution.py:397
  12.3 10.8 %collective-permute-start.3 = (bf16[512,512]{1,0:T(8,128)(2,1)S(1)}, bf16[512,512]{1,0:T(8,128)(2,1)S(1)}, u32[]{:S(2)}, u32[]{:S(2)}) collective-permute-start(bf16[512,512]{1,0:T(8,128)(2,1)S(1)} %constant_dynamic-update-slice_fusion), channel_id=1, source_target_pairs={{0,1},{1,0},{2,3},{3,2},{4,5},{5,4},{6,7},{7,6},{8,9},{9,8},{10,11... | collective-permute-start | bytes 1572872 | tf_op jit(solution)/shard_map/ppermute | solution.py:131
  14.5 13.9 %collective-permute-start.2 = (bf16[512,512]{1,0:T(8,128)(2,1)S(1)}, bf16[512,512]{1,0:T(8,128)(2,1)S(1)}, u32[]{:S(2)}, u32[]{:S(2)}) collective-permute-start(bf16[512,512]{1,0:T(8,128)(2,1)S(1)} %constant_dynamic-update-slice_fusion), channel_id=1, source_target_pairs={{1,2},{2,1},{3,4},{4,3},{5,6},{6,5},{9,10},{10,9},{11,12},{12,11},... | collective-permute-start | bytes 1572872 | tf_op jit(solution)/shard_map/ppermute | solution.py:131
  17.8 8.1 %collective-permute-start.6 = (f32[4,40,2,256]{3,2,1,0:T(2,128)S(1)}, f32[4,40,2,256]{3,2,1,0:T(2,128)S(1)}, u32[]{:S(2)}, u32[]{:S(2)}) collective-permute-start(f32[4,40,2,256]{3,2,1,0:T(2,128)S(1)} %pad_maximum_fusion.1), channel_id=1, source_target_pairs={{0,1},{1,0},{2,3},{3,2},{4,5},{5,4},{6,7},{7,6},{8,9},{9,8},{10,11... | collective-permute-start | bytes 983048 | tf_op jit(solution)/shard_map/ppermute | solution.py:397

commit v2 on v1

--- a/solution.py
+++ b/solution.py
@@ -9,6 +9,7 @@
 from jax.sharding import PartitionSpec as P
 
 CHUNK = 512
+LIMITS = {"block": 8, "pack": 4, "own": 16, "side": 16, "inner": 12, "last": 24}
 F32, BF16 = jnp.float32, jnp.bfloat16
 
 
@@ -224,11 +225,10 @@
                 store((2 * r + a) * 2 + c, value)
 
 
-def block_kernel(rows, cols, sides, table, src, interp, phase, fops, pattern, near, trig, fine, even, odd):
+def block_kernel(rows, cols, sides, table, src, phase, fops, near, trig, fine):
     trig[:4] = jnp.cos(phase[...])
     trig[4:] = jnp.sin(phase[...])
     widen(src, fine, 2 * sides)
-    aggregate(src, interp, trig, (even, odd), pattern, cols, sides)
     for a in range(2):
         for c in range(2 * cols):
             op_ids = [o for o, _ in fine_slots(a, c, rows, cols, 0, 0)[0]]
@@ -237,14 +237,19 @@
                 near[box] = value
 
 
-def halo_kernel(
-    rows, cols, sides, table, src, interp, trig, fops, pat_block, near_block, pattern, near, fine, even, odd
-):
+def pack_kernel(rows, cols, sides, own, first, second, after, strip):
+    at = 0
+    for ref in (own, first, second):
+        strip[at : at + ref.shape[0]] = ref[...]
+        at += ref.shape[0]
+
+
+def own_kernel(rows, cols, sides, table, strip, interp, trig, fops, near_block, pattern, near, fine, even, odd):
     base = starts(slot_counts(rows, cols, 2))[1]
-    widen(src, fine, 2 * sides)
+    inside = near.shape[0] * 2 * sides
+    widen(strip.at[pl.ds(inside, strip.shape[0] - inside)], fine, 2 * sides)
     near[...] = near_block[...]
-    pattern[: pat_block.shape[0]] = pat_block[...]
-    aggregate(src, interp, trig, (even, odd), pattern, cols, sides, pat_block.shape[0])
+    aggregate(strip, interp, trig, (even, odd), pattern, cols, sides)
     zero_box(pattern)
     for r in range(2 * rows):
         for c in range(2 * cols):
@@ -387,10 +392,6 @@
     n_dir, bits = lax.axis_size("dir"), swap_bits("dir")
 
     own = fine_out.reshape(frows * fcols * comps, fdirs)
-    patch_halo = exchange(own, "patch", 2 * fcols * comps, rows)
-    strip = jnp.concatenate([own] + patch_halo, axis=0)
-    side_a, side_b = exchange(strip, "dir", 1, cols)
-
     shards = [parent_ops[None]]
     for bit in reversed(range(bits)):
         held = jnp.concatenate(shards, axis=0)
@@ -403,7 +404,8 @@
     else:
         shards = [in_order(jnp.concatenate(shards, axis=0), "dir")]
         spots = jnp.zeros((n_dir,), jnp.int32)
-    info = jnp.stack([jnp.full((n_dir,), 1 - dir_odd, jnp.int32), spots])
+    first_row = lax.broadcasted_iota(jnp.int32, (2, n_dir), 0) == 0
+    info = jnp.where(first_row, 1 - dir_odd, spots[None])
 
     outside = boxes - rows * cols
     sources, op_ids, nothing = build_tables(
@@ -437,20 +439,26 @@
             in_specs=[smem] * n_smem + [vmem] * (len(args) - n_smem),
             out_specs=[vmem] * len(outs),
             scratch_shapes=scratches,
-            compiler_params=pltpu.CompilerParams(vmem_limit_bytes=40 * 1024 * 1024),
+            compiler_params=pltpu.CompilerParams(vmem_limit_bytes=LIMITS[name] << 20),
             name=name,
         )(*args)
 
     near = shape(frows * fcols, comps, fdirs)
     pattern = shape(boxes + 1, comps, pdirs)
-    pat_block, near_block, trig = call(
-        block_kernel, "block", 1,
-        [shape(rows * cols, comps, pdirs), near, shape(8, pdirs)], group_scratch(frows * fcols),
-        table, own, interp, child_phase, fine_ops,
-    )
+    patch_halo = exchange(own, "patch", 2 * fcols * comps, rows)
+    near_block, trig = call(
+        block_kernel, "block", 1, [near, shape(8, pdirs)], [scratch(frows * fcols + 1, comps, fdirs)],
+        table, own, child_phase, fine_ops,
+    )
+    strip = call(
+        pack_kernel, "pack", 0,
+        [jax.ShapeDtypeStruct((4 * boxes * comps, fdirs), BF16)], [], own, *patch_halo, near_block,
+    )[0]
+    side_a, side_b = exchange(strip, "dir", 1, cols)
     pat_own, near_own = call(
-        halo_kernel, "halo", 1, [pattern, near], group_scratch(4 * outside),
-        table, strip[own.shape[0] :], interp, trig, fine_ops, pat_block, near_block,
+        own_kernel, "own", 1, [pattern, near],
+        [scratch(4 * outside + 1, comps, fdirs)] + [scratch(4 * boxes, comps, CHUNK)] * 2,
+        table, strip, interp, trig, fine_ops, near_block,
     )
     pat_a, near_a = call(
         side_kernel, "side", 3, [pattern, shape(frows * 2, comps, fdirs)], group_scratch(4 * boxes),

time: 34.1 us -> 32.9 us (0.965)
  starting transfers between devices: 13.6 us -> 12.2 us
  other arithmetic: 1.21 us -> 2.21 us
  waiting for transfers between devices: 1.05 us -> 0.11 us
    ppermute x4, starting transfers between devices: 9.86 us -> 8.36 us  [exchange(): got.append(lax.ppermute(edge, axis, pairs(n, first)))]
    concatenate x2, other arithmetic: 0.22 us -> 1.17 us  [per_device(): held = jnp.concatenate(shards, axis=0)]
    ppermute x4, waiting for transfers between devices: 1.04 us -> 0.1 us  [exchange(): got.append(lax.ppermute(edge, axis, pairs(n, first)))]
    pallas_call x5 -> x6, Pallas kernels: 15 us -> 15.1 us  [call(): pl.pallas_call(functools.partial(body, rows, cols, sides), out_shape=outs...]
  transfers between devices with their start and end apart: 7 -> 7, of which waited for: 1 -> 1; matrix products, arithmetic and copies ran while one was open for 11% -> 14% of each run, Pallas kernels for 29% -> 30%
where the time goes in v2:
time: 32.9 us; the launch traced here: 32.3 us
  Pallas kernels  15.1 us (46%)
  starting transfers between devices  12.2 us (37%)
  local copies, waits for them, and re-layouts  2.48 us (8%)
  other arithmetic  2.21 us (7%)
    pallas_call x6, Pallas kernels, call(): pl.pallas_call(functools.partial(body, rows, cols, sides), out_shape=outs...  15.1 us
    ppermute x4, starting transfers between devices, exchange(): got.append(lax.ppermute(edge, axis, pairs(n, first)))  8.36 us
    ppermute x3, starting transfers between devices, per_device(): lax.ppermute(held, 'dir', [(i, i ^ 1 << bit) for i in range(n_dir)])  3.81 us
    concatenate x2, other arithmetic, per_device(): held = jnp.concatenate(shards, axis=0)  1.17 us
    reshape x1, local copies, waits for them, and re-layouts, per_device(): own = fine_out.reshape(frows * fcols * comps, fdirs)  0.98 us
    dynamic_slice x2, local copies, waits for them, and re-layouts, per_device(): lax.dynamic_slice_in_dim(op, dir_at * width, width, 1)  0.73 us
    eq x1, local copies, waits for them, and re-layouts, per_device(): present = jnp.any(lists == ids[:, :, None], axis=2)  0.73 us
    select_n x1, other arithmetic, per_device(): table = jnp.where(present, sources, jnp.asarray(nothing))  0.72 us
  transfers between devices with their start and end apart: 7, of which 1 were waited for; matrix products, arithmetic and copies ran while one was open for 14% of the time, Pallas kernels for 30%

profile of v2, /device:TPU:3, one launch (start us, length us, event | category | flops | bytes accessed | tf_op | source)
XLA Modules:
  0.0 32.3 jit_solution(7100048736077341308)
XLA Ops:
  0.0 0.0 copy-start
  0.0 0.0 copy-start.5
  0.0 0.0 copy-start.2
  0.0 0.0 copy-start.4
  0.0 2.4 %collective-permute-start.4 = (f32[1,40,2,256]{3,2,1,0:T(2,128)}, f32[1,40,2,256]{3,2,1,0:T(2,128)S(1)}, u32[]{:S(2)}, u32[]{:S(2)}) collective-permute-start(f32[1,40,2,256]{3,2,1,0:T(2,128)} %bitcast.8), channel_id=1, source_target_pairs={{0,4},{1,5},{2,6},{3,7},{4,0},{5,1},{6,2},{7,3},{8,12},{9,13},{10,... | collective-permute-start | bytes 245768 | tf_op jit(solution)/shard_map/ppermute | solution.py:398
  2.4 1.0 %reshape.29.src.own = bf16[192,512]{1,0:T(8,128)(2,1)S(1)} reshape(bf16[6,4,2,4,512]{4,3,2,1,0:T(4,128)(2,1)} %param.12) | data formatting | bytes 393216 | tf_op jit(solution)/shard_map/reshape | solution.py:394
  3.4 0.3 collective-permute-start
  3.7 4.1 %collective-permute-start.1 = (bf16[128,512]{1,0:T(8,128)(2,1)S(1)}, bf16[128,512]{1,0:T(8,128)(2,1)S(1)}, u32[]{:S(2)}, u32[]{:S(2)}) collective-permute-start(bf16[128,512]{1,0:T(8,128)(2,1)S(1)} %constant_dynamic-slice_fusion), channel_id=1, source_target_pairs={{8,16},{16,8},{9,17},{17,9},{10,18},{18,10},{11,19},{19,11},{12,20... | collective-permute-start | bytes 393224 | tf_op jit(solution)/shard_map/ppermute | solution.py:132
  7.8 0.7 %constant_dynamic-slice_fusion.1 = s32[3,2,32]{2,1,0:T(2,128)S(1)} fusion(s32[3,16,32]{2,1,0:T(8,128)} %param.18, s32[]{:T(128)S(6)} %select_n.22), kind=kLoop, calls=%fused_computation.7 | loop fusion | bytes 1540 | tf_op jit(solution)/shard_map/dynamic_slice | solution.py:417
  8.5 0.0 copy-done
  8.6 0.7 %dynamic-slice_bitcast_fusion.ids = s32[30,50]{1,0:T(8,128)S(1)} fusion(s32[4,30,50]{2,1,0:T(8,128)} %constant.41.clone, s32[]{:T(128)S(6)} %select_n.23), kind=kLoop, calls=%fused_computation.5 | loop fusion | bytes 12004 | tf_op jit(solution)/shard_map/eq | solution.py:420
  9.3 0.2 compare_reduce_fusion
  9.5 0.0 copy-start.3
  9.5 0.0 collective-permute-done.4.refs_1_
  9.6 1.0 %pad_maximum_fusion.1 = f32[2,40,2,256]{3,2,1,0:T(2,128)S(1)} fusion(f32[1,40,2,256]{3,2,1,0:T(2,128)S(1)} %collective-permute-done.4.refs_1_, f32[1,40,2,256]{3,2,1,0:T(2,128)} %bitcast.9), kind=kLoop, calls=%fused_computation.2 | loop fusion | flops 40960 | bytes 327680 | tf_op jit(solution)/shard_map/concatenate | solution.py:397
  10.6 1.4 %collective-permute-start.5 = (f32[2,40,2,256]{3,2,1,0:T(2,128)S(1)}, f32[2,40,2,256]{3,2,1,0:T(2,128)S(1)}, u32[]{:S(2)}, u32[]{:S(2)}) collective-permute-start(f32[2,40,2,256]{3,2,1,0:T(2,128)S(1)} %pad_maximum_fusion.1), channel_id=1, source_target_pairs={{0,2},{1,3},{2,0},{3,1},{4,6},{5,7},{6,4},{7,5},{8,10},{9,11},{10,... | collective-permute-start | bytes 491528 | tf_op jit(solution)/shard_map/ppermute | solution.py:398
  11.9 0.0 copy-done.5
  11.9 0.7 %bitcast_select_fusion.table = s32[30,50]{1,0:T(8,128)S(1)} fusion(pred[30,50]{1,0:T(8,128)(4,1)S(1)} %compare_reduce_fusion, s32[30,50]{1,0:T(8,128)S(1)} %copy-done.5, s32[4,30,50]{2,1,0:T(8,128)} %constant.40.clone, s32[]{:T(128)S(6)} %select_n.23), kind=kLoop, calls=%fused_computation.4 | loop fusion | flops 1500 | bytes 19504 | tf_op jit(solution)/shard_map/jit(_where)/select_n | solution.py:421
  12.7 0.0 copy-done.2
  12.7 0.0 copy-done.4
  12.7 1.9 %block.1 = (f32[24,8,512]{2,1,0:T(8,128)S(1)}, f32[8,2048]{1,0:T(8,128)S(1)}) custom-call(s32[30,50]{1,0:T(8,128)S(1)} %bitcast_select_fusion.table, bf16[192,512]{1,0:T(8,128)(2,1)S(1)} %reshape.29.src.own, f32[4,2048]{1,0:T(4,128)S(1)} %copy-done.4, f32[40,2,512]{2,1,0:T(2,128)S(1)} %copy-done.2), custom_call_target="tpu_custom_call" | custom-call | tf_op jit(solution)/shard_map/block/pallas_call | solution.py:436
  14.6 0.0 copy-start.1
  14.6 0.0 collective-permute-done.1.second
  14.6 0.0 collective-permute-done.first
  14.6 1.9 %collective-permute-start.3 = (bf16[512,512]{1,0:T(8,128)(2,1)S(1)}, bf16[512,512]{1,0:T(8,128)(2,1)S(1)}, u32[]{:S(2)}, u32[]{:S(2)}) collective-permute-start(bf16[512,512]{1,0:T(8,128)(2,1)S(1)} %pack.1.strip), channel_id=1, source_target_pairs={{0,1},{1,0},{2,3},{3,2},{4,5},{5,4},{6,7},{7,6},{8,9},{9,8},{10,11... | collective-permute-start | bytes 1572872 | tf_op jit(solution)/shard_map/ppermute | solution.py:132
  16.5 2.1 %collective-permute-start.2 = (bf16[512,512]{1,0:T(8,128)(2,1)S(1)}, bf16[512,512]{1,0:T(8,128)(2,1)S(1)}, u32[]{:S(2)}, u32[]{:S(2)}) collective-permute-start(bf16[512,512]{1,0:T(8,128)(2,1)S(1)} %pack.1.strip), channel_id=1, source_target_pairs={{1,2},{2,1},{3,4},{4,3},{5,6},{6,5},{9,10},{10,9},{11,12},{12,11},... | collective-permute-start | bytes 1572872 | tf_op jit(solution)/shard_map/ppermute | solution.py:132
  18.6 0.0 collective-permute-done.5.refs_2_
  18.6 0.0 copy-done.3
  18.7 0.2 pad_maximum_fusion
  18.8 0.1 collective-permute-start.6
  18.9 0.1 broadcast_select_fusion.info
  19.0 0.0 copy-done.1
  19.0 2.6 %own.1 = (f32[17,8,2048]{2,1,0:T(8,128)S(1)}, f32[24,8,512]{2,1,0:T(8,128)S(1)}) custom-call(s32[30,50]{1,0:T(8,128)S(1)} %bitcast_select_fusion.table, bf16[512,512]{1,0:T(8,128)(2,1)S(1)} %pack.1.strip, bf16[512,2048]{1,0:T(8,128)(2,1)S(1)} %copy-done.1, f32[8,2048]{1,0:T(8,128)S(1)} %get-tuple-element.15.trig, f32[40,2,512]{2,1,0:T(2,128)S(1)} %copy-done.2, ...), custom_call_target="tpu_custom_call" | custom-call | tf_op jit(solution)/shard_map/own/pallas_call | solution.py:436
  21.5 0.0 collective-permute-done.3.src
  21.5 2.9 %side.1 = (f32[17,8,2048]{2,1,0:T(8,128)S(1)}, f32[12,8,512]{2,1,0:T(8,128)S(1)}) custom-call(s32[30,50]{1,0:T(8,128)S(1)} %bitcast_select_fusion.table, s32[30,50]{1,0:T(8,128)S(1)} %dynamic-slice_bitcast_fusion.ids, s32[2,8]{1,0:T(2,128)S(1)} %broadcast_select_fusion.info, bf16[512,512]{1,0:T(8,128)(2,1)S(1)} %collective-permute-done.3.src, ...), custom_call_target="tpu_custom_call" | custom-call | tf_op jit(solution)/shard_map/side/pallas_call | solution.py:436
  24.5 0.0 collective-permute-done.6.refs_3_
  24.5 2.4 %inner.1 = (f32[40,2,2048]{2,1,0:T(2,128)S(1)}, f32[6,8,2048]{2,1,0:T(8,128)S(1)}, f32[6,8,2048]{2,1,0:T(8,128)S(1)}) custom-call(s32[30,50]{1,0:T(8,128)S(1)} %bitcast_select_fusion.table, s32[30,50]{1,0:T(8,128)S(1)} %dynamic-slice_bitcast_fusion.ids, s32[2,8]{1,0:T(2,128)S(1)} %broadcast_select_fusion.info, f32[17,8,2048]{2,1,0:T(8,128)S(1)} %get-tuple-element.16.pat_own, ...), custom_call_target="tpu_custom_call" | custom-call | tf_op jit(solution)/shard_map/inner/pallas_call | solution.py:436
  26.9 0.1 collective-permute-done.2.src
  27.0 5.3 %last.1 = f32[6,4,2,4,512]{4,3,2,1,0:T(4,128)} custom-call(s32[30,50]{1,0:T(8,128)S(1)} %bitcast_select_fusion.table, s32[30,50]{1,0:T(8,128)S(1)} %dynamic-slice_bitcast_fusion.ids, s32[2,8]{1,0:T(2,128)S(1)} %broadcast_select_fusion.info, bf16[512,512]{1,0:T(8,128)(2,1)S(1)} %collective-permute-done.2.src, bf16[512,2048]{1,0:T(8,128)(2,1)S(1)} %copy-done.1, ...), custom_call_target="tpu_custom_call" | custom-call | tf_op jit(solution)/shard_map/last/pallas_call | solution.py:436
  (7 shorter events, 0.1 us)
Async XLA Ops:
  0.0 8.5 %copy-start = (s32[6,32,32]{2,1,0:T(8,128)S(1)}, s32[6,32,32]{2,1,0:T(8,128)}, u32[]{:S(2)}) copy-start(s32[6,32,32]{2,1,0:T(8,128)} %param.17) | copy-start | bytes 73732
  0.0 11.9 %copy-start.5 = (s32[30,50]{1,0:T(8,128)S(1)}, s32[30,50]{1,0:T(8,128)}, u32[]{:S(2)}) copy-start(s32[30,50]{1,0:T(8,128)} %constant.42.clone) | copy-start | bytes 18004
  0.0 12.7 %copy-start.2 = (f32[40,2,512]{2,1,0:T(2,128)S(1)}, f32[40,2,512]{2,1,0:T(2,128)}, u32[]{:S(2)}) copy-start(f32[40,2,512]{2,1,0:T(2,128)} %fops.7) | copy-start | bytes 491524
  0.0 12.7 %copy-start.4 = (f32[4,2048]{1,0:T(4,128)S(1)}, f32[4,2048]{1,0:T(4,128)}, u32[]{:S(2)}) copy-start(f32[4,2048]{1,0:T(4,128)} %phase.1) | copy-start | bytes 98308
  0.0 9.5 %collective-permute-start.4 = (f32[1,40,2,256]{3,2,1,0:T(2,128)}, f32[1,40,2,256]{3,2,1,0:T(2,128)S(1)}, u32[]{:S(2)}, u32[]{:S(2)}) collective-permute-start(f32[1,40,2,256]{3,2,1,0:T(2,128)} %bitcast.8), channel_id=1, source_target_pairs={{0,4},{1,5},{2,6},{3,7},{4,0},{5,1},{6,2},{7,3},{8,12},{9,13},{10,... | collective-permute-start | bytes 245768 | tf_op jit(solution)/shard_map/ppermute | solution.py:398
  3.4 11.2 %collective-permute-start = (bf16[192,512]{1,0:T(8,128)(2,1)S(1)}, bf16[192,512]{1,0:T(8,128)(2,1)S(1)}, u32[]{:S(2)}, u32[]{:S(2)}) collective-permute-start(bf16[192,512]{1,0:T(8,128)(2,1)S(1)} %reshape.29.src.own), channel_id=1, source_target_pairs={{0,8},{8,0},{16,24},{24,16},{1,9},{9,1},{17,25},{25,17},{2,10},{10... | collective-permute-start | bytes 589832 | tf_op jit(solution)/shard_map/ppermute | solution.py:132
  3.7 10.9 %collective-permute-start.1 = (bf16[128,512]{1,0:T(8,128)(2,1)S(1)}, bf16[128,512]{1,0:T(8,128)(2,1)S(1)}, u32[]{:S(2)}, u32[]{:S(2)}) collective-permute-start(bf16[128,512]{1,0:T(8,128)(2,1)S(1)} %constant_dynamic-slice_fusion), channel_id=1, source_target_pairs={{8,16},{16,8},{9,17},{17,9},{10,18},{18,10},{11,19},{19,11},{12,20... | collective-permute-start | bytes 393224 | tf_op jit(solution)/shard_map/ppermute | solution.py:132
  9.5 9.1 %copy-start.3 = (f32[40,2,256]{2,1,0:T(2,128)S(1)}, f32[40,2,256]{2,1,0:T(2,128)}, u32[]{:S(2)}) copy-start(f32[40,2,256]{2,1,0:T(2,128)} %param.16) | copy-start | bytes 245764
  10.6 8.1 %collective-permute-start.5 = (f32[2,40,2,256]{3,2,1,0:T(2,128)S(1)}, f32[2,40,2,256]{3,2,1,0:T(2,128)S(1)}, u32[]{:S(2)}, u32[]{:S(2)}) collective-permute-start(f32[2,40,2,256]{3,2,1,0:T(2,128)S(1)} %pad_maximum_fusion.1), channel_id=1, source_target_pairs={{0,2},{1,3},{2,0},{3,1},{4,6},{5,7},{6,4},{7,5},{8,10},{9,11},{10,... | collective-permute-start | bytes 491528 | tf_op jit(solution)/shard_map/ppermute | solution.py:398
  14.6 4.4 %copy-start.1 = (bf16[512,2048]{1,0:T(8,128)(2,1)S(1)}, bf16[512,2048]{1,0:T(8,128)(2,1)}, u32[]{:S(2)}) copy-start(bf16[512,2048]{1,0:T(8,128)(2,1)} %interp.5) | copy-start | bytes 6291460
  14.6 6.9 %collective-permute-start.3 = (bf16[512,512]{1,0:T(8,128)(2,1)S(1)}, bf16[512,512]{1,0:T(8,128)(2,1)S(1)}, u32[]{:S(2)}, u32[]{:S(2)}) collective-permute-start(bf16[512,512]{1,0:T(8,128)(2,1)S(1)} %pack.1.strip), channel_id=1, source_target_pairs={{0,1},{1,0},{2,3},{3,2},{4,5},{5,4},{6,7},{7,6},{8,9},{9,8},{10,11... | collective-permute-start | bytes 1572872 | tf_op jit(solution)/shard_map/ppermute | solution.py:132
  16.5 10.5 %collective-permute-start.2 = (bf16[512,512]{1,0:T(8,128)(2,1)S(1)}, bf16[512,512]{1,0:T(8,128)(2,1)S(1)}, u32[]{:S(2)}, u32[]{:S(2)}) collective-permute-start(bf16[512,512]{1,0:T(8,128)(2,1)S(1)} %pack.1.strip), channel_id=1, source_target_pairs={{1,2},{2,1},{3,4},{4,3},{5,6},{6,5},{9,10},{10,9},{11,12},{12,11},... | collective-permute-start | bytes 1572872 | tf_op jit(solution)/shard_map/ppermute | solution.py:132
  18.8 5.7 %collective-permute-start.6 = (f32[4,40,2,256]{3,2,1,0:T(2,128)S(1)}, f32[4,40,2,256]{3,2,1,0:T(2,128)S(1)}, u32[]{:S(2)}, u32[]{:S(2)}) collective-permute-start(f32[4,40,2,256]{3,2,1,0:T(2,128)S(1)} %pad_maximum_fusion), channel_id=1, source_target_pairs={{0,1},{1,0},{2,3},{3,2},{4,5},{5,4},{6,7},{7,6},{8,9},{9,8},{10,11... | collective-permute-start | bytes 983048 | tf_op jit(solution)/shard_map/ppermute | solution.py:398

commit v3 on v2

--- a/solution.py
+++ b/solution.py
@@ -9,7 +9,8 @@
 from jax.sharding import PartitionSpec as P
 
 CHUNK = 512
-LIMITS = {"block": 8, "pack": 4, "own": 16, "side": 16, "inner": 12, "last": 24}
+PIECE = 256
+LIMITS = {"block": 8, "pack": 4, "edge": 4, "lists": 4, "own": 16, "side": 16, "inner": 12, "last": 24}
 F32, BF16 = jnp.float32, jnp.bfloat16
 
 
@@ -111,6 +112,35 @@
     return np.array(sources, np.int32), np.array(op_ids, np.int32), np.array(nothing, np.int32)
 
 
+def shared_ids(op_ids, rows, cols):
+    fine, par = slot_counts(rows, cols, 2), slot_counts(rows, cols, 1)
+    width = max(2 * fine[2], sum(par))
+    found = []
+    for which, (_, dir_odd) in enumerate(PARITIES):
+        entries = []
+        for a in range(2):
+            for c in range(2):
+                entry = []
+                for group, right in ((2, 1 - dir_odd), (3, dir_odd)):
+                    box = a * 2 * cols + right * (2 * cols - 2) + c
+                    at = starts(fine)[group]
+                    entry += list(op_ids[which, box, at : at + fine[group]])
+                entries.append(entry)
+        for c in range(cols):
+            for start in range(2):
+                entries.append(list(op_ids[which, 4 * rows * cols + start * cols + c, : sum(par)]))
+        found.append([entry + [0] * (width - len(entry)) for entry in entries])
+    return np.array(found, np.int32)
+
+
+def parity(axis):
+    return lax.rem(lax.axis_index(axis), 2)
+
+
+def parities():
+    return parity("patch") * 2 + parity("dir")
+
+
 def pairs(count, first):
     if first:
         return [(i, i ^ 1) for i in range(count) if (i ^ 1) < count]
@@ -120,27 +150,23 @@
     return found
 
 
-def exchange(block, axis, unit, count):
+def exchange(blocks, axis):
     n = lax.axis_size(axis)
-    odd = lax.rem(lax.axis_index(axis), 2)
-    got = []
-    for first, size in zip((True, False), halo_sizes(count)):
-        edge = block
-        if size < count:
-            low = (1 - odd) if first else odd
-            edge = lax.dynamic_slice_in_dim(block, low * ((count - size) * unit), size * unit, 0)
-        got.append(lax.ppermute(edge, axis, pairs(n, first)))
-    return got
+    return [lax.ppermute(block, axis, pairs(n, first)) for block, first in zip(blocks, (True, False))]
 
 
 def swap_bits(axis):
     return lax.axis_size(axis).bit_length() - 1
 
 
+def shard_order(axis):
+    bits = swap_bits(axis)
+    return [int(format(e, "0%db" % bits)[::-1], 2) if bits else 0 for e in range(lax.axis_size(axis))]
+
+
 def in_order(block, axis):
-    n, bits = lax.axis_size(axis), swap_bits(axis)
-    spots = [int(format(s, "0%db" % bits)[::-1], 2) for s in range(n)] if bits else [0]
-    at = jnp.asarray(np.array(spots, np.int32))[jnp.arange(n, dtype=jnp.int32) ^ lax.axis_index(axis)]
+    n = lax.axis_size(axis)
+    at = jnp.asarray(np.array(shard_order(axis), np.int32))[jnp.arange(n, dtype=jnp.int32) ^ lax.axis_index(axis)]
     block = jnp.take(block, at, axis=0)
     return block.transpose(1, 2, 0, 3).reshape(1, block.shape[1], 2, n * block.shape[3])
 
@@ -173,34 +199,42 @@
     buffer[...] = out.reshape(-1, comps, CHUNK)
 
 
-def shifts(trig, j, comps, width=CHUNK):
-    lanes = slice(j * CHUNK, j * CHUNK + width)
-    return [jnp.broadcast_to(trig[k : k + 1, lanes], (comps, width)) for k in range(8)]
-
-
-def aggregate_chunk(buffer, shift, pattern, lanes, width, sides, base=0):
-    for q in range(buffer.shape[0] // 4):
-        r, c = divmod(q, width)
-        total = [None, None]
-        for k in range(4):
-            piece = buffer[(2 * r + k // 2) * (2 * width) + 2 * c + k % 2]
-            for i in range(2):
-                add = shift[4 * i + k] * piece
-                total[i] = add if k == 0 else total[i] + add
-        whole = total[0] + times_i(total[1], sides)
-        pattern[base + q, :, lanes] = whole.astype(BF16).astype(F32)
-
-
-def aggregate(src, interp, trig, buffers, pattern, width, sides, base=0, done=lambda j: None):
+def shifts(trig, j, comps):
+    lanes = slice(j * CHUNK, (j + 1) * CHUNK)
+    return [jnp.broadcast_to(trig[k : k + 1, lanes], (comps, CHUNK)) for k in range(8)]
+
+
+def aggregate_chunk(buffer, trig, j, pattern, width, sides):
+    comps = 2 * sides
+    for at in range(0, CHUNK, PIECE):
+        lanes = slice(j * CHUNK + at, j * CHUNK + at + PIECE)
+        shift = [jnp.broadcast_to(trig[k : k + 1, lanes], (comps, PIECE)) for k in range(8)]
+        for q in range(buffer.shape[0] // 4):
+            r, c = divmod(q, width)
+            total = [None, None]
+            for k in range(4):
+                piece = buffer[(2 * r + k // 2) * (2 * width) + 2 * c + k % 2, :, at : at + PIECE]
+                for i in range(2):
+                    add = shift[4 * i + k] * piece
+                    total[i] = add if k == 0 else total[i] + add
+            whole = total[0] + times_i(total[1], sides)
+            pattern[q, :, lanes] = whole.astype(BF16).astype(F32)
+
+
+def aggregate(src, interp, trig, buffers, pattern, width, sides, beside=lambda j: None, done=lambda j: None):
     comps = 2 * sides
     steps = interp.shape[1] // CHUNK
     spread_chunk(src, interp, 0, buffers[0], comps)
     for j in range(steps):
         if j + 1 < steps:
             spread_chunk(src, interp, j + 1, buffers[(j + 1) % 2], comps)
-        lanes = slice(j * CHUNK, (j + 1) * CHUNK)
-        aggregate_chunk(buffers[j % 2], shifts(trig, j, comps), pattern, lanes, width, sides, base)
+        beside(j)
+        aggregate_chunk(buffers[j % 2], trig, j, pattern, width, sides)
         done(j)
+
+
+def dealt(items, j, steps):
+    return items[len(items) * j // steps : len(items) * (j + 1) // steps]
 
 
 def zero_box(pattern):
@@ -216,18 +250,23 @@
     return [real + times_i(imag, comps // 2) for real, imag in sums]
 
 
-def near_side(table, ids, fops, fine, rows, cols, base, count, first_col, store):
-    for a in range(2):
-        for c in range(2):
-            group = [(2 * r + a) * (2 * cols) + first_col + c for r in range(rows)]
-            op_ids = [ids[group[0], t] for t in range(base, base + count)]
-            for r, value in enumerate(near_sums(table, fops, fine, group, base, op_ids)):
-                store((2 * r + a) * 2 + c, value)
+def near_side(table, ids, fops, fine, rows, cols, group, right, store, classes):
+    counts = slot_counts(rows, cols, 2)
+    base, count, which = starts(counts)[group], counts[group], parities()
+    first_col = right * (2 * cols - 2)
+    for a, c in classes:
+        boxes = [(2 * r + a) * (2 * cols) + first_col + c for r in range(rows)]
+        op_ids = [ids[which, 2 * a + c, (group - 2) * count + t] for t in range(count)]
+        for r, value in enumerate(near_sums(table, fops, fine, boxes, base, op_ids)):
+            store((2 * r + a) * 2 + c, value)
 
 
 def block_kernel(rows, cols, sides, table, src, phase, fops, near, trig, fine):
-    trig[:4] = jnp.cos(phase[...])
-    trig[4:] = jnp.sin(phase[...])
+    half = phase.shape[1] // 2
+    both = jnp.concatenate([phase[:, :half], phase[:, half:]], axis=0)
+    for first, wave in ((0, jnp.cos(both)), (4, jnp.sin(both))):
+        trig[first : first + 4, :half] = wave[:4]
+        trig[first : first + 4, half:] = wave[4:]
     widen(src, fine, 2 * sides)
     for a in range(2):
         for c in range(2 * cols):
@@ -237,6 +276,30 @@
                 near[box] = value
 
 
+def lists_kernel(rows, cols, sides, fine_op, par_op, lists, table):
+    which = parities()
+    at, boxes = 0, table.shape[0]
+    for op, scale, none in ((fine_op, 2, 2 * boxes), (par_op, 1, 2 * boxes + 1)):
+        across = cols * scale
+        first = pl.multiple_of(lax.axis_index("dir") * across, across)
+        for r in range(rows * scale):
+            mine = op[r, pl.ds(first, across), :]
+            wanted = lists[which, boxes + at : boxes + at + across]
+            found = mine[:, 0:1] == wanted
+            for slot in range(1, op.shape[2]):
+                found = found | (mine[:, slot : slot + 1] == wanted)
+            zero = jnp.broadcast_to(lists[which, none : none + 1], wanted.shape)
+            table[at : at + across] = jnp.where(found, lists[which, at : at + across], zero)
+            at += across
+
+
+def edge_kernel(rows, cols, sides, own, edge):
+    size = halo_sizes(rows)[1]
+    unit = own.shape[0] // rows
+    at = pl.multiple_of(parity("patch") * ((rows - size) * unit), unit)
+    edge[...] = own[pl.ds(at, size * unit)]
+
+
 def pack_kernel(rows, cols, sides, own, first, second, after, strip):
     at = 0
     for ref in (own, first, second):
@@ -248,63 +311,65 @@
     base = starts(slot_counts(rows, cols, 2))[1]
     inside = near.shape[0] * 2 * sides
     widen(strip.at[pl.ds(inside, strip.shape[0] - inside)], fine, 2 * sides)
-    near[...] = near_block[...]
-    aggregate(strip, interp, trig, (even, odd), pattern, cols, sides)
+    steps = interp.shape[1] // CHUNK
+
+    def beside(j):
+        for box in dealt(range(near.shape[0]), j, min(steps, 2)) if j < 2 else ():
+            op_ids = [o for o, _ in fine_slots(*divmod(box, 2 * cols), rows, cols, 0, 0)[1]]
+            more = near_sums(table, fops, fine, [box], base, op_ids)[0] if op_ids else 0.0
+            near[box] = near_block[box] + more
+
+    aggregate(strip, interp, trig, (even, odd), pattern, cols, sides, beside)
     zero_box(pattern)
-    for r in range(2 * rows):
-        for c in range(2 * cols):
-            op_ids = [o for o, _ in fine_slots(r, c, rows, cols, 0, 0)[1]]
-            if op_ids:
-                box = r * 2 * cols + c
-                near[box] += near_sums(table, fops, fine, [box], base, op_ids)[0]
-
-
-def side_kernel(rows, cols, sides, table, ids, info, src, interp, trig, fops, pattern, near, fine, even, odd):
-    counts = slot_counts(rows, cols, 2)
+
+
+def side_kernel(rows, cols, sides, table, ids, src, interp, trig, fops, pattern, near, fine, even, odd):
     widen(src, fine, 2 * sides)
 
     def store(at, value):
         near[at] = value
 
-    aggregate(src, interp, trig, (even, odd), pattern, halo_sizes(cols)[0], sides)
+    steps = interp.shape[1] // CHUNK
+
+    def beside(j):
+        near_side(table, ids, fops, fine, rows, cols, 2, 1 - parity("dir"), store, dealt(PARITIES, j, steps))
+
+    aggregate(src, interp, trig, (even, odd), pattern, halo_sizes(cols)[0], sides, beside)
     zero_box(pattern)
-    near_side(
-        table, ids, fops, fine, rows, cols, starts(counts)[2], counts[2], info[0, 0] * (2 * cols - 2), store
-    )
 
 
 def parent_groups(rows, cols):
     return [[(r, c) for r in range(start, rows, 2)] for c in range(cols) for start in range(2)]
 
 
-def parent_sums(rows, cols, sides, table, ids, pops, sources, group, first, width):
-    comps = 2 * sides
+def parent_sums(rows, cols, sides, table, ids, pops, sources, index, group, first, width):
+    comps, which = 2 * sides, parities()
     rows_at = [4 * rows * cols + r * cols + c for r, c in group]
     sums = [None] * len(group)
     for base, count, ref in sources:
         for t in range(base, base + count):
-            op_id = ids[rows_at[0], t]
+            op_id = ids[which, 4 + index, t]
             coefs = [row_of(pops, (op_id,), i, first, width, comps) for i in range(2)]
             add_slots(sums, coefs, [ref[table[row, t], :, first : first + width] for row in rows_at])
     return sums
 
 
-def inner_kernel(rows, cols, sides, table, ids, info, pat_own, pat_a, *refs):
+def inner_kernel(rows, cols, sides, table, ids, pat_own, pat_a, *refs):
     *shards, pops, real, imag = refs
     at = 0
     for ref in shards:
         held = ref.shape[3]
         for k in range(ref.shape[0]):
-            lane = pl.multiple_of(info[1, at] * held, held)
+            lane = pl.multiple_of((shard_order("dir")[at] ^ lax.axis_index("dir")) * held, held) if held < pops.shape[2] else 0
             pops[:, :, pl.ds(lane, held)] = ref[k]
             at += 1
     counts = slot_counts(rows, cols, 1)
     at = starts(counts)
     sources = [(at[0], counts[0], pat_own), (at[1], counts[1], pat_a)]
     for first in range(0, real.shape[2], 2 * CHUNK):
-        for group in parent_groups(rows, cols):
+        for index, group in enumerate(parent_groups(rows, cols)):
             sums = parent_sums(
-                rows, cols, sides, table, ids, pops, sources, group, first, 2 * CHUNK
+                rows, cols, sides, table, ids, pops, sources, index, group, first, 2 * CHUNK
             )
             for (r, c), (re, im) in zip(group, sums):
                 real[r * cols + c, :, first : first + 2 * CHUNK] = re
@@ -313,55 +378,55 @@
 
 def last_kernel(
     rows, cols, sides,
-    table, ids, info,
+    table, ids,
     src, interp, trig, fops, pops, real, imag, near_own, near_a,
     out,
     fine, even, odd, pat_b, child, near_b, acc,
 ):
     comps, fdirs = fine.shape[1:]
     fcols = 2 * cols
-    wide = 2 * CHUNK
-    counts = slot_counts(rows, cols, 2)
     par_counts = slot_counts(rows, cols, 1)
-    a_right = info[0, 0]
+    a_right = 1 - parity("dir")
     widen(src, fine, comps)
     zero_box(pat_b)
 
     def store(at, value):
         near_b[1 - a_right, at] = value
 
-    near_side(
-        table, ids, fops, fine, rows, cols, starts(counts)[3], counts[3], (1 - a_right) * (fcols - 2), store
-    )
     for at in range(near_a.shape[0]):
         near_b[a_right, at] = near_a[at]
+    steps = interp.shape[1] // CHUNK
+
+    def beside(j):
+        near_side(table, ids, fops, fine, rows, cols, 3, 1 - a_right, store, dealt(PARITIES, j, steps))
+
+    def back(j):
+        lanes = slice(j * CHUNK, (j + 1) * CHUNK)
+        more = lax.dot_general(
+            child[:, :, lanes].reshape(-1, CHUNK), interp[:, lanes],
+            (((1,), (1,)), ((), ())), preferred_element_type=F32,
+        ).reshape(acc.shape)
+        acc[...] = more if j == 0 else acc[...] + more
 
     def far(j):
-        if j % 2 == 0:
-            return
-        first = (j - 1) * CHUNK
-        shift = shifts(trig, j - 1, comps, wide)
+        if j:
+            back(j - 1)
+        lanes = slice(j * CHUNK, (j + 1) * CHUNK)
+        shift = shifts(trig, j, comps)
         sources = [(starts(par_counts)[2], par_counts[2], pat_b)]
-        for group in parent_groups(rows, cols):
-            sums = parent_sums(rows, cols, sides, table, ids, pops, sources, group, first, wide)
+        for index, group in enumerate(parent_groups(rows, cols)):
+            sums = parent_sums(rows, cols, sides, table, ids, pops, sources, index, group, j * CHUNK, CHUNK)
             for (r, c), (re, im) in zip(group, sums):
                 box = r * cols + c
-                re = re + real[box, :, first : first + wide]
-                im = im + imag[box, :, first : first + wide]
-                total = (re + times_i(im, sides)).astype(BF16).astype(F32)
+                total = re + real[box, :, lanes] + times_i(im + imag[box, :, lanes], sides)
+                total = total.astype(BF16).astype(F32)
                 turned = times_i(total, sides)
                 for k in range(4):
                     at = (2 * r + k // 2) * fcols + 2 * c + k % 2
-                    child[at, :, first : first + wide] = (
-                        shift[k] * total - shift[4 + k] * turned
-                    ).astype(BF16)
-        back = lax.dot_general(
-            child[:, :, first : first + wide].reshape(-1, wide), interp[:, first : first + wide],
-            (((1,), (1,)), ((), ())), preferred_element_type=F32,
-        ).reshape(acc.shape)
-        acc[...] = back if j == 1 else acc[...] + back
-
-    aggregate(src, interp, trig, (even, odd), pat_b, halo_sizes(cols)[1], sides, 0, far)
+                    child[at, :, lanes] = (shift[k] * total - shift[4 + k] * turned).astype(BF16)
+
+    aggregate(src, interp, trig, (even, odd), pat_b, halo_sizes(cols)[1], sides, beside, far)
+    back(steps - 1)
 
     scale = fdirs / interp.shape[1]
     for r in range(2 * rows):
@@ -384,41 +449,18 @@
     comps = 2 * sides
     pdirs = interp.shape[1]
     assert all(size == cols for size in halo_sizes(cols)) and pdirs % (2 * CHUNK) == 0
-    patch_odd = lax.rem(lax.axis_index("patch"), 2)
-    dir_at = lax.axis_index("dir")
-    dir_odd = lax.rem(dir_at, 2)
     height = rows + sum(halo_sizes(rows))
     boxes = height * cols
     n_dir, bits = lax.axis_size("dir"), swap_bits("dir")
 
     own = fine_out.reshape(frows * fcols * comps, fdirs)
-    shards = [parent_ops[None]]
-    for bit in reversed(range(bits)):
-        held = jnp.concatenate(shards, axis=0)
-        shards.append(lax.ppermute(held, "dir", [(i, i ^ (1 << bit)) for i in range(n_dir)]))
-    if parent_ops.shape[2] % 128 == 0:
-        places = jnp.arange(n_dir, dtype=jnp.int32)
-        spots = dir_at
-        for b in range(bits):
-            spots = spots ^ (((places >> b) & 1) << (bits - 1 - b))
-    else:
-        shards = [in_order(jnp.concatenate(shards, axis=0), "dir")]
-        spots = jnp.zeros((n_dir,), jnp.int32)
-    first_row = lax.broadcasted_iota(jnp.int32, (2, n_dir), 0) == 0
-    info = jnp.where(first_row, 1 - dir_odd, spots[None])
-
     outside = boxes - rows * cols
     sources, op_ids, nothing = build_tables(
         rows, cols, {2: [frows * fcols, 4 * outside, 4 * boxes, 4 * boxes], 1: [boxes] * 3}
     )
-    which = patch_odd * 2 + dir_odd
-    sources, ids = jnp.asarray(sources)[which], jnp.asarray(op_ids)[which]
-    lists = jnp.concatenate([
-        lax.dynamic_slice_in_dim(op, dir_at * width, width, 1).reshape(-1, 1, op.shape[2])
-        for op, width in ((fine_op, fcols), (parent_op, cols))
-    ])
-    present = jnp.any(lists == ids[:, :, None], axis=2)
-    table = jnp.where(present, sources, jnp.asarray(nothing))
+    ids = jnp.asarray(shared_ids(op_ids, rows, cols))
+    nothing = np.broadcast_to(nothing[[0, -1]], (len(PARITIES), 2, nothing.shape[1]))
+    lists = jnp.asarray(np.concatenate([sources, op_ids, nothing], axis=1))
 
     smem = pl.BlockSpec(memory_space=pltpu.SMEM)
     vmem = pl.BlockSpec(memory_space=pltpu.VMEM)
@@ -445,7 +487,21 @@
 
     near = shape(frows * fcols, comps, fdirs)
     pattern = shape(boxes + 1, comps, pdirs)
-    patch_halo = exchange(own, "patch", 2 * fcols * comps, rows)
+    table = call(
+        lists_kernel, "lists", 0, [jax.ShapeDtypeStruct(sources.shape[1:], jnp.int32)], [],
+        fine_op, parent_op, lists,
+    )[0]
+    first, second = halo_sizes(rows)
+    assert first == rows
+    edge = call(
+        edge_kernel, "edge", 0,
+        [jax.ShapeDtypeStruct((own.shape[0] // rows * second, fdirs), BF16)], [], own,
+    )[0]
+    patch_halo = exchange([own, edge], "patch")
+    shards = [parent_ops[None]]
+    for bit in reversed(range(bits)):
+        held = jnp.concatenate(shards, axis=0)
+        shards.append(lax.ppermute(held, "dir", [(i, i ^ (1 << bit)) for i in range(n_dir)]))
     near_block, trig = call(
         block_kernel, "block", 1, [near, shape(8, pdirs)], [scratch(frows * fcols + 1, comps, fdirs)],
         table, own, child_phase, fine_ops,
@@ -454,30 +510,32 @@
         pack_kernel, "pack", 0,
         [jax.ShapeDtypeStruct((4 * boxes * comps, fdirs), BF16)], [], own, *patch_halo, near_block,
     )[0]
-    side_a, side_b = exchange(strip, "dir", 1, cols)
+    side_a, side_b = exchange([strip, strip], "dir")
+    if parent_ops.shape[2] % 128:
+        shards = [in_order(jnp.concatenate(shards, axis=0), "dir")]
     pat_own, near_own = call(
         own_kernel, "own", 1, [pattern, near],
         [scratch(4 * outside + 1, comps, fdirs)] + [scratch(4 * boxes, comps, CHUNK)] * 2,
         table, strip, interp, trig, fine_ops, near_block,
     )
     pat_a, near_a = call(
-        side_kernel, "side", 3, [pattern, shape(frows * 2, comps, fdirs)], group_scratch(4 * boxes),
-        table, ids, info, side_a, interp, trig, fine_ops,
+        side_kernel, "side", 2, [pattern, shape(frows * 2, comps, fdirs)], group_scratch(4 * boxes),
+        table, ids, side_a, interp, trig, fine_ops,
     )
     part = shape(rows * cols, comps, pdirs)
     pops, real, imag = call(
-        inner_kernel, "inner", 3, [shape(parent_ops.shape[0], 2, pdirs), part, part], [],
-        table, ids, info, pat_own, pat_a, *shards,
+        inner_kernel, "inner", 2, [shape(parent_ops.shape[0], 2, pdirs), part, part], [],
+        table, ids, pat_own, pat_a, *shards,
     )
     return call(
-        last_kernel, "last", 3, [jax.ShapeDtypeStruct(fine_out.shape, F32)],
+        last_kernel, "last", 2, [jax.ShapeDtypeStruct(fine_out.shape, F32)],
         group_scratch(4 * boxes) + [
             scratch(boxes + 1, comps, pdirs),
             scratch(frows * fcols, comps, pdirs, kind=BF16),
             scratch(2, frows * 2, comps, fdirs),
             scratch(frows * fcols, comps, fdirs),
         ],
-        table, ids, info, side_b, interp, trig, fine_ops, pops, real, imag, near_own, near_a,
+        table, ids, side_b, interp, trig, fine_ops, pops, real, imag, near_own, near_a,
     )[0]
 
 

time: 32.9 us -> 31.2 us (0.948); the launches traced: 32.3 us -> 31 us
  other arithmetic: 2.21 us -> 1.12 us
  local copies, waits for them, and re-layouts: 2.48 us -> 1.75 us
  starting transfers between devices: 12.2 us -> 12.6 us
    select_n x2 -> x0, other arithmetic: 0.79 us -> none  [the longest x1 0.72 us: per_device(): table = jnp.where(present, sources, jnp.asarray(nothing))]
    unnamed x12 -> x16, local copies, waits for them, and re-layouts: 0.03 us -> 0.77 us
    dynamic_slice x3 -> x0, local copies, waits for them, and re-layouts: 0.74 us -> none  [the longest x2 0.73 us: per_device(): lax.dynamic_slice_in_dim(op, dir_at * width, width, 1)]
    eq x1 -> x0, local copies, waits for them, and re-layouts: 0.73 us -> none  [per_device(): present = jnp.any(lists == ids[:, :, None], axis=2)]
    ppermute x4, starting transfers between devices: 8.36 us -> 8.76 us  [exchange(): lax.ppermute(block, axis, pairs(n, first))]
    pallas_call x6 -> x8, Pallas kernels: 15.1 us -> 15 us  [call(): pl.pallas_call(functools.partial(body, rows, cols, sides), out_shape=outs...]
  transfers between devices with their start and end apart: 7 -> 7, of which waited for: 1 -> 1; matrix products, arithmetic and copies ran while one was open for 14% -> 7% of each run, Pallas kernels for 30% -> 32%
where the time goes in v3:
time: 31.2 us; the launch traced here: 31 us
  Pallas kernels  15 us (48%)
  starting transfers between devices  12.6 us (40%)
  local copies, waits for them, and re-layouts  1.75 us (6%)
  other arithmetic  1.12 us (4%)
    pallas_call x8, Pallas kernels, call(): pl.pallas_call(functools.partial(body, rows, cols, sides), out_shape=outs...  15 us
    ppermute x4, starting transfers between devices, exchange(): lax.ppermute(block, axis, pairs(n, first))  8.76 us
    ppermute x3, starting transfers between devices, per_device(): lax.ppermute(held, 'dir', [(i, i ^ 1 << bit) for i in range(n_dir)])  3.81 us
    concatenate x2, other arithmetic, per_device(): held = jnp.concatenate(shards, axis=0)  1.12 us
    reshape x1, local copies, waits for them, and re-layouts, per_device(): own = fine_out.reshape(frows * fcols * comps, fdirs)  0.98 us
    unnamed x16, local copies, waits for them, and re-layouts  0.77 us
  transfers between devices with their start and end apart: 7, of which 1 were waited for; matrix products, arithmetic and copies ran while one was open for 7% of the time, Pallas kernels for 32%

profile of v3, /device:TPU:3, one launch (start us, length us, event | category | flops | bytes accessed | tf_op | source)
XLA Modules:
  0.0 31.0 jit_solution(12262964888901284692)
XLA Ops:
  0.0 0.0 copy-start.4
  0.0 0.0 copy-start.5
  0.0 0.0 copy-start.1
  0.0 0.0 copy-start.6
  0.0 2.4 %collective-permute-start.4 = (f32[1,40,2,256]{3,2,1,0:T(2,128)}, f32[1,40,2,256]{3,2,1,0:T(2,128)S(1)}, u32[]{:S(2)}, u32[]{:S(2)}) collective-permute-start(f32[1,40,2,256]{3,2,1,0:T(2,128)} %bitcast.1), channel_id=1, source_target_pairs={{0,4},{1,5},{2,6},{3,7},{4,0},{5,1},{6,2},{7,3},{8,12},{9,13},{10,... | collective-permute-start | bytes 245768 | tf_op jit(solution)/shard_map/ppermute | solution.py:504
  2.4 1.0 %reshape.3.own.src = bf16[192,512]{1,0:T(8,128)(2,1)S(1)} reshape(bf16[6,4,2,4,512]{4,3,2,1,0:T(4,128)(2,1)} %param.11) | data formatting | bytes 393216 | tf_op jit(solution)/shard_map/reshape | solution.py:456
  3.4 0.3 %collective-permute-start = (bf16[192,512]{1,0:T(8,128)(2,1)S(1)}, bf16[192,512]{1,0:T(8,128)(2,1)S(1)}, u32[]{:S(2)}, u32[]{:S(2)}) collective-permute-start(bf16[192,512]{1,0:T(8,128)(2,1)S(1)} %reshape.3.own.src), channel_id=1, source_target_pairs={{0,8},{8,0},{16,24},{24,16},{1,9},{9,1},{17,25},{25,17},{2,10},{10... | collective-permute-start | bytes 589832 | tf_op jit(solution)/shard_map/ppermute | solution.py:155
  3.7 4.1 %collective-permute-start.1 = (bf16[128,512]{1,0:T(8,128)(2,1)S(1)}, bf16[128,512]{1,0:T(8,128)(2,1)S(1)}, u32[]{:S(2)}, u32[]{:S(2)}) collective-permute-start(bf16[128,512]{1,0:T(8,128)(2,1)S(1)} %edge.1), channel_id=1, source_target_pairs={{8,16},{16,8},{9,17},{17,9},{10,18},{18,10},{11,19},{19,11},{12,20... | collective-permute-start | bytes 393224 | tf_op jit(solution)/shard_map/ppermute | solution.py:155
  7.8 0.0 collective-permute-done.4.refs_1_
  7.8 1.0 %pad_maximum_fusion.1 = f32[2,40,2,256]{3,2,1,0:T(2,128)S(1)} fusion(f32[1,40,2,256]{3,2,1,0:T(2,128)S(1)} %collective-permute-done.4.refs_1_, f32[1,40,2,256]{3,2,1,0:T(2,128)} %bitcast.2), kind=kLoop, calls=%fused_computation.1 | loop fusion | flops 40960 | bytes 327680 | tf_op jit(solution)/shard_map/concatenate | solution.py:503
  8.8 0.0 copy-start.2
  8.8 1.4 %collective-permute-start.5 = (f32[2,40,2,256]{3,2,1,0:T(2,128)S(1)}, f32[2,40,2,256]{3,2,1,0:T(2,128)S(1)}, u32[]{:S(2)}, u32[]{:S(2)}) collective-permute-start(f32[2,40,2,256]{3,2,1,0:T(2,128)S(1)} %pad_maximum_fusion.1), channel_id=1, source_target_pairs={{0,2},{1,3},{2,0},{3,1},{4,6},{5,7},{6,4},{7,5},{8,10},{9,11},{10,... | collective-permute-start | bytes 491528 | tf_op jit(solution)/shard_map/ppermute | solution.py:504
  10.1 0.0 copy-done.4
  10.1 0.0 copy-done.5
  10.2 0.0 copy-start.7
  10.2 0.7 %copy-done.7 = s32[3,16,32]{2,1,0:T(8,128)S(1)} copy-done((s32[3,16,32]{2,1,0:T(8,128)S(1)}, s32[3,16,32]{2,1,0:T(8,128)}, u32[]{:S(2)}) %copy-start.7) | copy-done | bytes 6168
  10.9 0.6 %lists.2.table = s32[30,50]{1,0:T(8,128)S(1)} custom-call(s32[6,32,32]{2,1,0:T(8,128)S(1)} %copy-done.5, s32[3,16,32]{2,1,0:T(8,128)S(1)} %copy-done.7, s32[4,62,50]{2,1,0:T(8,128)S(1)} %copy-done.4), custom_call_target="tpu_custom_call" | custom-call | tf_op jit(solution)/shard_map/lists/pallas_call | solution.py:478
  11.5 0.0 copy-done.1
  11.5 0.0 copy-done.6
  11.5 1.8 %block.1 = (f32[24,8,512]{2,1,0:T(8,128)S(1)}, f32[8,2048]{1,0:T(8,128)S(1)}) custom-call(s32[30,50]{1,0:T(8,128)S(1)} %lists.2.table, bf16[192,512]{1,0:T(8,128)(2,1)S(1)} %reshape.3.own.src, f32[4,2048]{1,0:T(4,128)S(1)} %copy-done.6, f32[40,2,512]{2,1,0:T(2,128)S(1)} %copy-done.1), custom_call_target="tpu_custom_call" | custom-call | tf_op jit(solution)/shard_map/block/pallas_call | solution.py:478
  13.3 0.0 copy-start
  13.3 0.0 collective-permute-done.1.second
  13.3 0.0 collective-permute-done.first
  13.4 1.9 %collective-permute-start.3 = (bf16[512,512]{1,0:T(8,128)(2,1)S(1)}, bf16[512,512]{1,0:T(8,128)(2,1)S(1)}, u32[]{:S(2)}, u32[]{:S(2)}) collective-permute-start(bf16[512,512]{1,0:T(8,128)(2,1)S(1)} %pack.1.strip), channel_id=1, source_target_pairs={{0,1},{1,0},{2,3},{3,2},{4,5},{5,4},{6,7},{7,6},{8,9},{9,8},{10,11... | collective-permute-start | bytes 1572872 | tf_op jit(solution)/shard_map/ppermute | solution.py:155
  15.2 2.5 %collective-permute-start.2 = (bf16[512,512]{1,0:T(8,128)(2,1)S(1)}, bf16[512,512]{1,0:T(8,128)(2,1)S(1)}, u32[]{:S(2)}, u32[]{:S(2)}) collective-permute-start(bf16[512,512]{1,0:T(8,128)(2,1)S(1)} %pack.1.strip), channel_id=1, source_target_pairs={{1,2},{2,1},{3,4},{4,3},{5,6},{6,5},{9,10},{10,9},{11,12},{12,11},... | collective-permute-start | bytes 1572872 | tf_op jit(solution)/shard_map/ppermute | solution.py:155
  17.7 0.0 collective-permute-done.5.refs_2_
  17.8 0.0 copy-done.2
  17.8 0.2 pad_maximum_fusion
  17.9 0.1 collective-permute-start.6
  18.0 0.0 copy-done
  18.0 0.0 copy-start.3
  18.0 2.4 %own.1 = (f32[17,8,2048]{2,1,0:T(8,128)S(1)}, f32[24,8,512]{2,1,0:T(8,128)S(1)}) custom-call(s32[30,50]{1,0:T(8,128)S(1)} %lists.2.table, bf16[512,512]{1,0:T(8,128)(2,1)S(1)} %pack.1.strip, bf16[512,2048]{1,0:T(8,128)(2,1)S(1)} %copy-done, f32[8,2048]{1,0:T(8,128)S(1)} %get-tuple-element.15.trig, f32[40,2,512]{2,1,0:T(2,128)S(1)} %copy-done.1, ...), custom_call_target="tpu_custom_call" | custom-call | tf_op jit(solution)/shard_map/own/pallas_call | solution.py:478
  20.4 0.0 collective-permute-done.3.src
  20.4 0.0 copy-done.3
  20.4 2.7 %side.1 = (f32[17,8,2048]{2,1,0:T(8,128)S(1)}, f32[12,8,512]{2,1,0:T(8,128)S(1)}) custom-call(s32[30,50]{1,0:T(8,128)S(1)} %lists.2.table, s32[4,8,30]{2,1,0:T(8,128)S(1)} %copy-done.3, bf16[512,512]{1,0:T(8,128)(2,1)S(1)} %collective-permute-done.3.src, bf16[512,2048]{1,0:T(8,128)(2,1)S(1)} %copy-done, f32[8,2048]{1,0:T(8,128)S(1)} %get-tuple-element.15.trig, ...), custom_call_target="tpu_custom_call" | custom-call | tf_op jit(solution)/shard_map/side/pallas_call | solution.py:478
  23.1 0.0 collective-permute-done.6.refs_3_
  23.1 2.3 %inner.1 = (f32[40,2,2048]{2,1,0:T(2,128)S(1)}, f32[6,8,2048]{2,1,0:T(8,128)S(1)}, f32[6,8,2048]{2,1,0:T(8,128)S(1)}) custom-call(s32[30,50]{1,0:T(8,128)S(1)} %lists.2.table, s32[4,8,30]{2,1,0:T(8,128)S(1)} %copy-done.3, f32[17,8,2048]{2,1,0:T(8,128)S(1)} %get-tuple-element.16.pat_own, f32[17,8,2048]{2,1,0:T(8,128)S(1)} %get-tuple-element.17.pat_a, ...), custom_call_target="tpu_custom_call" | custom-call | tf_op jit(solution)/shard_map/inner/pallas_call | solution.py:478
  25.5 0.3 collective-permute-done.2.src
  25.7 5.2 %last.1 = f32[6,4,2,4,512]{4,3,2,1,0:T(4,128)} custom-call(s32[30,50]{1,0:T(8,128)S(1)} %lists.2.table, s32[4,8,30]{2,1,0:T(8,128)S(1)} %copy-done.3, bf16[512,512]{1,0:T(8,128)(2,1)S(1)} %collective-permute-done.2.src, bf16[512,2048]{1,0:T(8,128)(2,1)S(1)} %copy-done, f32[8,2048]{1,0:T(8,128)S(1)} %get-tuple-element.15.trig, f32[40,2,512]{2,1,0:T(2,128)S(1)} %copy-done.1, ...), custom_call_target="tpu_custom_call" | custom-call | tf_op jit(solution)/shard_map/last/pallas_call | solution.py:478
  (2 shorter events, 0.0 us)
Async XLA Ops:
  0.0 10.1 %copy-start.4 = (s32[4,62,50]{2,1,0:T(8,128)S(1)}, s32[4,62,50]{2,1,0:T(8,128)}, u32[]{:S(2)}) copy-start(s32[4,62,50]{2,1,0:T(8,128)} %constant.5.clone.lists) | copy-start | bytes 148804
  0.0 10.1 %copy-start.5 = (s32[6,32,32]{2,1,0:T(8,128)S(1)}, s32[6,32,32]{2,1,0:T(8,128)}, u32[]{:S(2)}) copy-start(s32[6,32,32]{2,1,0:T(8,128)} %fine_op.1) | copy-start | bytes 73732
  0.0 11.5 %copy-start.1 = (f32[40,2,512]{2,1,0:T(2,128)S(1)}, f32[40,2,512]{2,1,0:T(2,128)}, u32[]{:S(2)}) copy-start(f32[40,2,512]{2,1,0:T(2,128)} %fops.7) | copy-start | bytes 491524
  0.0 11.5 %copy-start.6 = (f32[4,2048]{1,0:T(4,128)S(1)}, f32[4,2048]{1,0:T(4,128)}, u32[]{:S(2)}) copy-start(f32[4,2048]{1,0:T(4,128)} %phase.1) | copy-start | bytes 98308
  0.0 7.8 %collective-permute-start.4 = (f32[1,40,2,256]{3,2,1,0:T(2,128)}, f32[1,40,2,256]{3,2,1,0:T(2,128)S(1)}, u32[]{:S(2)}, u32[]{:S(2)}) collective-permute-start(f32[1,40,2,256]{3,2,1,0:T(2,128)} %bitcast.1), channel_id=1, source_target_pairs={{0,4},{1,5},{2,6},{3,7},{4,0},{5,1},{6,2},{7,3},{8,12},{9,13},{10,... | collective-permute-start | bytes 245768 | tf_op jit(solution)/shard_map/ppermute | solution.py:504
  3.4 9.9 %collective-permute-start = (bf16[192,512]{1,0:T(8,128)(2,1)S(1)}, bf16[192,512]{1,0:T(8,128)(2,1)S(1)}, u32[]{:S(2)}, u32[]{:S(2)}) collective-permute-start(bf16[192,512]{1,0:T(8,128)(2,1)S(1)} %reshape.3.own.src), channel_id=1, source_target_pairs={{0,8},{8,0},{16,24},{24,16},{1,9},{9,1},{17,25},{25,17},{2,10},{10... | collective-permute-start | bytes 589832 | tf_op jit(solution)/shard_map/ppermute | solution.py:155
  3.7 9.6 %collective-permute-start.1 = (bf16[128,512]{1,0:T(8,128)(2,1)S(1)}, bf16[128,512]{1,0:T(8,128)(2,1)S(1)}, u32[]{:S(2)}, u32[]{:S(2)}) collective-permute-start(bf16[128,512]{1,0:T(8,128)(2,1)S(1)} %edge.1), channel_id=1, source_target_pairs={{8,16},{16,8},{9,17},{17,9},{10,18},{18,10},{11,19},{19,11},{12,20... | collective-permute-start | bytes 393224 | tf_op jit(solution)/shard_map/ppermute | solution.py:155
  8.8 9.0 %copy-start.2 = (f32[40,2,256]{2,1,0:T(2,128)S(1)}, f32[40,2,256]{2,1,0:T(2,128)}, u32[]{:S(2)}) copy-start(f32[40,2,256]{2,1,0:T(2,128)} %param.15) | copy-start | bytes 245764
  8.8 9.0 %collective-permute-start.5 = (f32[2,40,2,256]{3,2,1,0:T(2,128)S(1)}, f32[2,40,2,256]{3,2,1,0:T(2,128)S(1)}, u32[]{:S(2)}, u32[]{:S(2)}) collective-permute-start(f32[2,40,2,256]{3,2,1,0:T(2,128)S(1)} %pad_maximum_fusion.1), channel_id=1, source_target_pairs={{0,2},{1,3},{2,0},{3,1},{4,6},{5,7},{6,4},{7,5},{8,10},{9,11},{10,... | collective-permute-start | bytes 491528 | tf_op jit(solution)/shard_map/ppermute | solution.py:504
  10.2 0.7 %copy-start.7 = (s32[3,16,32]{2,1,0:T(8,128)S(1)}, s32[3,16,32]{2,1,0:T(8,128)}, u32[]{:S(2)}) copy-start(s32[3,16,32]{2,1,0:T(8,128)} %par_op.1) | copy-start | bytes 18436
  13.3 4.7 %copy-start = (bf16[512,2048]{1,0:T(8,128)(2,1)S(1)}, bf16[512,2048]{1,0:T(8,128)(2,1)}, u32[]{:S(2)}) copy-start(bf16[512,2048]{1,0:T(8,128)(2,1)} %interp.5) | copy-start | bytes 6291460
  13.4 7.0 %collective-permute-start.3 = (bf16[512,512]{1,0:T(8,128)(2,1)S(1)}, bf16[512,512]{1,0:T(8,128)(2,1)S(1)}, u32[]{:S(2)}, u32[]{:S(2)}) collective-permute-start(bf16[512,512]{1,0:T(8,128)(2,1)S(1)} %pack.1.strip), channel_id=1, source_target_pairs={{0,1},{1,0},{2,3},{3,2},{4,5},{5,4},{6,7},{7,6},{8,9},{9,8},{10,11... | collective-permute-start | bytes 1572872 | tf_op jit(solution)/shard_map/ppermute | solution.py:155
  15.2 10.5 %collective-permute-start.2 = (bf16[512,512]{1,0:T(8,128)(2,1)S(1)}, bf16[512,512]{1,0:T(8,128)(2,1)S(1)}, u32[]{:S(2)}, u32[]{:S(2)}) collective-permute-start(bf16[512,512]{1,0:T(8,128)(2,1)S(1)} %pack.1.strip), channel_id=1, source_target_pairs={{1,2},{2,1},{3,4},{4,3},{5,6},{6,5},{9,10},{10,9},{11,12},{12,11},... | collective-permute-start | bytes 1572872 | tf_op jit(solution)/shard_map/ppermute | solution.py:155
  17.9 5.2 %collective-permute-start.6 = (f32[4,40,2,256]{3,2,1,0:T(2,128)S(1)}, f32[4,40,2,256]{3,2,1,0:T(2,128)S(1)}, u32[]{:S(2)}, u32[]{:S(2)}) collective-permute-start(f32[4,40,2,256]{3,2,1,0:T(2,128)S(1)} %pad_maximum_fusion), channel_id=1, source_target_pairs={{0,1},{1,0},{2,3},{3,2},{4,5},{5,4},{6,7},{7,6},{8,9},{9,8},{10,11... | collective-permute-start | bytes 983048 | tf_op jit(solution)/shard_map/ppermute | solution.py:504
  18.0 2.4 %copy-start.3 = (s32[4,8,30]{2,1,0:T(8,128)S(1)}, s32[4,8,30]{2,1,0:T(8,128)}, u32[]{:S(2)}) copy-start(s32[4,8,30]{2,1,0:T(8,128)} %constant.4.clone.ids) | copy-start | bytes 11524

commit v4 on v3

--- a/solution.py
+++ b/solution.py
@@ -10,7 +10,7 @@
 
 CHUNK = 512
 PIECE = 256
-LIMITS = {"block": 8, "pack": 4, "edge": 4, "lists": 4, "own": 16, "side": 16, "inner": 12, "last": 24}
+LIMITS = {"block": 8, "pack": 4, "edge": 4, "lists": 4, "both": 20, "inner": 12, "last": 24}
 F32, BF16 = jnp.float32, jnp.bfloat16
 
 
@@ -199,38 +199,45 @@
     buffer[...] = out.reshape(-1, comps, CHUNK)
 
 
-def shifts(trig, j, comps):
-    lanes = slice(j * CHUNK, (j + 1) * CHUNK)
-    return [jnp.broadcast_to(trig[k : k + 1, lanes], (comps, CHUNK)) for k in range(8)]
+def in_steps(steps):
+    for tasks in steps:
+        for task in tasks:
+            task()
+
+
+def shift_rows(trig, lanes, comps):
+    width = lanes.stop - lanes.start
+    sign = jnp.where(lax.broadcasted_iota(jnp.int32, (comps, 1), 0) < comps // 2, 1.0, -1.0).astype(F32)
+    rows = [jnp.broadcast_to(trig[k : k + 1, lanes], (comps, width)) for k in range(8)]
+    return rows[:4], [sign * row for row in rows[4:]]
 
 
 def aggregate_chunk(buffer, trig, j, pattern, width, sides):
     comps = 2 * sides
     for at in range(0, CHUNK, PIECE):
         lanes = slice(j * CHUNK + at, j * CHUNK + at + PIECE)
-        shift = [jnp.broadcast_to(trig[k : k + 1, lanes], (comps, PIECE)) for k in range(8)]
+        shift = shift_rows(trig, lanes, comps)
         for q in range(buffer.shape[0] // 4):
             r, c = divmod(q, width)
             total = [None, None]
             for k in range(4):
                 piece = buffer[(2 * r + k // 2) * (2 * width) + 2 * c + k % 2, :, at : at + PIECE]
                 for i in range(2):
-                    add = shift[4 * i + k] * piece
+                    add = shift[i][k] * piece
                     total[i] = add if k == 0 else total[i] + add
-            whole = total[0] + times_i(total[1], sides)
+            whole = total[0] + pltpu.roll(total[1], sides, 0)
             pattern[q, :, lanes] = whole.astype(BF16).astype(F32)
 
 
-def aggregate(src, interp, trig, buffers, pattern, width, sides, beside=lambda j: None, done=lambda j: None):
-    comps = 2 * sides
-    steps = interp.shape[1] // CHUNK
-    spread_chunk(src, interp, 0, buffers[0], comps)
-    for j in range(steps):
-        if j + 1 < steps:
-            spread_chunk(src, interp, j + 1, buffers[(j + 1) % 2], comps)
-        beside(j)
-        aggregate_chunk(buffers[j % 2], trig, j, pattern, width, sides)
-        done(j)
+def aggregate_tasks(src, interp, trig, buffers, pattern, width, sides):
+    steps = range(interp.shape[1] // CHUNK)
+    spread = [
+        functools.partial(spread_chunk, src, interp, j, buffers[j % 2], 2 * sides) for j in steps
+    ]
+    sums = [
+        functools.partial(aggregate_chunk, buffers[j % 2], trig, j, pattern, width, sides) for j in steps
+    ]
+    return spread, sums
 
 
 def dealt(items, j, steps):
@@ -250,13 +257,13 @@
     return [real + times_i(imag, comps // 2) for real, imag in sums]
 
 
-def near_side(table, ids, fops, fine, rows, cols, group, right, store, classes):
+def near_side(table, fops, fine, rows, cols, group, right, store, classes):
     counts = slot_counts(rows, cols, 2)
-    base, count, which = starts(counts)[group], counts[group], parities()
+    base, count = starts(counts)[group], counts[group]
     first_col = right * (2 * cols - 2)
     for a, c in classes:
         boxes = [(2 * r + a) * (2 * cols) + first_col + c for r in range(rows)]
-        op_ids = [ids[which, 2 * a + c, (group - 2) * count + t] for t in range(count)]
+        op_ids = [table[5 * rows * cols + 2 * a + c, (group - 2) * count + t] for t in range(count)]
         for r, value in enumerate(near_sums(table, fops, fine, boxes, base, op_ids)):
             store((2 * r + a) * 2 + c, value)
 
@@ -278,7 +285,8 @@
 
 def lists_kernel(rows, cols, sides, fine_op, par_op, lists, table):
     which = parities()
-    at, boxes = 0, table.shape[0]
+    at, boxes = 0, 5 * rows * cols
+    table[boxes:] = lists[which, 2 * boxes + 2 :]
     for op, scale, none in ((fine_op, 2, 2 * boxes), (par_op, 1, 2 * boxes + 1)):
         across = cols * scale
         first = pl.multiple_of(lax.axis_index("dir") * across, across)
@@ -307,54 +315,63 @@
         at += ref.shape[0]
 
 
-def own_kernel(rows, cols, sides, table, strip, interp, trig, fops, near_block, pattern, near, fine, even, odd):
+def both_kernel(
+    rows, cols, sides, table, strip, side_a, interp, trig, fops, near_block,
+    pat_own, near, pat_a, near_a, fine, fine_a, even, odd,
+):
     base = starts(slot_counts(rows, cols, 2))[1]
     inside = near.shape[0] * 2 * sides
-    widen(strip.at[pl.ds(inside, strip.shape[0] - inside)], fine, 2 * sides)
+    buffers = (even, odd)
     steps = interp.shape[1] // CHUNK
 
-    def beside(j):
-        for box in dealt(range(near.shape[0]), j, min(steps, 2)) if j < 2 else ():
+    def halo(boxes):
+        for box in boxes:
             op_ids = [o for o, _ in fine_slots(*divmod(box, 2 * cols), rows, cols, 0, 0)[1]]
             more = near_sums(table, fops, fine, [box], base, op_ids)[0] if op_ids else 0.0
             near[box] = near_block[box] + more
 
-    aggregate(strip, interp, trig, (even, odd), pattern, cols, sides, beside)
-    zero_box(pattern)
-
-
-def side_kernel(rows, cols, sides, table, ids, src, interp, trig, fops, pattern, near, fine, even, odd):
-    widen(src, fine, 2 * sides)
-
     def store(at, value):
-        near[at] = value
-
-    steps = interp.shape[1] // CHUNK
-
-    def beside(j):
-        near_side(table, ids, fops, fine, rows, cols, 2, 1 - parity("dir"), store, dealt(PARITIES, j, steps))
-
-    aggregate(src, interp, trig, (even, odd), pattern, halo_sizes(cols)[0], sides, beside)
-    zero_box(pattern)
+        near_a[at] = value
+
+    def beside(classes):
+        near_side(table, fops, fine_a, rows, cols, 2, 1 - parity("dir"), store, classes)
+
+    widen(strip.at[pl.ds(inside, strip.shape[0] - inside)], fine, 2 * sides)
+    widen(side_a, fine_a, 2 * sides)
+    zero_box(pat_own)
+    zero_box(pat_a)
+    boxes = strip.shape[0] // (2 * sides)
+    whole = jnp.concatenate([strip[...], side_a[...]], axis=0)
+    for j in range(steps + 1):
+        if j < steps:
+            spread_chunk(whole, interp, j, buffers[j % 2], 2 * sides)
+        if j < 2:
+            beside(PARITIES[2 * j : 2 * j + 2])
+        if j in (2, 3):
+            halo(dealt(range(near.shape[0]), j - 2, 2))
+        if j:
+            buffer = buffers[(j - 1) % 2]
+            aggregate_chunk(buffer.at[pl.ds(0, boxes)], trig, j - 1, pat_own, cols, sides)
+            aggregate_chunk(buffer.at[pl.ds(boxes, boxes)], trig, j - 1, pat_a, halo_sizes(cols)[0], sides)
 
 
 def parent_groups(rows, cols):
     return [[(r, c) for r in range(start, rows, 2)] for c in range(cols) for start in range(2)]
 
 
-def parent_sums(rows, cols, sides, table, ids, pops, sources, index, group, first, width):
-    comps, which = 2 * sides, parities()
+def parent_sums(rows, cols, sides, table, pops, sources, index, group, first, width):
+    comps = 2 * sides
     rows_at = [4 * rows * cols + r * cols + c for r, c in group]
     sums = [None] * len(group)
     for base, count, ref in sources:
         for t in range(base, base + count):
-            op_id = ids[which, 4 + index, t]
+            op_id = table[5 * rows * cols + 4 + index, t]
             coefs = [row_of(pops, (op_id,), i, first, width, comps) for i in range(2)]
             add_slots(sums, coefs, [ref[table[row, t], :, first : first + width] for row in rows_at])
     return sums
 
 
-def inner_kernel(rows, cols, sides, table, ids, pat_own, pat_a, *refs):
+def inner_kernel(rows, cols, sides, table, pat_own, pat_a, *refs):
     *shards, pops, real, imag = refs
     at = 0
     for ref in shards:
@@ -369,7 +386,7 @@
     for first in range(0, real.shape[2], 2 * CHUNK):
         for index, group in enumerate(parent_groups(rows, cols)):
             sums = parent_sums(
-                rows, cols, sides, table, ids, pops, sources, index, group, first, 2 * CHUNK
+                rows, cols, sides, table, pops, sources, index, group, first, 2 * CHUNK
             )
             for (r, c), (re, im) in zip(group, sums):
                 real[r * cols + c, :, first : first + 2 * CHUNK] = re
@@ -378,7 +395,7 @@
 
 def last_kernel(
     rows, cols, sides,
-    table, ids,
+    table,
     src, interp, trig, fops, pops, real, imag, near_own, near_a,
     out,
     fine, even, odd, pat_b, child, near_b, acc,
@@ -387,18 +404,32 @@
     fcols = 2 * cols
     par_counts = slot_counts(rows, cols, 1)
     a_right = 1 - parity("dir")
-    widen(src, fine, comps)
-    zero_box(pat_b)
+    steps = interp.shape[1] // CHUNK
 
     def store(at, value):
         near_b[1 - a_right, at] = value
 
-    for at in range(near_a.shape[0]):
-        near_b[a_right, at] = near_a[at]
-    steps = interp.shape[1] // CHUNK
-
-    def beside(j):
-        near_side(table, ids, fops, fine, rows, cols, 3, 1 - a_right, store, dealt(PARITIES, j, steps))
+    def beside():
+        near_side(table, fops, fine, rows, cols, 3, 1 - a_right, store, PARITIES)
+
+    def keep():
+        for at in range(near_a.shape[0]):
+            near_b[a_right, at] = near_a[at]
+
+    def far(j):
+        lanes = slice(j * CHUNK, (j + 1) * CHUNK)
+        cos, sin = shift_rows(trig, lanes, comps)
+        sources = [(starts(par_counts)[2], par_counts[2], pat_b)]
+        for index, group in enumerate(parent_groups(rows, cols)):
+            sums = parent_sums(rows, cols, sides, table, pops, sources, index, group, j * CHUNK, CHUNK)
+            for (r, c), (re, im) in zip(group, sums):
+                box = r * cols + c
+                total = re + real[box, :, lanes] + times_i(im + imag[box, :, lanes], sides)
+                total = total.astype(BF16).astype(F32)
+                turned = pltpu.roll(total, sides, 0)
+                for k in range(4):
+                    at = (2 * r + k // 2) * fcols + 2 * c + k % 2
+                    child[at, :, lanes] = (cos[k] * total + sin[k] * turned).astype(BF16)
 
     def back(j):
         lanes = slice(j * CHUNK, (j + 1) * CHUNK)
@@ -408,25 +439,17 @@
         ).reshape(acc.shape)
         acc[...] = more if j == 0 else acc[...] + more
 
-    def far(j):
-        if j:
-            back(j - 1)
-        lanes = slice(j * CHUNK, (j + 1) * CHUNK)
-        shift = shifts(trig, j, comps)
-        sources = [(starts(par_counts)[2], par_counts[2], pat_b)]
-        for index, group in enumerate(parent_groups(rows, cols)):
-            sums = parent_sums(rows, cols, sides, table, ids, pops, sources, index, group, j * CHUNK, CHUNK)
-            for (r, c), (re, im) in zip(group, sums):
-                box = r * cols + c
-                total = re + real[box, :, lanes] + times_i(im + imag[box, :, lanes], sides)
-                total = total.astype(BF16).astype(F32)
-                turned = times_i(total, sides)
-                for k in range(4):
-                    at = (2 * r + k // 2) * fcols + 2 * c + k % 2
-                    child[at, :, lanes] = (shift[k] * total - shift[4 + k] * turned).astype(BF16)
-
-    aggregate(src, interp, trig, (even, odd), pat_b, halo_sizes(cols)[1], sides, beside, far)
-    back(steps - 1)
+    spread, sums = aggregate_tasks(src, interp, trig, (even, odd), pat_b, halo_sizes(cols)[1], sides)
+    plan = [[] for _ in range(steps + 3)]
+    for j in range(steps):
+        plan[j].append(spread[j])
+        plan[j + 1].append(sums[j])
+        plan[j + 2].append(functools.partial(far, j))
+        plan[min(j + 4, steps + 2) if j + 1 < steps else steps + 2].append(functools.partial(back, j))
+    plan[0] += [
+        functools.partial(widen, src, fine, comps), functools.partial(zero_box, pat_b), beside, keep,
+    ]
+    in_steps(plan)
 
     scale = fdirs / interp.shape[1]
     for r in range(2 * rows):
@@ -458,9 +481,10 @@
     sources, op_ids, nothing = build_tables(
         rows, cols, {2: [frows * fcols, 4 * outside, 4 * boxes, 4 * boxes], 1: [boxes] * 3}
     )
-    ids = jnp.asarray(shared_ids(op_ids, rows, cols))
+    ids = shared_ids(op_ids, rows, cols)
+    ids = np.pad(ids, [(0, 0), (0, 0), (0, sources.shape[2] - ids.shape[2])])
     nothing = np.broadcast_to(nothing[[0, -1]], (len(PARITIES), 2, nothing.shape[1]))
-    lists = jnp.asarray(np.concatenate([sources, op_ids, nothing], axis=1))
+    lists = jnp.asarray(np.concatenate([sources, op_ids, nothing, ids], axis=1))
 
     smem = pl.BlockSpec(memory_space=pltpu.SMEM)
     vmem = pl.BlockSpec(memory_space=pltpu.VMEM)
@@ -488,7 +512,7 @@
     near = shape(frows * fcols, comps, fdirs)
     pattern = shape(boxes + 1, comps, pdirs)
     table = call(
-        lists_kernel, "lists", 0, [jax.ShapeDtypeStruct(sources.shape[1:], jnp.int32)], [],
+        lists_kernel, "lists", 0, [jax.ShapeDtypeStruct((5 * rows * cols + ids.shape[1], ids.shape[2]), jnp.int32)], [],
         fine_op, parent_op, lists,
     )[0]
     first, second = halo_sizes(rows)
@@ -513,29 +537,25 @@
     side_a, side_b = exchange([strip, strip], "dir")
     if parent_ops.shape[2] % 128:
         shards = [in_order(jnp.concatenate(shards, axis=0), "dir")]
-    pat_own, near_own = call(
-        own_kernel, "own", 1, [pattern, near],
-        [scratch(4 * outside + 1, comps, fdirs)] + [scratch(4 * boxes, comps, CHUNK)] * 2,
-        table, strip, interp, trig, fine_ops, near_block,
-    )
-    pat_a, near_a = call(
-        side_kernel, "side", 2, [pattern, shape(frows * 2, comps, fdirs)], group_scratch(4 * boxes),
-        table, ids, side_a, interp, trig, fine_ops,
+    pat_own, near_own, pat_a, near_a = call(
+        both_kernel, "both", 1, [pattern, near, pattern, shape(frows * 2, comps, fdirs)],
+        [scratch(4 * outside + 1, comps, fdirs), scratch(4 * boxes + 1, comps, fdirs)] + [scratch(8 * boxes, comps, CHUNK)] * 2,
+        table, strip, side_a, interp, trig, fine_ops, near_block,
     )
     part = shape(rows * cols, comps, pdirs)
     pops, real, imag = call(
-        inner_kernel, "inner", 2, [shape(parent_ops.shape[0], 2, pdirs), part, part], [],
-        table, ids, pat_own, pat_a, *shards,
+        inner_kernel, "inner", 1, [shape(parent_ops.shape[0], 2, pdirs), part, part], [],
+        table, pat_own, pat_a, *shards,
     )
     return call(
-        last_kernel, "last", 2, [jax.ShapeDtypeStruct(fine_out.shape, F32)],
+        last_kernel, "last", 1, [jax.ShapeDtypeStruct(fine_out.shape, F32)],
         group_scratch(4 * boxes) + [
             scratch(boxes + 1, comps, pdirs),
             scratch(frows * fcols, comps, pdirs, kind=BF16),
             scratch(2, frows * 2, comps, fdirs),
             scratch(frows * fcols, comps, fdirs),
         ],
-        table, ids, side_b, interp, trig, fine_ops, pops, real, imag, near_own, near_a,
+        table, side_b, interp, trig, fine_ops, pops, real, imag, near_own, near_a,
     )[0]
 
 

time: 31.2 us -> 31 us (level)
  Pallas kernels: 15 us -> 13.8 us
  waiting for transfers between devices: 0.29 us -> 1.26 us
    pallas_call x8 -> x7, Pallas kernels: 15 us -> 13.8 us  [call(): pl.pallas_call(functools.partial(body, rows, cols, sides), out_shape=outs...]
    ppermute x4, waiting for transfers between devices: 0.28 us -> 1.25 us  [exchange(): lax.ppermute(block, axis, pairs(n, first))]
    unnamed x16 -> x14, local copies, waits for them, and re-layouts: 0.77 us -> 0.77 us
  transfers between devices with their start and end apart: 7 -> 7, of which waited for: 1 -> 1; matrix products, arithmetic and copies ran while one was open for 7% -> 7% of each run, Pallas kernels for 32% -> 29%
where the time goes in v4:
time: 31 us; the launch traced here: 30.8 us
  Pallas kernels  13.8 us (45%)
  starting transfers between devices  12.6 us (41%)
  local copies, waits for them, and re-layouts  1.74 us (6%)
  waiting for transfers between devices  1.26 us (4%)
  other arithmetic  1.12 us (4%)
    pallas_call x7, Pallas kernels, call(): pl.pallas_call(functools.partial(body, rows, cols, sides), out_shape=outs...  13.8 us
    ppermute x4, starting transfers between devices, exchange(): lax.ppermute(block, axis, pairs(n, first))  8.82 us
    ppermute x3, starting transfers between devices, per_device(): lax.ppermute(held, 'dir', [(i, i ^ 1 << bit) for i in range(n_dir)])  3.81 us
    ppermute x4, waiting for transfers between devices, exchange(): lax.ppermute(block, axis, pairs(n, first))  1.25 us
    concatenate x2, other arithmetic, per_device(): held = jnp.concatenate(shards, axis=0)  1.12 us
    reshape x1, local copies, waits for them, and re-layouts, per_device(): own = fine_out.reshape(frows * fcols * comps, fdirs)  0.98 us
    unnamed x14, local copies, waits for them, and re-layouts  0.77 us
  transfers between devices with their start and end apart: 7, of which 1 were waited for; matrix products, arithmetic and copies ran while one was open for 7% of the time, Pallas kernels for 29%

profile of v4, /device:TPU:3, one launch (start us, length us, event | category | flops | bytes accessed | tf_op | source)
XLA Modules:
  0.0 30.8 jit_solution(152316145864690019)
XLA Ops:
  0.0 0.0 copy-start.3
  0.0 0.0 copy-start.4
  0.0 0.0 copy-start.1
  0.0 0.0 copy-start.5
  0.0 2.4 %collective-permute-start.4 = (f32[1,40,2,256]{3,2,1,0:T(2,128)}, f32[1,40,2,256]{3,2,1,0:T(2,128)S(1)}, u32[]{:S(2)}, u32[]{:S(2)}) collective-permute-start(f32[1,40,2,256]{3,2,1,0:T(2,128)} %bitcast.1), channel_id=1, source_target_pairs={{0,4},{1,5},{2,6},{3,7},{4,0},{5,1},{6,2},{7,3},{8,12},{9,13},{10,... | collective-permute-start | bytes 245768 | tf_op jit(solution)/shard_map/ppermute | solution.py:528
  2.4 1.0 %reshape.3.own.src = bf16[192,512]{1,0:T(8,128)(2,1)S(1)} reshape(bf16[6,4,2,4,512]{4,3,2,1,0:T(4,128)(2,1)} %param.10) | data formatting | bytes 393216 | tf_op jit(solution)/shard_map/reshape | solution.py:479
  3.4 0.3 %collective-permute-start = (bf16[192,512]{1,0:T(8,128)(2,1)S(1)}, bf16[192,512]{1,0:T(8,128)(2,1)S(1)}, u32[]{:S(2)}, u32[]{:S(2)}) collective-permute-start(bf16[192,512]{1,0:T(8,128)(2,1)S(1)} %reshape.3.own.src), channel_id=1, source_target_pairs={{0,8},{8,0},{16,24},{24,16},{1,9},{9,1},{17,25},{25,17},{2,10},{10... | collective-permute-start | bytes 589832 | tf_op jit(solution)/shard_map/ppermute | solution.py:155
  3.7 4.1 %collective-permute-start.1 = (bf16[128,512]{1,0:T(8,128)(2,1)S(1)}, bf16[128,512]{1,0:T(8,128)(2,1)S(1)}, u32[]{:S(2)}, u32[]{:S(2)}) collective-permute-start(bf16[128,512]{1,0:T(8,128)(2,1)S(1)} %edge.1), channel_id=1, source_target_pairs={{8,16},{16,8},{9,17},{17,9},{10,18},{18,10},{11,19},{19,11},{12,20... | collective-permute-start | bytes 393224 | tf_op jit(solution)/shard_map/ppermute | solution.py:155
  7.8 0.0 collective-permute-done.4.refs_1_
  7.8 1.0 %pad_maximum_fusion.1 = f32[2,40,2,256]{3,2,1,0:T(2,128)S(1)} fusion(f32[1,40,2,256]{3,2,1,0:T(2,128)S(1)} %collective-permute-done.4.refs_1_, f32[1,40,2,256]{3,2,1,0:T(2,128)} %bitcast.2), kind=kLoop, calls=%fused_computation.1 | loop fusion | flops 40960 | bytes 327680 | tf_op jit(solution)/shard_map/concatenate | solution.py:527
  8.8 0.0 copy-start.2
  8.8 1.4 %collective-permute-start.5 = (f32[2,40,2,256]{3,2,1,0:T(2,128)S(1)}, f32[2,40,2,256]{3,2,1,0:T(2,128)S(1)}, u32[]{:S(2)}, u32[]{:S(2)}) collective-permute-start(f32[2,40,2,256]{3,2,1,0:T(2,128)S(1)} %pad_maximum_fusion.1), channel_id=1, source_target_pairs={{0,2},{1,3},{2,0},{3,1},{4,6},{5,7},{6,4},{7,5},{8,10},{9,11},{10,... | collective-permute-start | bytes 491528 | tf_op jit(solution)/shard_map/ppermute | solution.py:528
  10.1 0.0 copy-done.3
  10.1 0.0 copy-done.4
  10.2 0.0 copy-start.6
  10.2 0.7 %copy-done.6 = s32[3,16,32]{2,1,0:T(8,128)S(1)} copy-done((s32[3,16,32]{2,1,0:T(8,128)S(1)}, s32[3,16,32]{2,1,0:T(8,128)}, u32[]{:S(2)}) %copy-start.6) | copy-done | bytes 6168
  10.9 0.6 %lists.2.table = s32[38,50]{1,0:T(8,128)S(1)} custom-call(s32[6,32,32]{2,1,0:T(8,128)S(1)} %copy-done.4, s32[3,16,32]{2,1,0:T(8,128)S(1)} %copy-done.6, s32[4,70,50]{2,1,0:T(8,128)S(1)} %copy-done.3), custom_call_target="tpu_custom_call" | custom-call | tf_op jit(solution)/shard_map/lists/pallas_call | solution.py:502
  11.5 0.0 copy-done.1
  11.5 0.0 copy-done.5
  11.5 1.9 %block.1 = (f32[24,8,512]{2,1,0:T(8,128)S(1)}, f32[8,2048]{1,0:T(8,128)S(1)}) custom-call(s32[38,50]{1,0:T(8,128)S(1)} %lists.2.table, bf16[192,512]{1,0:T(8,128)(2,1)S(1)} %reshape.3.own.src, f32[4,2048]{1,0:T(4,128)S(1)} %copy-done.5, f32[40,2,512]{2,1,0:T(2,128)S(1)} %copy-done.1), custom_call_target="tpu_custom_call" | custom-call | tf_op jit(solution)/shard_map/block/pallas_call | solution.py:502
  13.4 0.0 copy-start
  13.4 0.0 collective-permute-done.1.second
  13.4 0.0 collective-permute-done.first
  13.4 1.9 %collective-permute-start.3 = (bf16[512,512]{1,0:T(8,128)(2,1)S(1)}, bf16[512,512]{1,0:T(8,128)(2,1)S(1)}, u32[]{:S(2)}, u32[]{:S(2)}) collective-permute-start(bf16[512,512]{1,0:T(8,128)(2,1)S(1)} %pack.1.strip), channel_id=1, source_target_pairs={{0,1},{1,0},{2,3},{3,2},{4,5},{5,4},{6,7},{7,6},{8,9},{9,8},{10,11... | collective-permute-start | bytes 1572872 | tf_op jit(solution)/shard_map/ppermute | solution.py:155
  15.3 2.6 %collective-permute-start.2 = (bf16[512,512]{1,0:T(8,128)(2,1)S(1)}, bf16[512,512]{1,0:T(8,128)(2,1)S(1)}, u32[]{:S(2)}, u32[]{:S(2)}) collective-permute-start(bf16[512,512]{1,0:T(8,128)(2,1)S(1)} %pack.1.strip), channel_id=1, source_target_pairs={{1,2},{2,1},{3,4},{4,3},{5,6},{6,5},{9,10},{10,9},{11,12},{12,11},... | collective-permute-start | bytes 1572872 | tf_op jit(solution)/shard_map/ppermute | solution.py:155
  17.9 0.0 collective-permute-done.5.refs_2_
  17.9 0.0 copy-done.2
  17.9 0.2 pad_maximum_fusion
  18.1 0.1 collective-permute-start.6
  18.1 0.0 collective-permute-done.3.side_a
  18.1 0.0 copy-done
  18.2 4.2 %both.1 = (f32[17,8,2048]{2,1,0:T(8,128)S(1)}, f32[24,8,512]{2,1,0:T(8,128)S(1)}, f32[17,8,2048]{2,1,0:T(8,128)S(1)}, f32[12,8,512]{2,1,0:T(8,128)S(1)}) custom-call(s32[38,50]{1,0:T(8,128)S(1)} %lists.2.table, bf16[512,512]{1,0:T(8,128)(2,1)S(1)} %pack.1.strip, bf16[512,512]{1,0:T(8,128)(2,1)S(1)} %collective-permute-done.3.side_a, ...), custom_call_target="tpu_custom_call" | custom-call | tf_op jit(solution)/shard_map/both/pallas_call | solution.py:502
  22.3 0.0 collective-permute-done.6.refs_3_
  22.3 2.2 %inner.1 = (f32[40,2,2048]{2,1,0:T(2,128)S(1)}, f32[6,8,2048]{2,1,0:T(8,128)S(1)}, f32[6,8,2048]{2,1,0:T(8,128)S(1)}) custom-call(s32[38,50]{1,0:T(8,128)S(1)} %lists.2.table, f32[17,8,2048]{2,1,0:T(8,128)S(1)} %get-tuple-element.16.pat_own, f32[17,8,2048]{2,1,0:T(8,128)S(1)} %get-tuple-element.17.pat_a, f32[1,40,2,256]{3,2,1,0:T(2,128)S(1)} %bitcast.4, ...), custom_call_target="tpu_custom_call" | custom-call | tf_op jit(solution)/shard_map/inner/pallas_call | solution.py:502
  24.5 1.2 %collective-permute-done.2.src = bf16[512,512]{1,0:T(8,128)(2,1)S(1)} collective-permute-done((bf16[512,512]{1,0:T(8,128)(2,1)S(1)}, bf16[512,512]{1,0:T(8,128)(2,1)S(1)}, u32[]{:S(2)}, u32[]{:S(2)}) %collective-permute-start.2) | collective-permute-done | bytes 524320 | tf_op jit(solution)/shard_map/ppermute | solution.py:155
  25.8 5.0 %last.1 = f32[6,4,2,4,512]{4,3,2,1,0:T(4,128)} custom-call(s32[38,50]{1,0:T(8,128)S(1)} %lists.2.table, bf16[512,512]{1,0:T(8,128)(2,1)S(1)} %collective-permute-done.2.src, bf16[512,2048]{1,0:T(8,128)(2,1)S(1)} %copy-done, f32[8,2048]{1,0:T(8,128)S(1)} %get-tuple-element.15.trig, f32[40,2,512]{2,1,0:T(2,128)S(1)} %copy-done.1, ...), custom_call_target="tpu_custom_call" | custom-call | tf_op jit(solution)/shard_map/last/pallas_call | solution.py:502
  (2 shorter events, 0.0 us)
Async XLA Ops:
  0.0 10.1 %copy-start.3 = (s32[4,70,50]{2,1,0:T(8,128)S(1)}, s32[4,70,50]{2,1,0:T(8,128)}, u32[]{:S(2)}) copy-start(s32[4,70,50]{2,1,0:T(8,128)} %constant.2.clone.lists) | copy-start | bytes 168004
  0.0 10.1 %copy-start.4 = (s32[6,32,32]{2,1,0:T(8,128)S(1)}, s32[6,32,32]{2,1,0:T(8,128)}, u32[]{:S(2)}) copy-start(s32[6,32,32]{2,1,0:T(8,128)} %fine_op.1) | copy-start | bytes 73732
  0.0 11.5 %copy-start.1 = (f32[40,2,512]{2,1,0:T(2,128)S(1)}, f32[40,2,512]{2,1,0:T(2,128)}, u32[]{:S(2)}) copy-start(f32[40,2,512]{2,1,0:T(2,128)} %fops.5) | copy-start | bytes 491524
  0.0 11.5 %copy-start.5 = (f32[4,2048]{1,0:T(4,128)S(1)}, f32[4,2048]{1,0:T(4,128)}, u32[]{:S(2)}) copy-start(f32[4,2048]{1,0:T(4,128)} %phase.1) | copy-start | bytes 98308
  0.0 7.8 %collective-permute-start.4 = (f32[1,40,2,256]{3,2,1,0:T(2,128)}, f32[1,40,2,256]{3,2,1,0:T(2,128)S(1)}, u32[]{:S(2)}, u32[]{:S(2)}) collective-permute-start(f32[1,40,2,256]{3,2,1,0:T(2,128)} %bitcast.1), channel_id=1, source_target_pairs={{0,4},{1,5},{2,6},{3,7},{4,0},{5,1},{6,2},{7,3},{8,12},{9,13},{10,... | collective-permute-start | bytes 245768 | tf_op jit(solution)/shard_map/ppermute | solution.py:528
  3.4 10.0 %collective-permute-start = (bf16[192,512]{1,0:T(8,128)(2,1)S(1)}, bf16[192,512]{1,0:T(8,128)(2,1)S(1)}, u32[]{:S(2)}, u32[]{:S(2)}) collective-permute-start(bf16[192,512]{1,0:T(8,128)(2,1)S(1)} %reshape.3.own.src), channel_id=1, source_target_pairs={{0,8},{8,0},{16,24},{24,16},{1,9},{9,1},{17,25},{25,17},{2,10},{10... | collective-permute-start | bytes 589832 | tf_op jit(solution)/shard_map/ppermute | solution.py:155
  3.7 9.7 %collective-permute-start.1 = (bf16[128,512]{1,0:T(8,128)(2,1)S(1)}, bf16[128,512]{1,0:T(8,128)(2,1)S(1)}, u32[]{:S(2)}, u32[]{:S(2)}) collective-permute-start(bf16[128,512]{1,0:T(8,128)(2,1)S(1)} %edge.1), channel_id=1, source_target_pairs={{8,16},{16,8},{9,17},{17,9},{10,18},{18,10},{11,19},{19,11},{12,20... | collective-permute-start | bytes 393224 | tf_op jit(solution)/shard_map/ppermute | solution.py:155
  8.8 9.1 %copy-start.2 = (f32[40,2,256]{2,1,0:T(2,128)S(1)}, f32[40,2,256]{2,1,0:T(2,128)}, u32[]{:S(2)}) copy-start(f32[40,2,256]{2,1,0:T(2,128)} %param.14) | copy-start | bytes 245764
  8.8 9.1 %collective-permute-start.5 = (f32[2,40,2,256]{3,2,1,0:T(2,128)S(1)}, f32[2,40,2,256]{3,2,1,0:T(2,128)S(1)}, u32[]{:S(2)}, u32[]{:S(2)}) collective-permute-start(f32[2,40,2,256]{3,2,1,0:T(2,128)S(1)} %pad_maximum_fusion.1), channel_id=1, source_target_pairs={{0,2},{1,3},{2,0},{3,1},{4,6},{5,7},{6,4},{7,5},{8,10},{9,11},{10,... | collective-permute-start | bytes 491528 | tf_op jit(solution)/shard_map/ppermute | solution.py:528
  10.2 0.7 %copy-start.6 = (s32[3,16,32]{2,1,0:T(8,128)S(1)}, s32[3,16,32]{2,1,0:T(8,128)}, u32[]{:S(2)}) copy-start(s32[3,16,32]{2,1,0:T(8,128)} %par_op.1) | copy-start | bytes 18436
  13.4 4.8 %copy-start = (bf16[512,2048]{1,0:T(8,128)(2,1)S(1)}, bf16[512,2048]{1,0:T(8,128)(2,1)}, u32[]{:S(2)}) copy-start(bf16[512,2048]{1,0:T(8,128)(2,1)} %interp.3) | copy-start | bytes 6291460
  13.4 4.7 %collective-permute-start.3 = (bf16[512,512]{1,0:T(8,128)(2,1)S(1)}, bf16[512,512]{1,0:T(8,128)(2,1)S(1)}, u32[]{:S(2)}, u32[]{:S(2)}) collective-permute-start(bf16[512,512]{1,0:T(8,128)(2,1)S(1)} %pack.1.strip), channel_id=1, source_target_pairs={{0,1},{1,0},{2,3},{3,2},{4,5},{5,4},{6,7},{7,6},{8,9},{9,8},{10,11... | collective-permute-start | bytes 1572872 | tf_op jit(solution)/shard_map/ppermute | solution.py:155
  15.3 10.5 %collective-permute-start.2 = (bf16[512,512]{1,0:T(8,128)(2,1)S(1)}, bf16[512,512]{1,0:T(8,128)(2,1)S(1)}, u32[]{:S(2)}, u32[]{:S(2)}) collective-permute-start(bf16[512,512]{1,0:T(8,128)(2,1)S(1)} %pack.1.strip), channel_id=1, source_target_pairs={{1,2},{2,1},{3,4},{4,3},{5,6},{6,5},{9,10},{10,9},{11,12},{12,11},... | collective-permute-start | bytes 1572872 | tf_op jit(solution)/shard_map/ppermute | solution.py:155
  18.1 4.3 %collective-permute-start.6 = (f32[4,40,2,256]{3,2,1,0:T(2,128)S(1)}, f32[4,40,2,256]{3,2,1,0:T(2,128)S(1)}, u32[]{:S(2)}, u32[]{:S(2)}) collective-permute-start(f32[4,40,2,256]{3,2,1,0:T(2,128)S(1)} %pad_maximum_fusion), channel_id=1, source_target_pairs={{0,1},{1,0},{2,3},{3,2},{4,5},{5,4},{6,7},{7,6},{8,9},{9,8},{10,11... | collective-permute-start | bytes 983048 | tf_op jit(solution)/shard_map/ppermute | solution.py:528

commit v5 on v4

--- a/solution.py
+++ b/solution.py
@@ -9,6 +9,7 @@
 from jax.sharding import PartitionSpec as P
 
 CHUNK = 512
+COSTS = {"hold2": 0.5, "hold3": 0.5, "edge": 0.5}
 PIECE = 256
 LIMITS = {"block": 8, "pack": 4, "edge": 4, "lists": 4, "both": 20, "inner": 12, "last": 24}
 F32, BF16 = jnp.float32, jnp.bfloat16
@@ -283,6 +284,14 @@
                 near[box] = value
 
 
+def hold_kernel(rows, cols, sides, *refs):
+    *shards, out = refs
+    at = 0
+    for ref in shards:
+        out[at : at + ref.shape[0]] = ref[...]
+        at += ref.shape[0]
+
+
 def lists_kernel(rows, cols, sides, fine_op, par_op, lists, table):
     which = parities()
     at, boxes = 0, 5 * rows * cols
@@ -505,7 +514,8 @@
             in_specs=[smem] * n_smem + [vmem] * (len(args) - n_smem),
             out_specs=[vmem] * len(outs),
             scratch_shapes=scratches,
-            compiler_params=pltpu.CompilerParams(vmem_limit_bytes=LIMITS[name] << 20),
+            compiler_params=pltpu.CompilerParams(vmem_limit_bytes=LIMITS.get(name, 4) << 20),
+            cost_estimate=pl.CostEstimate(flops=int(COSTS.get(name, 0) * 10**9), bytes_accessed=0, transcendentals=0),
             name=name,
         )(*args)
 
@@ -524,7 +534,10 @@
     patch_halo = exchange([own, edge], "patch")
     shards = [parent_ops[None]]
     for bit in reversed(range(bits)):
-        held = jnp.concatenate(shards, axis=0)
+        held = shards[0]
+        if len(shards) > 1:
+            count = sum(part.shape[0] for part in shards)
+            held = call(hold_kernel, "hold%d" % len(shards), 0, [shape(count, *parent_ops.shape)], [], *shards)[0]
         shards.append(lax.ppermute(held, "dir", [(i, i ^ (1 << bit)) for i in range(n_dir)]))
     near_block, trig = call(
         block_kernel, "block", 1, [near, shape(8, pdirs)], [scratch(frows * fcols + 1, comps, fdirs)],

time: 31 us -> 30.1 us (0.971)
  the two profiles are of different devices: /device:TPU:3 before, /device:TPU:1 now
where the time goes in v5:
time: 30.1 us; the launch traced here: 30 us
  Pallas kernels  14.1 us (47%)
  starting transfers between devices  12.6 us (42%)
  waiting for transfers between devices  2.09 us (7%)
  local copies, waits for them, and re-layouts  1.05 us (3%)
    pallas_call x9, Pallas kernels, call(): pl.pallas_call(functools.partial(body, rows, cols, sides), out_shape=outs...  14.1 us
    ppermute x4, starting transfers between devices, exchange(): lax.ppermute(block, axis, pairs(n, first))  7.52 us
    ppermute x3, starting transfers between devices, per_device(): lax.ppermute(held, 'dir', [(i, i ^ 1 << bit) for i in range(n_dir)])  5.04 us
    ppermute x3, waiting for transfers between devices, per_device(): lax.ppermute(held, 'dir', [(i, i ^ 1 << bit) for i in range(n_dir)])  1.21 us
    reshape x1, local copies, waits for them, and re-layouts, per_device(): own = fine_out.reshape(frows * fcols * comps, fdirs)  1.01 us
    ppermute x4, waiting for transfers between devices, exchange(): lax.ppermute(block, axis, pairs(n, first))  0.88 us
  transfers between devices with their start and end apart: 7, of which 2 were waited for; matrix products, arithmetic and copies ran while one was open for 0% of the time, Pallas kernels for 30%

profile of v5, /device:TPU:1, one launch (start us, length us, event | category | flops | bytes accessed | tf_op | source)
XLA Modules:
  0.0 30.0 jit_solution(1664340394554465949)
XLA Ops:
  0.0 0.0 copy-start.4
  0.0 1.0 %reshape.3.own.src = bf16[192,512]{1,0:T(8,128)(2,1)S(1)} reshape(bf16[6,4,2,4,512]{4,3,2,1,0:T(4,128)(2,1)} %param.10) | data formatting | bytes 393216 | tf_op jit(solution)/shard_map/reshape | solution.py:488
  1.0 2.1 %collective-permute-start = (bf16[192,512]{1,0:T(8,128)(2,1)S(1)}, bf16[192,512]{1,0:T(8,128)(2,1)S(1)}, u32[]{:S(2)}, u32[]{:S(2)}) collective-permute-start(bf16[192,512]{1,0:T(8,128)(2,1)S(1)} %reshape.3.own.src), channel_id=1, source_target_pairs={{0,8},{8,0},{16,24},{24,16},{1,9},{9,1},{17,25},{25,17},{2,10},{10... | collective-permute-start | bytes 589832 | tf_op jit(solution)/shard_map/ppermute | solution.py:156
  3.1 2.3 %collective-permute-start.4 = (f32[1,40,2,256]{3,2,1,0:T(2,128)}, f32[1,40,2,256]{3,2,1,0:T(2,128)S(1)}, u32[]{:S(2)}, u32[]{:S(2)}) collective-permute-start(f32[1,40,2,256]{3,2,1,0:T(2,128)} %bitcast.1), channel_id=1, source_target_pairs={{0,4},{1,5},{2,6},{3,7},{4,0},{5,1},{6,2},{7,3},{8,12},{9,13},{10,... | collective-permute-start | bytes 245768 | tf_op jit(solution)/shard_map/ppermute | solution.py:541
  5.4 0.0 copy-start.2
  5.5 0.0 copy-start.3
  5.5 0.0 copy-start.6
  5.5 0.0 copy-start.1
  5.5 0.0 copy-start.5
  5.5 0.8 %collective-permute-start.1 = (bf16[128,512]{1,0:T(8,128)(2,1)S(1)}, bf16[128,512]{1,0:T(8,128)(2,1)S(1)}, u32[]{:S(2)}, u32[]{:S(2)}) collective-permute-start(bf16[128,512]{1,0:T(8,128)(2,1)S(1)} %edge.1), channel_id=1, source_target_pairs={{8,16},{16,8},{9,17},{17,9},{10,18},{18,10},{11,19},{19,11},{12,20... | collective-permute-start | bytes 393224 | tf_op jit(solution)/shard_map/ppermute | solution.py:156
  6.3 1.2 %collective-permute-done.4.refs_1_ = f32[1,40,2,256]{3,2,1,0:T(2,128)S(1)} collective-permute-done((f32[1,40,2,256]{3,2,1,0:T(2,128)}, f32[1,40,2,256]{3,2,1,0:T(2,128)S(1)}, u32[]{:S(2)}, u32[]{:S(2)}) %collective-permute-start.4) | collective-permute-done | bytes 81952 | tf_op jit(solution)/shard_map/ppermute | solution.py:541
  7.5 0.0 copy-done.4
  7.5 2.7 %collective-permute-start.5 = (f32[2,40,2,256]{3,2,1,0:T(2,128)S(1)}, f32[2,40,2,256]{3,2,1,0:T(2,128)S(1)}, u32[]{:S(2)}, u32[]{:S(2)}) collective-permute-start(f32[2,40,2,256]{3,2,1,0:T(2,128)S(1)} %hold2.1), channel_id=1, source_target_pairs={{0,2},{1,3},{2,0},{3,1},{4,6},{5,7},{6,4},{7,5},{8,10},{9,11},{10,... | collective-permute-start | bytes 491528 | tf_op jit(solution)/shard_map/ppermute | solution.py:541
  10.2 0.0 copy-done.2
  10.2 0.0 copy-done.3
  10.2 0.0 copy-done.6
  10.2 0.6 %lists.2.table = s32[38,50]{1,0:T(8,128)S(1)} custom-call(s32[6,32,32]{2,1,0:T(8,128)S(1)} %copy-done.3, s32[3,16,32]{2,1,0:T(8,128)S(1)} %copy-done.6, s32[4,70,50]{2,1,0:T(8,128)S(1)} %copy-done.2), custom_call_target="tpu_custom_call" | custom-call | tf_op jit(solution)/shard_map/lists/pallas_call | solution.py:511
  10.8 0.0 copy-done.1
  10.8 0.0 copy-done.5
  10.8 2.0 %block.1 = (f32[24,8,512]{2,1,0:T(8,128)S(1)}, f32[8,2048]{1,0:T(8,128)S(1)}) custom-call(s32[38,50]{1,0:T(8,128)S(1)} %lists.2.table, bf16[192,512]{1,0:T(8,128)(2,1)S(1)} %reshape.3.own.src, f32[4,2048]{1,0:T(4,128)S(1)} %copy-done.5, f32[40,2,512]{2,1,0:T(2,128)S(1)} %copy-done.1), custom_call_target="tpu_custom_call" | custom-call | tf_op jit(solution)/shard_map/block/pallas_call | solution.py:511
  12.8 0.0 collective-permute-done.1.second
  12.8 0.0 collective-permute-done.first
  12.8 0.0 copy-start
  12.9 1.6 %collective-permute-start.3 = (bf16[512,512]{1,0:T(8,128)(2,1)S(1)}, bf16[512,512]{1,0:T(8,128)(2,1)S(1)}, u32[]{:S(2)}, u32[]{:S(2)}) collective-permute-start(bf16[512,512]{1,0:T(8,128)(2,1)S(1)} %pack.1.strip), channel_id=1, source_target_pairs={{0,1},{1,0},{2,3},{3,2},{4,5},{5,4},{6,7},{7,6},{8,9},{9,8},{10,11... | collective-permute-start | bytes 1572872 | tf_op jit(solution)/shard_map/ppermute | solution.py:156
  14.4 3.0 %collective-permute-start.2 = (bf16[512,512]{1,0:T(8,128)(2,1)S(1)}, bf16[512,512]{1,0:T(8,128)(2,1)S(1)}, u32[]{:S(2)}, u32[]{:S(2)}) collective-permute-start(bf16[512,512]{1,0:T(8,128)(2,1)S(1)} %pack.1.strip), channel_id=1, source_target_pairs={{1,2},{2,1},{3,4},{4,3},{5,6},{6,5},{9,10},{10,9},{11,12},{12,11},... | collective-permute-start | bytes 1572872 | tf_op jit(solution)/shard_map/ppermute | solution.py:156
  17.5 0.0 collective-permute-done.5.refs_2_
  17.5 0.1 collective-permute-start.6
  17.6 0.0 collective-permute-done.3.side_a
  17.6 0.0 copy-done
  17.6 4.2 %both.1 = (f32[17,8,2048]{2,1,0:T(8,128)S(1)}, f32[24,8,512]{2,1,0:T(8,128)S(1)}, f32[17,8,2048]{2,1,0:T(8,128)S(1)}, f32[12,8,512]{2,1,0:T(8,128)S(1)}) custom-call(s32[38,50]{1,0:T(8,128)S(1)} %lists.2.table, bf16[512,512]{1,0:T(8,128)(2,1)S(1)} %pack.1.strip, bf16[512,512]{1,0:T(8,128)(2,1)S(1)} %collective-permute-done.3.side_a, ...), custom_call_target="tpu_custom_call" | custom-call | tf_op jit(solution)/shard_map/both/pallas_call | solution.py:511
  21.8 0.0 collective-permute-done.6.refs_3_
  21.8 2.2 %inner.1 = (f32[40,2,2048]{2,1,0:T(2,128)S(1)}, f32[6,8,2048]{2,1,0:T(8,128)S(1)}, f32[6,8,2048]{2,1,0:T(8,128)S(1)}) custom-call(s32[38,50]{1,0:T(8,128)S(1)} %lists.2.table, f32[17,8,2048]{2,1,0:T(8,128)S(1)} %get-tuple-element.16.pat_own, f32[17,8,2048]{2,1,0:T(8,128)S(1)} %get-tuple-element.17.pat_a, f32[1,40,2,256]{3,2,1,0:T(2,128)S(1)} %bitcast.4, ...), custom_call_target="tpu_custom_call" | custom-call | tf_op jit(solution)/shard_map/inner/pallas_call | solution.py:511
  24.1 0.9 %collective-permute-done.2.src = bf16[512,512]{1,0:T(8,128)(2,1)S(1)} collective-permute-done((bf16[512,512]{1,0:T(8,128)(2,1)S(1)}, bf16[512,512]{1,0:T(8,128)(2,1)S(1)}, u32[]{:S(2)}, u32[]{:S(2)}) %collective-permute-start.2) | collective-permute-done | bytes 524320 | tf_op jit(solution)/shard_map/ppermute | solution.py:156
  24.9 5.0 %last.1 = f32[6,4,2,4,512]{4,3,2,1,0:T(4,128)} custom-call(s32[38,50]{1,0:T(8,128)S(1)} %lists.2.table, bf16[512,512]{1,0:T(8,128)(2,1)S(1)} %collective-permute-done.2.src, bf16[512,2048]{1,0:T(8,128)(2,1)S(1)} %copy-done, f32[8,2048]{1,0:T(8,128)S(1)} %get-tuple-element.15.trig, f32[40,2,512]{2,1,0:T(2,128)S(1)} %copy-done.1, ...), custom_call_target="tpu_custom_call" | custom-call | tf_op jit(solution)/shard_map/last/pallas_call | solution.py:511
  (4 shorter events, 0.1 us)
Async XLA Ops:
  0.0 7.5 %copy-start.4 = (f32[40,2,256]{2,1,0:T(2,128)S(1)}, f32[40,2,256]{2,1,0:T(2,128)}, u32[]{:S(2)}) copy-start(f32[40,2,256]{2,1,0:T(2,128)} %param.14) | copy-start | bytes 245764
  1.0 11.8 %collective-permute-start = (bf16[192,512]{1,0:T(8,128)(2,1)S(1)}, bf16[192,512]{1,0:T(8,128)(2,1)S(1)}, u32[]{:S(2)}, u32[]{:S(2)}) collective-permute-start(bf16[192,512]{1,0:T(8,128)(2,1)S(1)} %reshape.3.own.src), channel_id=1, source_target_pairs={{0,8},{8,0},{16,24},{24,16},{1,9},{9,1},{17,25},{25,17},{2,10},{10... | collective-permute-start | bytes 589832 | tf_op jit(solution)/shard_map/ppermute | solution.py:156
  3.1 4.4 %collective-permute-start.4 = (f32[1,40,2,256]{3,2,1,0:T(2,128)}, f32[1,40,2,256]{3,2,1,0:T(2,128)S(1)}, u32[]{:S(2)}, u32[]{:S(2)}) collective-permute-start(f32[1,40,2,256]{3,2,1,0:T(2,128)} %bitcast.1), channel_id=1, source_target_pairs={{0,4},{1,5},{2,6},{3,7},{4,0},{5,1},{6,2},{7,3},{8,12},{9,13},{10,... | collective-permute-start | bytes 245768 | tf_op jit(solution)/shard_map/ppermute | solution.py:541
  5.4 4.8 %copy-start.2 = (s32[4,70,50]{2,1,0:T(8,128)S(1)}, s32[4,70,50]{2,1,0:T(8,128)}, u32[]{:S(2)}) copy-start(s32[4,70,50]{2,1,0:T(8,128)} %constant.2.clone.lists) | copy-start | bytes 168004
  5.5 4.7 %copy-start.3 = (s32[6,32,32]{2,1,0:T(8,128)S(1)}, s32[6,32,32]{2,1,0:T(8,128)}, u32[]{:S(2)}) copy-start(s32[6,32,32]{2,1,0:T(8,128)} %fine_op.1) | copy-start | bytes 73732
  5.5 4.7 %copy-start.6 = (s32[3,16,32]{2,1,0:T(8,128)S(1)}, s32[3,16,32]{2,1,0:T(8,128)}, u32[]{:S(2)}) copy-start(s32[3,16,32]{2,1,0:T(8,128)} %par_op.1) | copy-start | bytes 18436
  5.5 5.3 %copy-start.1 = (f32[40,2,512]{2,1,0:T(2,128)S(1)}, f32[40,2,512]{2,1,0:T(2,128)}, u32[]{:S(2)}) copy-start(f32[40,2,512]{2,1,0:T(2,128)} %fops.5) | copy-start | bytes 491524
  5.5 5.3 %copy-start.5 = (f32[4,2048]{1,0:T(4,128)S(1)}, f32[4,2048]{1,0:T(4,128)}, u32[]{:S(2)}) copy-start(f32[4,2048]{1,0:T(4,128)} %phase.1) | copy-start | bytes 98308
  5.5 7.3 %collective-permute-start.1 = (bf16[128,512]{1,0:T(8,128)(2,1)S(1)}, bf16[128,512]{1,0:T(8,128)(2,1)S(1)}, u32[]{:S(2)}, u32[]{:S(2)}) collective-permute-start(bf16[128,512]{1,0:T(8,128)(2,1)S(1)} %edge.1), channel_id=1, source_target_pairs={{8,16},{16,8},{9,17},{17,9},{10,18},{18,10},{11,19},{19,11},{12,20... | collective-permute-start | bytes 393224 | tf_op jit(solution)/shard_map/ppermute | solution.py:156
  7.5 9.9 %collective-permute-start.5 = (f32[2,40,2,256]{3,2,1,0:T(2,128)S(1)}, f32[2,40,2,256]{3,2,1,0:T(2,128)S(1)}, u32[]{:S(2)}, u32[]{:S(2)}) collective-permute-start(f32[2,40,2,256]{3,2,1,0:T(2,128)S(1)} %hold2.1), channel_id=1, source_target_pairs={{0,2},{1,3},{2,0},{3,1},{4,6},{5,7},{6,4},{7,5},{8,10},{9,11},{10,... | collective-permute-start | bytes 491528 | tf_op jit(solution)/shard_map/ppermute | solution.py:541
  12.8 4.8 %copy-start = (bf16[512,2048]{1,0:T(8,128)(2,1)S(1)}, bf16[512,2048]{1,0:T(8,128)(2,1)}, u32[]{:S(2)}) copy-start(bf16[512,2048]{1,0:T(8,128)(2,1)} %interp.3) | copy-start | bytes 6291460
  12.9 4.7 %collective-permute-start.3 = (bf16[512,512]{1,0:T(8,128)(2,1)S(1)}, bf16[512,512]{1,0:T(8,128)(2,1)S(1)}, u32[]{:S(2)}, u32[]{:S(2)}) collective-permute-start(bf16[512,512]{1,0:T(8,128)(2,1)S(1)} %pack.1.strip), channel_id=1, source_target_pairs={{0,1},{1,0},{2,3},{3,2},{4,5},{5,4},{6,7},{7,6},{8,9},{9,8},{10,11... | collective-permute-start | bytes 1572872 | tf_op jit(solution)/shard_map/ppermute | solution.py:156
  14.4 10.5 %collective-permute-start.2 = (bf16[512,512]{1,0:T(8,128)(2,1)S(1)}, bf16[512,512]{1,0:T(8,128)(2,1)S(1)}, u32[]{:S(2)}, u32[]{:S(2)}) collective-permute-start(bf16[512,512]{1,0:T(8,128)(2,1)S(1)} %pack.1.strip), channel_id=1, source_target_pairs={{1,2},{2,1},{3,4},{4,3},{5,6},{6,5},{9,10},{10,9},{11,12},{12,11},... | collective-permute-start | bytes 1572872 | tf_op jit(solution)/shard_map/ppermute | solution.py:156
  17.5 4.3 %collective-permute-start.6 = (f32[4,40,2,256]{3,2,1,0:T(2,128)S(1)}, f32[4,40,2,256]{3,2,1,0:T(2,128)S(1)}, u32[]{:S(2)}, u32[]{:S(2)}) collective-permute-start(f32[4,40,2,256]{3,2,1,0:T(2,128)S(1)} %hold3.1), channel_id=1, source_target_pairs={{0,1},{1,0},{2,3},{3,2},{4,5},{5,4},{6,7},{7,6},{8,9},{9,8},{10,11... | collective-permute-start | bytes 983048 | tf_op jit(solution)/shard_map/ppermute | solution.py:541

commit v6 on v5

--- a/solution.py
+++ b/solution.py
@@ -11,6 +11,7 @@
 CHUNK = 512
 COSTS = {"hold2": 0.5, "hold3": 0.5, "edge": 0.5}
 PIECE = 256
+TILE = 8
 LIMITS = {"block": 8, "pack": 4, "edge": 4, "lists": 4, "both": 20, "inner": 12, "last": 24}
 F32, BF16 = jnp.float32, jnp.bfloat16
 
@@ -298,9 +299,14 @@
     table[boxes:] = lists[which, 2 * boxes + 2 :]
     for op, scale, none in ((fine_op, 2, 2 * boxes), (par_op, 1, 2 * boxes + 1)):
         across = cols * scale
-        first = pl.multiple_of(lax.axis_index("dir") * across, across)
+        assert TILE % across == 0 and op.shape[1] % TILE == 0
+        place = lax.axis_index("dir") * across
+        first = pl.multiple_of(place // TILE * TILE, TILE)
         for r in range(rows * scale):
-            mine = op[r, pl.ds(first, across), :]
+            tile = op[r, pl.ds(first, TILE), :]
+            mine = tile[:across]
+            for skip in range(across, TILE, across):
+                mine = jnp.where(lax.rem(place, TILE) == skip, tile[skip : skip + across], mine)
             wanted = lists[which, boxes + at : boxes + at + across]
             found = mine[:, 0:1] == wanted
             for slot in range(1, op.shape[2]):

time: 30.1 us -> 30.1 us (level)
  no operation moved by 1% of the time
where the time goes in v6:
time: 30.1 us; the launch traced here: 30 us
  Pallas kernels  14.1 us (47%)
  starting transfers between devices  12.6 us (42%)
  waiting for transfers between devices  2.09 us (7%)
  local copies, waits for them, and re-layouts  1.05 us (3%)
    pallas_call x9, Pallas kernels, call(): pl.pallas_call(functools.partial(body, rows, cols, sides), out_shape=outs...  14.1 us
    ppermute x4, starting transfers between devices, exchange(): lax.ppermute(block, axis, pairs(n, first))  7.52 us
    ppermute x3, starting transfers between devices, per_device(): lax.ppermute(held, 'dir', [(i, i ^ 1 << bit) for i in range(n_dir)])  5.04 us
    ppermute x3, waiting for transfers between devices, per_device(): lax.ppermute(held, 'dir', [(i, i ^ 1 << bit) for i in range(n_dir)])  1.21 us
    reshape x1, local copies, waits for them, and re-layouts, per_device(): own = fine_out.reshape(frows * fcols * comps, fdirs)  1.01 us
    ppermute x4, waiting for transfers between devices, exchange(): lax.ppermute(block, axis, pairs(n, first))  0.88 us
  transfers between devices with their start and end apart: 7, of which 2 were waited for; matrix products, arithmetic and copies ran while one was open for 0% of the time, Pallas kernels for 30%

profile of v6, /device:TPU:1, one launch (start us, length us, event | category | flops | bytes accessed | tf_op | source)
XLA Modules:
  0.0 30.0 jit_solution(18174266335656531261)
XLA Ops:
  0.0 0.0 copy-start.4
  0.0 1.0 %reshape.3.own.src = bf16[192,512]{1,0:T(8,128)(2,1)S(1)} reshape(bf16[6,4,2,4,512]{4,3,2,1,0:T(4,128)(2,1)} %param.10) | data formatting | bytes 393216 | tf_op jit(solution)/shard_map/reshape | solution.py:494
  1.0 2.1 %collective-permute-start = (bf16[192,512]{1,0:T(8,128)(2,1)S(1)}, bf16[192,512]{1,0:T(8,128)(2,1)S(1)}, u32[]{:S(2)}, u32[]{:S(2)}) collective-permute-start(bf16[192,512]{1,0:T(8,128)(2,1)S(1)} %reshape.3.own.src), channel_id=1, source_target_pairs={{0,8},{8,0},{16,24},{24,16},{1,9},{9,1},{17,25},{25,17},{2,10},{10... | collective-permute-start | bytes 589832 | tf_op jit(solution)/shard_map/ppermute | solution.py:157
  3.1 2.3 %collective-permute-start.4 = (f32[1,40,2,256]{3,2,1,0:T(2,128)}, f32[1,40,2,256]{3,2,1,0:T(2,128)S(1)}, u32[]{:S(2)}, u32[]{:S(2)}) collective-permute-start(f32[1,40,2,256]{3,2,1,0:T(2,128)} %bitcast.1), channel_id=1, source_target_pairs={{0,4},{1,5},{2,6},{3,7},{4,0},{5,1},{6,2},{7,3},{8,12},{9,13},{10,... | collective-permute-start | bytes 245768 | tf_op jit(solution)/shard_map/ppermute | solution.py:547
  5.4 0.0 copy-start.2
  5.5 0.0 copy-start.3
  5.5 0.0 copy-start.6
  5.5 0.0 copy-start.1
  5.5 0.0 copy-start.5
  5.5 0.8 %collective-permute-start.1 = (bf16[128,512]{1,0:T(8,128)(2,1)S(1)}, bf16[128,512]{1,0:T(8,128)(2,1)S(1)}, u32[]{:S(2)}, u32[]{:S(2)}) collective-permute-start(bf16[128,512]{1,0:T(8,128)(2,1)S(1)} %edge.1), channel_id=1, source_target_pairs={{8,16},{16,8},{9,17},{17,9},{10,18},{18,10},{11,19},{19,11},{12,20... | collective-permute-start | bytes 393224 | tf_op jit(solution)/shard_map/ppermute | solution.py:157
  6.3 1.2 %collective-permute-done.4.refs_1_ = f32[1,40,2,256]{3,2,1,0:T(2,128)S(1)} collective-permute-done((f32[1,40,2,256]{3,2,1,0:T(2,128)}, f32[1,40,2,256]{3,2,1,0:T(2,128)S(1)}, u32[]{:S(2)}, u32[]{:S(2)}) %collective-permute-start.4) | collective-permute-done | bytes 81952 | tf_op jit(solution)/shard_map/ppermute | solution.py:547
  7.5 0.0 copy-done.4
  7.5 2.7 %collective-permute-start.5 = (f32[2,40,2,256]{3,2,1,0:T(2,128)S(1)}, f32[2,40,2,256]{3,2,1,0:T(2,128)S(1)}, u32[]{:S(2)}, u32[]{:S(2)}) collective-permute-start(f32[2,40,2,256]{3,2,1,0:T(2,128)S(1)} %hold2.1), channel_id=1, source_target_pairs={{0,2},{1,3},{2,0},{3,1},{4,6},{5,7},{6,4},{7,5},{8,10},{9,11},{10,... | collective-permute-start | bytes 491528 | tf_op jit(solution)/shard_map/ppermute | solution.py:547
  10.2 0.0 copy-done.2
  10.2 0.0 copy-done.3
  10.2 0.0 copy-done.6
  10.2 0.6 %lists.2.table = s32[38,50]{1,0:T(8,128)S(1)} custom-call(s32[6,32,32]{2,1,0:T(8,128)S(1)} %copy-done.3, s32[3,16,32]{2,1,0:T(8,128)S(1)} %copy-done.6, s32[4,70,50]{2,1,0:T(8,128)S(1)} %copy-done.2), custom_call_target="tpu_custom_call" | custom-call | tf_op jit(solution)/shard_map/lists/pallas_call | solution.py:517
  10.8 0.0 copy-done.1
  10.8 0.0 copy-done.5
  10.8 2.0 %block.1 = (f32[24,8,512]{2,1,0:T(8,128)S(1)}, f32[8,2048]{1,0:T(8,128)S(1)}) custom-call(s32[38,50]{1,0:T(8,128)S(1)} %lists.2.table, bf16[192,512]{1,0:T(8,128)(2,1)S(1)} %reshape.3.own.src, f32[4,2048]{1,0:T(4,128)S(1)} %copy-done.5, f32[40,2,512]{2,1,0:T(2,128)S(1)} %copy-done.1), custom_call_target="tpu_custom_call" | custom-call | tf_op jit(solution)/shard_map/block/pallas_call | solution.py:517
  12.8 0.0 collective-permute-done.1.second
  12.8 0.0 collective-permute-done.first
  12.8 0.0 copy-start
  12.9 1.6 %collective-permute-start.3 = (bf16[512,512]{1,0:T(8,128)(2,1)S(1)}, bf16[512,512]{1,0:T(8,128)(2,1)S(1)}, u32[]{:S(2)}, u32[]{:S(2)}) collective-permute-start(bf16[512,512]{1,0:T(8,128)(2,1)S(1)} %pack.1.strip), channel_id=1, source_target_pairs={{0,1},{1,0},{2,3},{3,2},{4,5},{5,4},{6,7},{7,6},{8,9},{9,8},{10,11... | collective-permute-start | bytes 1572872 | tf_op jit(solution)/shard_map/ppermute | solution.py:157
  14.4 3.0 %collective-permute-start.2 = (bf16[512,512]{1,0:T(8,128)(2,1)S(1)}, bf16[512,512]{1,0:T(8,128)(2,1)S(1)}, u32[]{:S(2)}, u32[]{:S(2)}) collective-permute-start(bf16[512,512]{1,0:T(8,128)(2,1)S(1)} %pack.1.strip), channel_id=1, source_target_pairs={{1,2},{2,1},{3,4},{4,3},{5,6},{6,5},{9,10},{10,9},{11,12},{12,11},... | collective-permute-start | bytes 1572872 | tf_op jit(solution)/shard_map/ppermute | solution.py:157
  17.5 0.0 collective-permute-done.5.refs_2_
  17.5 0.1 collective-permute-start.6
  17.6 0.0 collective-permute-done.3.side_a
  17.6 0.0 copy-done
  17.6 4.2 %both.1 = (f32[17,8,2048]{2,1,0:T(8,128)S(1)}, f32[24,8,512]{2,1,0:T(8,128)S(1)}, f32[17,8,2048]{2,1,0:T(8,128)S(1)}, f32[12,8,512]{2,1,0:T(8,128)S(1)}) custom-call(s32[38,50]{1,0:T(8,128)S(1)} %lists.2.table, bf16[512,512]{1,0:T(8,128)(2,1)S(1)} %pack.1.strip, bf16[512,512]{1,0:T(8,128)(2,1)S(1)} %collective-permute-done.3.side_a, ...), custom_call_target="tpu_custom_call" | custom-call | tf_op jit(solution)/shard_map/both/pallas_call | solution.py:517
  21.8 0.0 collective-permute-done.6.refs_3_
  21.9 2.2 %inner.1 = (f32[40,2,2048]{2,1,0:T(2,128)S(1)}, f32[6,8,2048]{2,1,0:T(8,128)S(1)}, f32[6,8,2048]{2,1,0:T(8,128)S(1)}) custom-call(s32[38,50]{1,0:T(8,128)S(1)} %lists.2.table, f32[17,8,2048]{2,1,0:T(8,128)S(1)} %get-tuple-element.16.pat_own, f32[17,8,2048]{2,1,0:T(8,128)S(1)} %get-tuple-element.17.pat_a, f32[1,40,2,256]{3,2,1,0:T(2,128)S(1)} %bitcast.4, ...), custom_call_target="tpu_custom_call" | custom-call | tf_op jit(solution)/shard_map/inner/pallas_call | solution.py:517
  24.1 0.9 %collective-permute-done.2.src = bf16[512,512]{1,0:T(8,128)(2,1)S(1)} collective-permute-done((bf16[512,512]{1,0:T(8,128)(2,1)S(1)}, bf16[512,512]{1,0:T(8,128)(2,1)S(1)}, u32[]{:S(2)}, u32[]{:S(2)}) %collective-permute-start.2) | collective-permute-done | bytes 524320 | tf_op jit(solution)/shard_map/ppermute | solution.py:157
  24.9 5.0 %last.1 = f32[6,4,2,4,512]{4,3,2,1,0:T(4,128)} custom-call(s32[38,50]{1,0:T(8,128)S(1)} %lists.2.table, bf16[512,512]{1,0:T(8,128)(2,1)S(1)} %collective-permute-done.2.src, bf16[512,2048]{1,0:T(8,128)(2,1)S(1)} %copy-done, f32[8,2048]{1,0:T(8,128)S(1)} %get-tuple-element.15.trig, f32[40,2,512]{2,1,0:T(2,128)S(1)} %copy-done.1, ...), custom_call_target="tpu_custom_call" | custom-call | tf_op jit(solution)/shard_map/last/pallas_call | solution.py:517
  (4 shorter events, 0.1 us)
Async XLA Ops:
  0.0 7.5 %copy-start.4 = (f32[40,2,256]{2,1,0:T(2,128)S(1)}, f32[40,2,256]{2,1,0:T(2,128)}, u32[]{:S(2)}) copy-start(f32[40,2,256]{2,1,0:T(2,128)} %param.14) | copy-start | bytes 245764
  1.0 11.8 %collective-permute-start = (bf16[192,512]{1,0:T(8,128)(2,1)S(1)}, bf16[192,512]{1,0:T(8,128)(2,1)S(1)}, u32[]{:S(2)}, u32[]{:S(2)}) collective-permute-start(bf16[192,512]{1,0:T(8,128)(2,1)S(1)} %reshape.3.own.src), channel_id=1, source_target_pairs={{0,8},{8,0},{16,24},{24,16},{1,9},{9,1},{17,25},{25,17},{2,10},{10... | collective-permute-start | bytes 589832 | tf_op jit(solution)/shard_map/ppermute | solution.py:157
  3.1 4.4 %collective-permute-start.4 = (f32[1,40,2,256]{3,2,1,0:T(2,128)}, f32[1,40,2,256]{3,2,1,0:T(2,128)S(1)}, u32[]{:S(2)}, u32[]{:S(2)}) collective-permute-start(f32[1,40,2,256]{3,2,1,0:T(2,128)} %bitcast.1), channel_id=1, source_target_pairs={{0,4},{1,5},{2,6},{3,7},{4,0},{5,1},{6,2},{7,3},{8,12},{9,13},{10,... | collective-permute-start | bytes 245768 | tf_op jit(solution)/shard_map/ppermute | solution.py:547
  5.4 4.8 %copy-start.2 = (s32[4,70,50]{2,1,0:T(8,128)S(1)}, s32[4,70,50]{2,1,0:T(8,128)}, u32[]{:S(2)}) copy-start(s32[4,70,50]{2,1,0:T(8,128)} %constant.2.clone.lists) | copy-start | bytes 168004
  5.5 4.7 %copy-start.3 = (s32[6,32,32]{2,1,0:T(8,128)S(1)}, s32[6,32,32]{2,1,0:T(8,128)}, u32[]{:S(2)}) copy-start(s32[6,32,32]{2,1,0:T(8,128)} %fine_op.1) | copy-start | bytes 73732
  5.5 4.7 %copy-start.6 = (s32[3,16,32]{2,1,0:T(8,128)S(1)}, s32[3,16,32]{2,1,0:T(8,128)}, u32[]{:S(2)}) copy-start(s32[3,16,32]{2,1,0:T(8,128)} %par_op.1) | copy-start | bytes 18436
  5.5 5.3 %copy-start.1 = (f32[40,2,512]{2,1,0:T(2,128)S(1)}, f32[40,2,512]{2,1,0:T(2,128)}, u32[]{:S(2)}) copy-start(f32[40,2,512]{2,1,0:T(2,128)} %fops.5) | copy-start | bytes 491524
  5.5 5.3 %copy-start.5 = (f32[4,2048]{1,0:T(4,128)S(1)}, f32[4,2048]{1,0:T(4,128)}, u32[]{:S(2)}) copy-start(f32[4,2048]{1,0:T(4,128)} %phase.1) | copy-start | bytes 98308
  5.5 7.3 %collective-permute-start.1 = (bf16[128,512]{1,0:T(8,128)(2,1)S(1)}, bf16[128,512]{1,0:T(8,128)(2,1)S(1)}, u32[]{:S(2)}, u32[]{:S(2)}) collective-permute-start(bf16[128,512]{1,0:T(8,128)(2,1)S(1)} %edge.1), channel_id=1, source_target_pairs={{8,16},{16,8},{9,17},{17,9},{10,18},{18,10},{11,19},{19,11},{12,20... | collective-permute-start | bytes 393224 | tf_op jit(solution)/shard_map/ppermute | solution.py:157
  7.5 10.0 %collective-permute-start.5 = (f32[2,40,2,256]{3,2,1,0:T(2,128)S(1)}, f32[2,40,2,256]{3,2,1,0:T(2,128)S(1)}, u32[]{:S(2)}, u32[]{:S(2)}) collective-permute-start(f32[2,40,2,256]{3,2,1,0:T(2,128)S(1)} %hold2.1), channel_id=1, source_target_pairs={{0,2},{1,3},{2,0},{3,1},{4,6},{5,7},{6,4},{7,5},{8,10},{9,11},{10,... | collective-permute-start | bytes 491528 | tf_op jit(solution)/shard_map/ppermute | solution.py:547
  12.8 4.8 %copy-start = (bf16[512,2048]{1,0:T(8,128)(2,1)S(1)}, bf16[512,2048]{1,0:T(8,128)(2,1)}, u32[]{:S(2)}) copy-start(bf16[512,2048]{1,0:T(8,128)(2,1)} %interp.3) | copy-start | bytes 6291460
  12.9 4.7 %collective-permute-start.3 = (bf16[512,512]{1,0:T(8,128)(2,1)S(1)}, bf16[512,512]{1,0:T(8,128)(2,1)S(1)}, u32[]{:S(2)}, u32[]{:S(2)}) collective-permute-start(bf16[512,512]{1,0:T(8,128)(2,1)S(1)} %pack.1.strip), channel_id=1, source_target_pairs={{0,1},{1,0},{2,3},{3,2},{4,5},{5,4},{6,7},{7,6},{8,9},{9,8},{10,11... | collective-permute-start | bytes 1572872 | tf_op jit(solution)/shard_map/ppermute | solution.py:157
  14.4 10.5 %collective-permute-start.2 = (bf16[512,512]{1,0:T(8,128)(2,1)S(1)}, bf16[512,512]{1,0:T(8,128)(2,1)S(1)}, u32[]{:S(2)}, u32[]{:S(2)}) collective-permute-start(bf16[512,512]{1,0:T(8,128)(2,1)S(1)} %pack.1.strip), channel_id=1, source_target_pairs={{1,2},{2,1},{3,4},{4,3},{5,6},{6,5},{9,10},{10,9},{11,12},{12,11},... | collective-permute-start | bytes 1572872 | tf_op jit(solution)/shard_map/ppermute | solution.py:157
  17.5 4.3 %collective-permute-start.6 = (f32[4,40,2,256]{3,2,1,0:T(2,128)S(1)}, f32[4,40,2,256]{3,2,1,0:T(2,128)S(1)}, u32[]{:S(2)}, u32[]{:S(2)}) collective-permute-start(f32[4,40,2,256]{3,2,1,0:T(2,128)S(1)} %hold3.1), channel_id=1, source_target_pairs={{0,1},{1,0},{2,3},{3,2},{4,5},{5,4},{6,7},{7,6},{8,9},{9,8},{10,11... | collective-permute-start | bytes 983048 | tf_op jit(solution)/shard_map/ppermute | solution.py:547

commit v7 on v6

--- a/solution.py
+++ b/solution.py
@@ -398,14 +398,14 @@
     counts = slot_counts(rows, cols, 1)
     at = starts(counts)
     sources = [(at[0], counts[0], pat_own), (at[1], counts[1], pat_a)]
-    for first in range(0, real.shape[2], 2 * CHUNK):
+    for first in range(0, real.shape[2], CHUNK):
         for index, group in enumerate(parent_groups(rows, cols)):
             sums = parent_sums(
-                rows, cols, sides, table, pops, sources, index, group, first, 2 * CHUNK
+                rows, cols, sides, table, pops, sources, index, group, first, CHUNK
             )
             for (r, c), (re, im) in zip(group, sums):
-                real[r * cols + c, :, first : first + 2 * CHUNK] = re
-                imag[r * cols + c, :, first : first + 2 * CHUNK] = im
+                real[r * cols + c, :, first : first + CHUNK] = re
+                imag[r * cols + c, :, first : first + CHUNK] = im
 
 
 def last_kernel(

time: 30.1 us -> 30.1 us (level)
  transfers between devices with their start and end apart: 7 -> 7, of which waited for: 2 -> 2; matrix products, arithmetic and copies ran while one was open for 0% -> 0% of each run, Pallas kernels for 30% -> 29%
where the time goes in v7:
time: 30.1 us; the launch traced here: 30 us
  Pallas kernels  13.8 us (46%)
  starting transfers between devices  12.6 us (42%)
  waiting for transfers between devices  2.33 us (8%)
  local copies, waits for them, and re-layouts  1.05 us (3%)
    pallas_call x9, Pallas kernels, call(): pl.pallas_call(functools.partial(body, rows, cols, sides), out_shape=outs...  13.8 us
    ppermute x4, starting transfers between devices, exchange(): lax.ppermute(block, axis, pairs(n, first))  7.52 us
    ppermute x3, starting transfers between devices, per_device(): lax.ppermute(held, 'dir', [(i, i ^ 1 << bit) for i in range(n_dir)])  5.04 us
    ppermute x3, waiting for transfers between devices, per_device(): lax.ppermute(held, 'dir', [(i, i ^ 1 << bit) for i in range(n_dir)])  1.21 us
    ppermute x4, waiting for transfers between devices, exchange(): lax.ppermute(block, axis, pairs(n, first))  1.11 us
    reshape x1, local copies, waits for them, and re-layouts, per_device(): own = fine_out.reshape(frows * fcols * comps, fdirs)  1.01 us
  transfers between devices with their start and end apart: 7, of which 2 were waited for; matrix products, arithmetic and copies ran while one was open for 0% of the time, Pallas kernels for 29%

profile of v7, /device:TPU:1, one launch (start us, length us, event | category | flops | bytes accessed | tf_op | source)
XLA Modules:
  0.0 30.0 jit_solution(8321064256007686541)
XLA Ops:
  0.0 0.0 copy-start.4
  0.0 1.0 %reshape.3.own.src = bf16[192,512]{1,0:T(8,128)(2,1)S(1)} reshape(bf16[6,4,2,4,512]{4,3,2,1,0:T(4,128)(2,1)} %param.10) | data formatting | bytes 393216 | tf_op jit(solution)/shard_map/reshape | solution.py:494
  1.0 2.1 %collective-permute-start = (bf16[192,512]{1,0:T(8,128)(2,1)S(1)}, bf16[192,512]{1,0:T(8,128)(2,1)S(1)}, u32[]{:S(2)}, u32[]{:S(2)}) collective-permute-start(bf16[192,512]{1,0:T(8,128)(2,1)S(1)} %reshape.3.own.src), channel_id=1, source_target_pairs={{0,8},{8,0},{16,24},{24,16},{1,9},{9,1},{17,25},{25,17},{2,10},{10... | collective-permute-start | bytes 589832 | tf_op jit(solution)/shard_map/ppermute | solution.py:157
  3.1 2.3 %collective-permute-start.4 = (f32[1,40,2,256]{3,2,1,0:T(2,128)}, f32[1,40,2,256]{3,2,1,0:T(2,128)S(1)}, u32[]{:S(2)}, u32[]{:S(2)}) collective-permute-start(f32[1,40,2,256]{3,2,1,0:T(2,128)} %bitcast.1), channel_id=1, source_target_pairs={{0,4},{1,5},{2,6},{3,7},{4,0},{5,1},{6,2},{7,3},{8,12},{9,13},{10,... | collective-permute-start | bytes 245768 | tf_op jit(solution)/shard_map/ppermute | solution.py:547
  5.4 0.0 copy-start.2
  5.5 0.0 copy-start.3
  5.5 0.0 copy-start.6
  5.5 0.0 copy-start.1
  5.5 0.0 copy-start.5
  5.5 0.8 %collective-permute-start.1 = (bf16[128,512]{1,0:T(8,128)(2,1)S(1)}, bf16[128,512]{1,0:T(8,128)(2,1)S(1)}, u32[]{:S(2)}, u32[]{:S(2)}) collective-permute-start(bf16[128,512]{1,0:T(8,128)(2,1)S(1)} %edge.1), channel_id=1, source_target_pairs={{8,16},{16,8},{9,17},{17,9},{10,18},{18,10},{11,19},{19,11},{12,20... | collective-permute-start | bytes 393224 | tf_op jit(solution)/shard_map/ppermute | solution.py:157
  6.3 1.2 %collective-permute-done.4.refs_1_ = f32[1,40,2,256]{3,2,1,0:T(2,128)S(1)} collective-permute-done((f32[1,40,2,256]{3,2,1,0:T(2,128)}, f32[1,40,2,256]{3,2,1,0:T(2,128)S(1)}, u32[]{:S(2)}, u32[]{:S(2)}) %collective-permute-start.4) | collective-permute-done | bytes 81952 | tf_op jit(solution)/shard_map/ppermute | solution.py:547
  7.5 0.0 copy-done.4
  7.5 2.7 %collective-permute-start.5 = (f32[2,40,2,256]{3,2,1,0:T(2,128)S(1)}, f32[2,40,2,256]{3,2,1,0:T(2,128)S(1)}, u32[]{:S(2)}, u32[]{:S(2)}) collective-permute-start(f32[2,40,2,256]{3,2,1,0:T(2,128)S(1)} %hold2.1), channel_id=1, source_target_pairs={{0,2},{1,3},{2,0},{3,1},{4,6},{5,7},{6,4},{7,5},{8,10},{9,11},{10,... | collective-permute-start | bytes 491528 | tf_op jit(solution)/shard_map/ppermute | solution.py:547
  10.2 0.0 copy-done.2
  10.2 0.0 copy-done.3
  10.2 0.0 copy-done.6
  10.2 0.6 %lists.2.table = s32[38,50]{1,0:T(8,128)S(1)} custom-call(s32[6,32,32]{2,1,0:T(8,128)S(1)} %copy-done.3, s32[3,16,32]{2,1,0:T(8,128)S(1)} %copy-done.6, s32[4,70,50]{2,1,0:T(8,128)S(1)} %copy-done.2), custom_call_target="tpu_custom_call" | custom-call | tf_op jit(solution)/shard_map/lists/pallas_call | solution.py:517
  10.8 0.0 copy-done.1
  10.8 0.0 copy-done.5
  10.8 2.0 %block.1 = (f32[24,8,512]{2,1,0:T(8,128)S(1)}, f32[8,2048]{1,0:T(8,128)S(1)}) custom-call(s32[38,50]{1,0:T(8,128)S(1)} %lists.2.table, bf16[192,512]{1,0:T(8,128)(2,1)S(1)} %reshape.3.own.src, f32[4,2048]{1,0:T(4,128)S(1)} %copy-done.5, f32[40,2,512]{2,1,0:T(2,128)S(1)} %copy-done.1), custom_call_target="tpu_custom_call" | custom-call | tf_op jit(solution)/shard_map/block/pallas_call | solution.py:517
  12.8 0.0 collective-permute-done.1.second
  12.8 0.0 collective-permute-done.first
  12.8 0.0 copy-start
  12.9 1.6 %collective-permute-start.3 = (bf16[512,512]{1,0:T(8,128)(2,1)S(1)}, bf16[512,512]{1,0:T(8,128)(2,1)S(1)}, u32[]{:S(2)}, u32[]{:S(2)}) collective-permute-start(bf16[512,512]{1,0:T(8,128)(2,1)S(1)} %pack.1.strip), channel_id=1, source_target_pairs={{0,1},{1,0},{2,3},{3,2},{4,5},{5,4},{6,7},{7,6},{8,9},{9,8},{10,11... | collective-permute-start | bytes 1572872 | tf_op jit(solution)/shard_map/ppermute | solution.py:157
  14.4 3.0 %collective-permute-start.2 = (bf16[512,512]{1,0:T(8,128)(2,1)S(1)}, bf16[512,512]{1,0:T(8,128)(2,1)S(1)}, u32[]{:S(2)}, u32[]{:S(2)}) collective-permute-start(bf16[512,512]{1,0:T(8,128)(2,1)S(1)} %pack.1.strip), channel_id=1, source_target_pairs={{1,2},{2,1},{3,4},{4,3},{5,6},{6,5},{9,10},{10,9},{11,12},{12,11},... | collective-permute-start | bytes 1572872 | tf_op jit(solution)/shard_map/ppermute | solution.py:157
  17.5 0.0 collective-permute-done.5.refs_2_
  17.5 0.1 collective-permute-start.6
  17.6 0.0 collective-permute-done.3.side_a
  17.6 0.0 copy-done
  17.6 4.2 %both.1 = (f32[17,8,2048]{2,1,0:T(8,128)S(1)}, f32[24,8,512]{2,1,0:T(8,128)S(1)}, f32[17,8,2048]{2,1,0:T(8,128)S(1)}, f32[12,8,512]{2,1,0:T(8,128)S(1)}) custom-call(s32[38,50]{1,0:T(8,128)S(1)} %lists.2.table, bf16[512,512]{1,0:T(8,128)(2,1)S(1)} %pack.1.strip, bf16[512,512]{1,0:T(8,128)(2,1)S(1)} %collective-permute-done.3.side_a, ...), custom_call_target="tpu_custom_call" | custom-call | tf_op jit(solution)/shard_map/both/pallas_call | solution.py:517
  21.8 0.0 collective-permute-done.6.refs_3_
  21.9 2.0 %inner.1 = (f32[40,2,2048]{2,1,0:T(2,128)S(1)}, f32[6,8,2048]{2,1,0:T(8,128)S(1)}, f32[6,8,2048]{2,1,0:T(8,128)S(1)}) custom-call(s32[38,50]{1,0:T(8,128)S(1)} %lists.2.table, f32[17,8,2048]{2,1,0:T(8,128)S(1)} %get-tuple-element.16.pat_own, f32[17,8,2048]{2,1,0:T(8,128)S(1)} %get-tuple-element.17.pat_a, f32[1,40,2,256]{3,2,1,0:T(2,128)S(1)} %bitcast.4, ...), custom_call_target="tpu_custom_call" | custom-call | tf_op jit(solution)/shard_map/inner/pallas_call | solution.py:517
  23.8 1.1 %collective-permute-done.2.src = bf16[512,512]{1,0:T(8,128)(2,1)S(1)} collective-permute-done((bf16[512,512]{1,0:T(8,128)(2,1)S(1)}, bf16[512,512]{1,0:T(8,128)(2,1)S(1)}, u32[]{:S(2)}, u32[]{:S(2)}) %collective-permute-start.2) | collective-permute-done | bytes 524320 | tf_op jit(solution)/shard_map/ppermute | solution.py:157
  24.9 5.0 %last.1 = f32[6,4,2,4,512]{4,3,2,1,0:T(4,128)} custom-call(s32[38,50]{1,0:T(8,128)S(1)} %lists.2.table, bf16[512,512]{1,0:T(8,128)(2,1)S(1)} %collective-permute-done.2.src, bf16[512,2048]{1,0:T(8,128)(2,1)S(1)} %copy-done, f32[8,2048]{1,0:T(8,128)S(1)} %get-tuple-element.15.trig, f32[40,2,512]{2,1,0:T(2,128)S(1)} %copy-done.1, ...), custom_call_target="tpu_custom_call" | custom-call | tf_op jit(solution)/shard_map/last/pallas_call | solution.py:517
  (4 shorter events, 0.1 us)
Async XLA Ops:
  0.0 7.5 %copy-start.4 = (f32[40,2,256]{2,1,0:T(2,128)S(1)}, f32[40,2,256]{2,1,0:T(2,128)}, u32[]{:S(2)}) copy-start(f32[40,2,256]{2,1,0:T(2,128)} %param.14) | copy-start | bytes 245764
  1.0 11.8 %collective-permute-start = (bf16[192,512]{1,0:T(8,128)(2,1)S(1)}, bf16[192,512]{1,0:T(8,128)(2,1)S(1)}, u32[]{:S(2)}, u32[]{:S(2)}) collective-permute-start(bf16[192,512]{1,0:T(8,128)(2,1)S(1)} %reshape.3.own.src), channel_id=1, source_target_pairs={{0,8},{8,0},{16,24},{24,16},{1,9},{9,1},{17,25},{25,17},{2,10},{10... | collective-permute-start | bytes 589832 | tf_op jit(solution)/shard_map/ppermute | solution.py:157
  3.1 4.4 %collective-permute-start.4 = (f32[1,40,2,256]{3,2,1,0:T(2,128)}, f32[1,40,2,256]{3,2,1,0:T(2,128)S(1)}, u32[]{:S(2)}, u32[]{:S(2)}) collective-permute-start(f32[1,40,2,256]{3,2,1,0:T(2,128)} %bitcast.1), channel_id=1, source_target_pairs={{0,4},{1,5},{2,6},{3,7},{4,0},{5,1},{6,2},{7,3},{8,12},{9,13},{10,... | collective-permute-start | bytes 245768 | tf_op jit(solution)/shard_map/ppermute | solution.py:547
  5.4 4.8 %copy-start.2 = (s32[4,70,50]{2,1,0:T(8,128)S(1)}, s32[4,70,50]{2,1,0:T(8,128)}, u32[]{:S(2)}) copy-start(s32[4,70,50]{2,1,0:T(8,128)} %constant.2.clone.lists) | copy-start | bytes 168004
  5.5 4.7 %copy-start.3 = (s32[6,32,32]{2,1,0:T(8,128)S(1)}, s32[6,32,32]{2,1,0:T(8,128)}, u32[]{:S(2)}) copy-start(s32[6,32,32]{2,1,0:T(8,128)} %fine_op.1) | copy-start | bytes 73732
  5.5 4.7 %copy-start.6 = (s32[3,16,32]{2,1,0:T(8,128)S(1)}, s32[3,16,32]{2,1,0:T(8,128)}, u32[]{:S(2)}) copy-start(s32[3,16,32]{2,1,0:T(8,128)} %par_op.1) | copy-start | bytes 18436
  5.5 5.3 %copy-start.1 = (f32[40,2,512]{2,1,0:T(2,128)S(1)}, f32[40,2,512]{2,1,0:T(2,128)}, u32[]{:S(2)}) copy-start(f32[40,2,512]{2,1,0:T(2,128)} %fops.5) | copy-start | bytes 491524
  5.5 5.3 %copy-start.5 = (f32[4,2048]{1,0:T(4,128)S(1)}, f32[4,2048]{1,0:T(4,128)}, u32[]{:S(2)}) copy-start(f32[4,2048]{1,0:T(4,128)} %phase.1) | copy-start | bytes 98308
  5.5 7.3 %collective-permute-start.1 = (bf16[128,512]{1,0:T(8,128)(2,1)S(1)}, bf16[128,512]{1,0:T(8,128)(2,1)S(1)}, u32[]{:S(2)}, u32[]{:S(2)}) collective-permute-start(bf16[128,512]{1,0:T(8,128)(2,1)S(1)} %edge.1), channel_id=1, source_target_pairs={{8,16},{16,8},{9,17},{17,9},{10,18},{18,10},{11,19},{19,11},{12,20... | collective-permute-start | bytes 393224 | tf_op jit(solution)/shard_map/ppermute | solution.py:157
  7.5 10.0 %collective-permute-start.5 = (f32[2,40,2,256]{3,2,1,0:T(2,128)S(1)}, f32[2,40,2,256]{3,2,1,0:T(2,128)S(1)}, u32[]{:S(2)}, u32[]{:S(2)}) collective-permute-start(f32[2,40,2,256]{3,2,1,0:T(2,128)S(1)} %hold2.1), channel_id=1, source_target_pairs={{0,2},{1,3},{2,0},{3,1},{4,6},{5,7},{6,4},{7,5},{8,10},{9,11},{10,... | collective-permute-start | bytes 491528 | tf_op jit(solution)/shard_map/ppermute | solution.py:547
  12.8 4.8 %copy-start = (bf16[512,2048]{1,0:T(8,128)(2,1)S(1)}, bf16[512,2048]{1,0:T(8,128)(2,1)}, u32[]{:S(2)}) copy-start(bf16[512,2048]{1,0:T(8,128)(2,1)} %interp.3) | copy-start | bytes 6291460
  12.9 4.7 %collective-permute-start.3 = (bf16[512,512]{1,0:T(8,128)(2,1)S(1)}, bf16[512,512]{1,0:T(8,128)(2,1)S(1)}, u32[]{:S(2)}, u32[]{:S(2)}) collective-permute-start(bf16[512,512]{1,0:T(8,128)(2,1)S(1)} %pack.1.strip), channel_id=1, source_target_pairs={{0,1},{1,0},{2,3},{3,2},{4,5},{5,4},{6,7},{7,6},{8,9},{9,8},{10,11... | collective-permute-start | bytes 1572872 | tf_op jit(solution)/shard_map/ppermute | solution.py:157
  14.4 10.5 %collective-permute-start.2 = (bf16[512,512]{1,0:T(8,128)(2,1)S(1)}, bf16[512,512]{1,0:T(8,128)(2,1)S(1)}, u32[]{:S(2)}, u32[]{:S(2)}) collective-permute-start(bf16[512,512]{1,0:T(8,128)(2,1)S(1)} %pack.1.strip), channel_id=1, source_target_pairs={{1,2},{2,1},{3,4},{4,3},{5,6},{6,5},{9,10},{10,9},{11,12},{12,11},... | collective-permute-start | bytes 1572872 | tf_op jit(solution)/shard_map/ppermute | solution.py:157
  17.5 4.3 %collective-permute-start.6 = (f32[4,40,2,256]{3,2,1,0:T(2,128)S(1)}, f32[4,40,2,256]{3,2,1,0:T(2,128)S(1)}, u32[]{:S(2)}, u32[]{:S(2)}) collective-permute-start(f32[4,40,2,256]{3,2,1,0:T(2,128)S(1)} %hold3.1), channel_id=1, source_target_pairs={{0,1},{1,0},{2,3},{3,2},{4,5},{5,4},{6,7},{7,6},{8,9},{9,8},{10,11... | collective-permute-start | bytes 983048 | tf_op jit(solution)/shard_map/ppermute | solution.py:547
